TPU v7x, 32 devices: a whole 2x2x4 slice. The times are simulated.
32 devices in a mesh: chan: 8 (over z, y), tm: 4 (over x, core).
Axes of the slice: x: 2, y: 2, z: 4, core: 2. Of those that a mesh axis runs over, the one named last changes fastest.
Arguments:
- series: bfloat16 [4096, 3072], P('chan', 'tm'), may hold values from -6 to 6
- ref_list: int32 [8, 256], replicated, may hold values from 0 to 4095, as said below
Outputs:
- hankel: bfloat16 [128, 4096, 256], P('tm', 'chan')
Inputs may be any that keep to these rules, and one draw needn't show every extreme that they name: `ref_list`: each row names 256 different channels. Over all rows together, exactly 32 different channels of each group's 512 channels (c // 512 equal) are named.
All inputs are finite; a program needn't handle non-finite values.
Results may differ from a plain program's by a relative error of at most 0.018.
Values may be sent and summed in bfloat16 or wider, within the bound.
No kernel may reach another device: no remote copies, remote signals or barrier semaphores. Data moves between devices by JAX's collectives and lax.ppermute only.
A program may use at most 128 MiB of HBM per device.

v0:
```python
import math

import jax
import jax.numpy as jnp
from jax import lax
from jax.sharding import PartitionSpec as P

LAGS = 128


def shifted(array, axis, by):
    size = lax.axis_size(axis)
    pairs = [(i, i + by) for i in range(size) if 0 <= i + by < size]
    return lax.ppermute(array, axis, pairs)


def lag_block(extended_rows, ref_block, first_lag, time_len, scale_factor):
    offsets = first_lag + jnp.arange(8, dtype=jnp.int32)
    windows = jax.vmap(lambda offset: lax.dynamic_slice_in_dim(extended_rows, offset, time_len, 1))(
        offsets
    )
    return (
        jnp.einsum("jct,rt->jcr", windows, ref_block, preferred_element_type=jnp.float32)
        * scale_factor
    )


def shards(series, ref_list):
    chan_rows, time_len = series.shape
    ref_count = ref_list.shape[1]
    group_index = lax.axis_index("chan")
    my_list = lax.dynamic_index_in_dim(ref_list, group_index, 0, keepdims=False)
    gathered_all = lax.all_gather(series, "chan", axis=0, tiled=True)
    ref_rows = jnp.take(gathered_all, my_list, axis=0)
    lag_tail = shifted(series[:, :LAGS], "tm", -1)
    extended = jnp.concatenate([series, lag_tail], axis=1)
    scale_factor = 1.0 / math.sqrt(time_len * lax.axis_size("tm"))
    lags_dev = LAGS // lax.axis_size("tm")

    def lag_step(carry, block_index):
        return (carry, lag_block(extended, ref_rows, 8 * block_index, time_len, scale_factor))

    _, stacked = lax.scan(
        lag_step, None, jnp.arange(lax.axis_size("tm") * lags_dev // 8, dtype=jnp.int32)
    )
    return lax.psum_scatter(
        stacked.reshape(lax.axis_size("tm") * lags_dev, chan_rows, ref_count).astype(jnp.bfloat16),
        "tm",
        scatter_dimension=0,
        tiled=True,
    )


def solution(mesh):
    in_specs = (P("chan", "tm"), P())
    out_specs = P("tm", "chan", None)
    return jax.shard_map(shards, mesh=mesh, in_specs=in_specs, out_specs=out_specs, check_vma=False)
```

profile of v0, /device:TPU:0, one launch (start us, length us, event | category | flops | bytes accessed | tf_op | source)
XLA Modules:
  0.0 782.9 jit_solution(3682779407110777230)
XLA Ops:
  12.7 98.6 %all-gather.2.cloned.1.call-done = bf16[4096,768]{1,0:T(8,128)(2,1)} async-done(((bf16[512,768]{1,0:T(8,128)(2,1)}), bf16[4096,768]{1,0:T(8,128)(2,1)}) %all-gather.2.cloned.1.call-update) | async-done | bytes 6291472 | tf_op jit(solution)/shard_map/all_gather | solution.py:33
  111.3 5.0 gather_fusion
  116.4 426.4 %while.13 = (s32[]{:T(128)}, bf16[16,8,512,256]{3,2,1,0:T(8,128)(2,1)}, s32[16]{0:T(128)S(1)}, bf16[512,896]{1,0:T(8,128)(2,1)S(1)}, bf16[256,768]{1,0:T(8,128)(...) while((s32[]{:T(128)}, bf16[16,8,512,256]{3,2,1,0:T(8,128)(2,1)}, s32[16]{0:T(128)S(1)}, ...), condition=%wide.region_1.2_spmd, body=%wide.region_0.1_spmd.sunk | while | flops 1611661312 | bytes 12453766 | solution.py:43
  117.7 19.4 %while.14 = (s32[]{:T(128)}, bf16[512,896]{1,0:T(8,128)(2,1)S(1)}, s32[8,2]{0,1:T(2,128)S(1)}, bf16[8,512,768]{2,1,0:T(8,128)(2,1)}, s32[]{:T(128)}) while((s32[]{:T(128)}, bf16[512,896]{1,0:T(8,128)(2,1)S(1)}, s32[8,2]{0,1:T(2,128)S(1)}, bf16[8,512,768]{2,1,0:T(8,128)(2,1)}, s32[]{:T(128)}) %tuple.34), condition=%wide.while_cond, body=%wide.while_body.sunk | while | flops 2 | bytes 1573977 | solution.py:19
  118.3 1.9 bitcast_dynamic-update-slice_fusion.5
  120.7 1.9 bitcast_dynamic-update-slice_fusion.5
  123.1 1.9 bitcast_dynamic-update-slice_fusion.5
  125.6 1.9 bitcast_dynamic-update-slice_fusion.5
  128.0 1.9 bitcast_dynamic-update-slice_fusion.5
  130.4 1.9 bitcast_dynamic-update-slice_fusion.5
  132.8 1.9 bitcast_dynamic-update-slice_fusion.5
  135.3 1.9 bitcast_dynamic-update-slice_fusion.5
  137.1 6.0 bitcast_dynamic-update-slice_fusion.4
  144.4 19.4 %while.14 = (s32[]{:T(128)}, bf16[512,896]{1,0:T(8,128)(2,1)S(1)}, s32[8,2]{0,1:T(2,128)S(1)}, bf16[8,512,768]{2,1,0:T(8,128)(2,1)}, s32[]{:T(128)}) while((s32[]{:T(128)}, bf16[512,896]{1,0:T(8,128)(2,1)S(1)}, s32[8,2]{0,1:T(2,128)S(1)}, bf16[8,512,768]{2,1,0:T(8,128)(2,1)}, s32[]{:T(128)}) %tuple.34), condition=%wide.while_cond, body=%wide.while_body.sunk | while | flops 2 | bytes 1573977 | solution.py:19
  144.9 1.9 bitcast_dynamic-update-slice_fusion.5
  147.4 1.9 bitcast_dynamic-update-slice_fusion.5
  149.8 1.9 bitcast_dynamic-update-slice_fusion.5
  159.5 1.9 bitcast_dynamic-update-slice_fusion.5
  163.8 5.9 bitcast_dynamic-update-slice_fusion.4
  171.0 19.4 %while.14 = (s32[]{:T(128)}, bf16[512,896]{1,0:T(8,128)(2,1)S(1)}, s32[8,2]{0,1:T(2,128)S(1)}, bf16[8,512,768]{2,1,0:T(8,128)(2,1)}, s32[]{:T(128)}) while((s32[]{:T(128)}, bf16[512,896]{1,0:T(8,128)(2,1)S(1)}, s32[8,2]{0,1:T(2,128)S(1)}, bf16[8,512,768]{2,1,0:T(8,128)(2,1)}, s32[]{:T(128)}) %tuple.34), condition=%wide.while_cond, body=%wide.while_body.sunk | while | flops 2 | bytes 1573977 | solution.py:19
  186.1 1.9 bitcast_dynamic-update-slice_fusion.5
  190.4 5.9 bitcast_dynamic-update-slice_fusion.4
  197.6 19.4 %while.14 = (s32[]{:T(128)}, bf16[512,896]{1,0:T(8,128)(2,1)S(1)}, s32[8,2]{0,1:T(2,128)S(1)}, bf16[8,512,768]{2,1,0:T(8,128)(2,1)}, s32[]{:T(128)}) while((s32[]{:T(128)}, bf16[512,896]{1,0:T(8,128)(2,1)S(1)}, s32[8,2]{0,1:T(2,128)S(1)}, bf16[8,512,768]{2,1,0:T(8,128)(2,1)}, s32[]{:T(128)}) %tuple.34), condition=%wide.while_cond, body=%wide.while_body.sunk | while | flops 2 | bytes 1573977 | solution.py:19
  203.1 1.9 bitcast_dynamic-update-slice_fusion.5
  215.2 1.9 bitcast_dynamic-update-slice_fusion.5
  217.1 6.0 bitcast_dynamic-update-slice_fusion.4
  224.3 19.4 %while.14 = (s32[]{:T(128)}, bf16[512,896]{1,0:T(8,128)(2,1)S(1)}, s32[8,2]{0,1:T(2,128)S(1)}, bf16[8,512,768]{2,1,0:T(8,128)(2,1)}, s32[]{:T(128)}) while((s32[]{:T(128)}, bf16[512,896]{1,0:T(8,128)(2,1)S(1)}, s32[8,2]{0,1:T(2,128)S(1)}, bf16[8,512,768]{2,1,0:T(8,128)(2,1)}, s32[]{:T(128)}) %tuple.34), condition=%wide.while_cond, body=%wide.while_body.sunk | while | flops 2 | bytes 1573977 | solution.py:19
  227.3 1.9 bitcast_dynamic-update-slice_fusion.5
  239.5 1.9 bitcast_dynamic-update-slice_fusion.5
  243.8 6.0 bitcast_dynamic-update-slice_fusion.4
  251.0 19.4 %while.14 = (s32[]{:T(128)}, bf16[512,896]{1,0:T(8,128)(2,1)S(1)}, s32[8,2]{0,1:T(2,128)S(1)}, bf16[8,512,768]{2,1,0:T(8,128)(2,1)}, s32[]{:T(128)}) while((s32[]{:T(128)}, bf16[512,896]{1,0:T(8,128)(2,1)S(1)}, s32[8,2]{0,1:T(2,128)S(1)}, bf16[8,512,768]{2,1,0:T(8,128)(2,1)}, s32[]{:T(128)}) %tuple.34), condition=%wide.while_cond, body=%wide.while_body.sunk | while | flops 2 | bytes 1573977 | solution.py:19
  254.0 1.9 bitcast_dynamic-update-slice_fusion.5
  270.4 5.9 bitcast_dynamic-update-slice_fusion.4
  277.6 19.4 %while.14 = (s32[]{:T(128)}, bf16[512,896]{1,0:T(8,128)(2,1)S(1)}, s32[8,2]{0,1:T(2,128)S(1)}, bf16[8,512,768]{2,1,0:T(8,128)(2,1)}, s32[]{:T(128)}) while((s32[]{:T(128)}, bf16[512,896]{1,0:T(8,128)(2,1)S(1)}, s32[8,2]{0,1:T(2,128)S(1)}, bf16[8,512,768]{2,1,0:T(8,128)(2,1)}, s32[]{:T(128)}) %tuple.34), condition=%wide.while_cond, body=%wide.while_body.sunk | while | flops 2 | bytes 1573977 | solution.py:19
  292.8 1.9 bitcast_dynamic-update-slice_fusion.5
  297.1 5.9 bitcast_dynamic-update-slice_fusion.4
  304.3 19.4 %while.14 = (s32[]{:T(128)}, bf16[512,896]{1,0:T(8,128)(2,1)S(1)}, s32[8,2]{0,1:T(2,128)S(1)}, bf16[8,512,768]{2,1,0:T(8,128)(2,1)}, s32[]{:T(128)}) while((s32[]{:T(128)}, bf16[512,896]{1,0:T(8,128)(2,1)S(1)}, s32[8,2]{0,1:T(2,128)S(1)}, bf16[8,512,768]{2,1,0:T(8,128)(2,1)}, s32[]{:T(128)}) %tuple.34), condition=%wide.while_cond, body=%wide.while_body.sunk | while | flops 2 | bytes 1573977 | solution.py:19
  304.9 1.9 bitcast_dynamic-update-slice_fusion.5
  323.7 5.9 bitcast_dynamic-update-slice_fusion.4
  330.9 19.4 %while.14 = (s32[]{:T(128)}, bf16[512,896]{1,0:T(8,128)(2,1)S(1)}, s32[8,2]{0,1:T(2,128)S(1)}, bf16[8,512,768]{2,1,0:T(8,128)(2,1)}, s32[]{:T(128)}) while((s32[]{:T(128)}, bf16[512,896]{1,0:T(8,128)(2,1)S(1)}, s32[8,2]{0,1:T(2,128)S(1)}, bf16[8,512,768]{2,1,0:T(8,128)(2,1)}, s32[]{:T(128)}) %tuple.34), condition=%wide.while_cond, body=%wide.while_body.sunk | while | flops 2 | bytes 1573977 | solution.py:19
  338.8 1.9 bitcast_dynamic-update-slice_fusion.5
  350.3 6.0 bitcast_dynamic-update-slice_fusion.4
  357.6 19.4 %while.14 = (s32[]{:T(128)}, bf16[512,896]{1,0:T(8,128)(2,1)S(1)}, s32[8,2]{0,1:T(2,128)S(1)}, bf16[8,512,768]{2,1,0:T(8,128)(2,1)}, s32[]{:T(128)}) while((s32[]{:T(128)}, bf16[512,896]{1,0:T(8,128)(2,1)S(1)}, s32[8,2]{0,1:T(2,128)S(1)}, bf16[8,512,768]{2,1,0:T(8,128)(2,1)}, s32[]{:T(128)}) %tuple.34), condition=%wide.while_cond, body=%wide.while_body.sunk | while | flops 2 | bytes 1573977 | solution.py:19
  367.9 1.9 bitcast_dynamic-update-slice_fusion.5
  377.0 5.9 bitcast_dynamic-update-slice_fusion.4
  384.2 19.4 %while.14 = (s32[]{:T(128)}, bf16[512,896]{1,0:T(8,128)(2,1)S(1)}, s32[8,2]{0,1:T(2,128)S(1)}, bf16[8,512,768]{2,1,0:T(8,128)(2,1)}, s32[]{:T(128)}) while((s32[]{:T(128)}, bf16[512,896]{1,0:T(8,128)(2,1)S(1)}, s32[8,2]{0,1:T(2,128)S(1)}, bf16[8,512,768]{2,1,0:T(8,128)(2,1)}, s32[]{:T(128)}) %tuple.34), condition=%wide.while_cond, body=%wide.while_body.sunk | while | flops 2 | bytes 1573977 | solution.py:19
  389.6 1.9 bitcast_dynamic-update-slice_fusion.5
  403.6 5.9 bitcast_dynamic-update-slice_fusion.4
  410.8 19.4 %while.14 = (s32[]{:T(128)}, bf16[512,896]{1,0:T(8,128)(2,1)S(1)}, s32[8,2]{0,1:T(2,128)S(1)}, bf16[8,512,768]{2,1,0:T(8,128)(2,1)}, s32[]{:T(128)}) while((s32[]{:T(128)}, bf16[512,896]{1,0:T(8,128)(2,1)S(1)}, s32[8,2]{0,1:T(2,128)S(1)}, bf16[8,512,768]{2,1,0:T(8,128)(2,1)}, s32[]{:T(128)}) %tuple.34), condition=%wide.while_cond, body=%wide.while_body.sunk | while | flops 2 | bytes 1573977 | solution.py:19
  428.4 1.9 bitcast_dynamic-update-slice_fusion.5
  430.3 6.0 bitcast_dynamic-update-slice_fusion.4
  437.5 19.4 %while.14 = (s32[]{:T(128)}, bf16[512,896]{1,0:T(8,128)(2,1)S(1)}, s32[8,2]{0,1:T(2,128)S(1)}, bf16[8,512,768]{2,1,0:T(8,128)(2,1)}, s32[]{:T(128)}) while((s32[]{:T(128)}, bf16[512,896]{1,0:T(8,128)(2,1)S(1)}, s32[8,2]{0,1:T(2,128)S(1)}, bf16[8,512,768]{2,1,0:T(8,128)(2,1)}, s32[]{:T(128)}) %tuple.34), condition=%wide.while_cond, body=%wide.while_body.sunk | while | flops 2 | bytes 1573977 | solution.py:19
  456.9 6.0 bitcast_dynamic-update-slice_fusion.4
  464.2 19.4 %while.14 = (s32[]{:T(128)}, bf16[512,896]{1,0:T(8,128)(2,1)S(1)}, s32[8,2]{0,1:T(2,128)S(1)}, bf16[8,512,768]{2,1,0:T(8,128)(2,1)}, s32[]{:T(128)}) while((s32[]{:T(128)}, bf16[512,896]{1,0:T(8,128)(2,1)S(1)}, s32[8,2]{0,1:T(2,128)S(1)}, bf16[8,512,768]{2,1,0:T(8,128)(2,1)}, s32[]{:T(128)}) %tuple.34), condition=%wide.while_cond, body=%wide.while_body.sunk | while | flops 2 | bytes 1573977 | solution.py:19
  469.6 1.9 bitcast_dynamic-update-slice_fusion.5
  481.8 1.9 bitcast_dynamic-update-slice_fusion.5
  483.6 5.9 bitcast_dynamic-update-slice_fusion.4
  490.8 19.4 %while.14 = (s32[]{:T(128)}, bf16[512,896]{1,0:T(8,128)(2,1)S(1)}, s32[8,2]{0,1:T(2,128)S(1)}, bf16[8,512,768]{2,1,0:T(8,128)(2,1)}, s32[]{:T(128)}) while((s32[]{:T(128)}, bf16[512,896]{1,0:T(8,128)(2,1)S(1)}, s32[8,2]{0,1:T(2,128)S(1)}, bf16[8,512,768]{2,1,0:T(8,128)(2,1)}, s32[]{:T(128)}) %tuple.34), condition=%wide.while_cond, body=%wide.while_body.sunk | while | flops 2 | bytes 1573977 | solution.py:19
  501.1 1.9 bitcast_dynamic-update-slice_fusion.5
  510.3 5.9 bitcast_dynamic-update-slice_fusion.4
  517.5 19.4 %while.14 = (s32[]{:T(128)}, bf16[512,896]{1,0:T(8,128)(2,1)S(1)}, s32[8,2]{0,1:T(2,128)S(1)}, bf16[8,512,768]{2,1,0:T(8,128)(2,1)}, s32[]{:T(128)}) while((s32[]{:T(128)}, bf16[512,896]{1,0:T(8,128)(2,1)S(1)}, s32[8,2]{0,1:T(2,128)S(1)}, bf16[8,512,768]{2,1,0:T(8,128)(2,1)}, s32[]{:T(128)}) %tuple.34), condition=%wide.while_cond, body=%wide.while_body.sunk | while | flops 2 | bytes 1573977 | solution.py:19
  527.8 1.9 bitcast_dynamic-update-slice_fusion.5
  536.9 5.9 bitcast_dynamic-update-slice_fusion.4
  542.9 233.2 %reduce-scatter.4.cloned.1.call-done = bf16[32,512,256]{2,1,0:T(8,128)(2,1)} async-done(((bf16[128,512,256]{2,1,0:T(8,128)(2,1)}), bf16[32,512,256]{2,1,0:T(8,128)(2,1)}) %reduce-scatter.4.cloned.1.call-update) | async-done | bytes 8388624
  (434 shorter events, 274.0 us)
Async XLA Ops:
  6.5 104.8 %all-gather.2.cloned.1.call-start = ((), (), s32[]{:S(2)}) async-start(), calls=%async_computation.1 | async-start | bytes 7077888 | tf_op jit(solution)/shard_map/all_gather | solution.py:33
  7.3 768.8 %reduce-scatter.4.cloned.1.call-start = ((), (), s32[]{:S(2)}) async-start(), calls=%async_computation.2 | async-start | bytes 41943040
  8.2 3.2 collective-permute-start
Sparse Core Ops, SparseCore 0:
  9.5 101.7 all-gather.1
  543.0 233.0 reduce-scatter.3
where the time goes:
time: 785 us; the launch traced here: 783 us
  waiting for transfers between devices  334 us (43%)
  local copies, waits for them, and re-layouts  326 us (42%)
  matrix products  95.2 us (12%)
  between operations  13.5 us (2%)
  loops' own time  11.2 us (1%)
    gather x384, local copies, waits for them, and re-layouts  310 us
    unnamed x3, waiting for transfers between devices  234 us
    all_gather x1, waiting for transfers between devices, shards(): gathered_all = lax.all_gather(series, 'chan', axis=0, tiled=True)  98.6 us
    dot_general x16, matrix products, lag_block(): jnp.einsum('jct,rt->jcr', windows, ref_block, preferred_element_type=jnp....  95.2 us
  transfers between devices with their start and end apart: 3, of which 3 were waited for; matrix products, arithmetic and copies ran while one was open for 0% of the time, Pallas kernels for 0%

commit v1 on v0

--- a/solution.py
+++ b/solution.py
@@ -1,11 +1,21 @@
+import functools
 import math
 
 import jax
 import jax.numpy as jnp
 from jax import lax
+from jax.experimental import pallas as pl
+from jax.experimental.pallas import tpu as pltpu
 from jax.sharding import PartitionSpec as P
 
 LAGS = 128
+POOL = 32
+BF16 = jnp.bfloat16
+F32 = jnp.float32
+
+
+def dot(a, b):
+    return jnp.dot(a, b, preferred_element_type=F32)
 
 
 def shifted(array, axis, by):
@@ -25,7 +35,7 @@
     )
 
 
-def shards(series, ref_list):
+def general_shards(series, ref_list):
     chan_rows, time_len = series.shape
     ref_count = ref_list.shape[1]
     group_index = lax.axis_index("chan")
@@ -51,7 +61,216 @@
     )
 
 
+def named_slots(list_ref, base, chan_rows):
+    rows, width = list_ref.shape
+    chan = base + lax.broadcasted_iota(jnp.int32, (chan_rows, 128), 0)
+    hit = jnp.zeros((chan_rows, 128), jnp.bool_)
+    for g in range(rows):
+        for c in range(0, width, 128):
+            hit = hit | (chan == list_ref[g : g + 1, c : c + 128])
+    hits = jnp.where(hit, 1.0, 0.0).astype(BF16)
+    named = jnp.where(dot(hits, jnp.ones((128, 128), BF16)) > 0.5, 1.0, 0.0)
+    below = lax.broadcasted_iota(jnp.int32, (chan_rows, chan_rows), 1) < lax.broadcasted_iota(
+        jnp.int32, (chan_rows, chan_rows), 0
+    )
+    rank = dot(jnp.where(below, 1.0, 0.0).astype(BF16), named.astype(BF16))
+    slot = lax.broadcasted_iota(jnp.int32, (chan_rows, 128), 1).astype(F32)
+    return jnp.where(rank == slot, named, 0.0)
+
+
+def select_kernel(group_ref, list_ref, s_ref, pool_ref):
+    chan_rows = s_ref.shape[0]
+    picks = named_slots(list_ref, group_ref[0] * chan_rows, chan_rows)
+    pool_ref[...] = dot(picks.T[:POOL].astype(BF16), s_ref[...]).astype(BF16)
+
+
+def order_kernel(group_ref, list_ref, mine_ref, order_ref, *, chan_rows):
+    width = mine_ref.shape[1]
+
+    @pl.loop(0, order_ref.shape[0] // POOL)
+    def _(d):
+        base = (group_ref[0] ^ d) * chan_rows
+        picks = named_slots(list_ref, base, chan_rows)
+        chan = base + lax.broadcasted_iota(jnp.int32, (chan_rows, width), 0)
+        wanted = jnp.where(chan == mine_ref[...], 1.0, 0.0).astype(BF16)
+        rows = pl.ds(pl.multiple_of(d * POOL, POOL), POOL)
+        order_ref[rows, :] = dot(picks.T[:POOL].astype(BF16), wanted).astype(BF16)
+
+
+PH = 16
+WIN = 512
+COMBOS = ((0, 0), (1, 0), (1, 4), (2, 0), (3, 0), (3, 4), (2, 8), (3, 8), (3, 12))
+
+
+def corr_kernel(tm_ref, order_ref, *refs, time_len, n_tm, n_pool, scale):
+    pieces = refs[: n_tm + n_pool]
+    out_ref, s_raw, r_raw, xf, s9, rv, sem_s, sem_r = refs[n_tm + n_pool :]
+    me = tm_ref[0]
+    total = s_raw.shape[1]
+    windows = total // WIN
+    per = WIN // PH
+    quarter = WIN // 4
+
+    @pl.when(pl.program_id(0) == 0)
+    def _():
+        def s_copy(e):
+            lanes = pl.ds(pl.multiple_of((me ^ e) * time_len, 128), time_len)
+            return pltpu.make_async_copy(pieces[e], s_raw.at[:, lanes], sem_s.at[e])
+
+        def r_copy(d, c, x):
+            lanes = pl.ds(pl.multiple_of((me ^ (c + 2 * x)) * time_len, 128), time_len)
+            return pltpu.make_async_copy(
+                pieces[n_tm + 2 * d + c].at[POOL * x : POOL * (x + 1)],
+                r_raw.at[POOL * d : POOL * (d + 1), lanes],
+                sem_r.at[d, c, x],
+            )
+
+        r_copies = [r_copy(d, c, x) for d in range(n_pool // 2) for c in range(2) for x in range(2)]
+        s_copies = [s_copy(e) for e in range(n_tm)]
+        for copy in r_copies + s_copies:
+            copy.start()
+        for copy in r_copies:
+            copy.wait()
+
+        at = lax.broadcasted_iota(jnp.int32, (256, 256), 0)
+        to = lax.broadcasted_iota(jnp.int32, (256, 256), 1)
+        turn = jnp.where(to == PH * (at & 15) + (at >> 4), 1.0, 0.0).astype(BF16)
+        for h in range(2):
+            for p in range(PH):
+                xf[h, p, 0:8, :] = jnp.zeros((8, 128), F32)
+
+        @pl.loop(0, total // 256)
+        def _(b):
+            block = r_raw[:, pl.ds(pl.multiple_of(b * 256, 256), 256)]
+            turned = lax.dot_general(
+                turn, block, (((1,), (1,)), ((), ())), preferred_element_type=F32
+            ).astype(BF16)
+            placed = dot(turned, order_ref[...])
+            for p in range(PH):
+                for h in range(2):
+                    xf[h, p, pl.ds(pl.multiple_of(8 + 16 * b, 8), 16), :] = placed[
+                        16 * p : 16 * p + 16, 128 * h : 128 * h + 128
+                    ]
+
+        @pl.loop(0, 35)
+        def _(idx):
+            k = idx - 31
+
+            def rows(kk, b, h):
+                level = kk >> 4
+                return xf[h, kk & 15, pl.ds(8 + per * b + level - 2 * me, per), :]
+
+            here = pl.ds(pl.multiple_of(idx * per, per), per)
+            for b in range(windows):
+                for h in range(2):
+                    x0, x4, x8, x12 = (rows(k + o, b, h) for o in (0, 4, 8, 12))
+                    lanes = slice(128 * h, 128 * h + 128)
+                    f0, f8 = x4 - x0, x12 - x8
+                    rv[0, b, here, lanes] = x0.astype(BF16)
+                    rv[1, b, here, lanes] = f0.astype(BF16)
+                    rv[2, b, here, lanes] = (x8 - x0).astype(BF16)
+                    rv[3, b, here, lanes] = (f8 - f0).astype(BF16)
+
+        for copy in s_copies:
+            copy.wait()
+        at = lax.broadcasted_iota(jnp.int32, (WIN, WIN), 0)
+        to = lax.broadcasted_iota(jnp.int32, (WIN, WIN), 1)
+        turn = jnp.where(at == PH * (to & (per - 1)) + to // per, 1.0, 0.0).astype(BF16)
+
+        @pl.loop(0, windows)
+        def _(b):
+            window = s_raw[:, pl.ds(pl.multiple_of(b * WIN, WIN), WIN)]
+            turned = dot(window, turn)
+            t = [turned[:, quarter * g : quarter * (g + 1)] for g in range(4)]
+            u0, u1 = t[0] + t[2], t[1] + t[3]
+            sums = (u0 + u1, u1, -u0, t[2] + t[3], t[3], -t[2], -(t[0] + t[1]), -t[1], t[0])
+            lanes = pl.ds(pl.multiple_of(b * quarter, quarter), quarter)
+            for i, value in enumerate(sums):
+                s9[i, :, lanes] = value.astype(BF16)
+
+    step = pl.program_id(0)
+    first = 31 - 16 * (step >> 2) - (step & 3)
+
+    def product(i):
+        v, off = COMBOS[i]
+        rows = pl.ds(pl.multiple_of((first - off) * per, per), 4 * per)
+        slab = jnp.concatenate([rv[v, b, rows, :] for b in range(windows)], axis=0)
+        return dot(s9[i], slab)
+
+    p = [product(i) for i in range(9)]
+    for at, parts in enumerate(((0, 1, 3, 4), (0, 2, 3, 5), (0, 1, 6, 7), (0, 2, 6, 8))):
+        out_ref[0, at, 0] = (scale * sum([p[i] for i in parts[1:]], p[parts[0]])).astype(BF16)
+
+
+def flip(array, axis, by):
+    return lax.ppermute(array, axis, [(i, i ^ by) for i in range(lax.axis_size(axis))])
+
+
+def block_shards(series, ref_list):
+    chan_rows, time_len = series.shape
+    groups, refs = ref_list.shape
+    n_tm = lax.axis_size("tm")
+    total = time_len * n_tm
+    lags_dev = LAGS // n_tm
+    group = lax.axis_index("chan").astype(jnp.int32)
+    smem = pl.BlockSpec(memory_space=pltpu.SMEM)
+    vmem = pl.BlockSpec(memory_space=pltpu.VMEM)
+    hbm = pl.BlockSpec(memory_space=pl.ANY)
+    big = pltpu.CompilerParams(vmem_limit_bytes=58 * 2**20)
+    own_pool = pl.pallas_call(
+        select_kernel,
+        in_specs=[smem, vmem, vmem],
+        out_specs=vmem,
+        out_shape=jax.ShapeDtypeStruct((POOL, time_len), BF16),
+    )(group[None], ref_list, series)
+    pool_x = flip(own_pool, "tm", 2)
+    series_x = flip(series, "tm", 2)
+    series_c = flip(series, "tm", 1)
+    series_xc = flip(series_x, "tm", 1)
+    mine = lax.dynamic_slice_in_dim(ref_list, group, 1, 0)
+    order = pl.pallas_call(
+        functools.partial(order_kernel, chan_rows=chan_rows),
+        in_specs=[smem, vmem, vmem],
+        out_specs=vmem,
+        out_shape=jax.ShapeDtypeStruct((groups * POOL, refs), BF16),
+        cost_estimate=pl.CostEstimate(flops=10**9, bytes_accessed=10**6, transcendentals=0),
+    )(group[None], ref_list, mine)
+    pair = jnp.concatenate([own_pool, pool_x], axis=0)
+    along_z = [pair] + [flip(pair, "chan", 2 * d) for d in range(1, groups // 2)]
+    pool = []
+    for piece in along_z:
+        pool += [piece, flip(piece, "chan", 1)]
+    pieces = []
+    for piece in pool:
+        pieces += [piece, flip(piece, "tm", 1)]
+    n_pool = len(pieces)
+    windows = total // WIN
+    out = pl.pallas_call(
+        functools.partial(
+            corr_kernel, time_len=time_len, n_tm=n_tm, n_pool=n_pool, scale=1.0 / math.sqrt(total)
+        ),
+        grid=(8,),
+        in_specs=[smem, pl.BlockSpec((groups * POOL, refs), lambda i: (0, 0))] + [hbm] * (n_tm + n_pool),
+        out_specs=pl.BlockSpec((1, 4, 1, chan_rows, refs), lambda i: (i // 4, 0, i % 4, 0, 0)),
+        out_shape=jax.ShapeDtypeStruct((2, 4, 4, chan_rows, refs), BF16),
+        scratch_shapes=[
+            pltpu.VMEM((chan_rows, total), BF16),
+            pltpu.VMEM((groups * POOL, total), BF16),
+            pltpu.VMEM((2, PH, total // PH + 8, 128), F32),
+            pltpu.VMEM((9, chan_rows, total // 4), BF16),
+            pltpu.VMEM((4, windows, 35 * (WIN // PH), refs), BF16),
+            pltpu.SemaphoreType.DMA((n_tm,)),
+            pltpu.SemaphoreType.DMA((n_pool // 2, 2, 2)),
+        ],
+        compiler_params=big,
+        cost_estimate=pl.CostEstimate(flops=15 * 10**9, bytes_accessed=2 * 10**7, transcendentals=0),
+    )(lax.axis_index("tm").astype(jnp.int32)[None], order, series, series_c, series_x, series_xc, *pieces)
+    return out.reshape(lags_dev, chan_rows, refs)
+
+
 def solution(mesh):
     in_specs = (P("chan", "tm"), P())
     out_specs = P("tm", "chan", None)
-    return jax.shard_map(shards, mesh=mesh, in_specs=in_specs, out_specs=out_specs, check_vma=False)
+    sizes = (mesh.shape["chan"], mesh.shape["tm"])
+    body = block_shards if sizes == (8, 4) else general_shards
+    return jax.shard_map(body, mesh=mesh, in_specs=in_specs, out_specs=out_specs, check_vma=False)

time: 785 us -> 95.3 us (0.12)
  local copies, waits for them, and re-layouts: 326 us -> 2.31 us
  waiting for transfers between devices: 334 us -> 31.7 us
  matrix products: 95.2 us -> 0 us
  Pallas kernels: 0 us -> 43.8 us
  starting transfers between devices: 1.33 us -> 16.2 us
  between operations: 13.5 us -> 0.2 us
  loops' own time: 11.2 us -> 0 us
    gather x385 -> x0, local copies, waits for them, and re-layouts: 315 us -> none
    unnamed x3 -> x0, waiting for transfers between devices: 234 us -> none
    all_gather x1 -> x0, waiting for transfers between devices: 98.6 us -> none  [shards(): gathered_all = lax.all_gather(series, 'chan', axis=0, tiled=True)]
    dot_general x16 -> x0, matrix products: 95.2 us -> none  [lag_block(): jnp.einsum('jct,rt->jcr', windows, ref_block, preferred_element_type=jnp....]
    pallas_call x0 -> x3, Pallas kernels: none -> 43.8 us  [the longest x1 30.7 us: block_shards(): pl.pallas_call(functools.partial(corr_kernel, time_len=time_len, n_tm=n_t...]
    ppermute x1 -> x19, waiting for transfers between devices: 1.2 us -> 31.7 us  [flip(): lax.ppermute(array, axis, [(i, i ^ by) for i in range(lax.axis_size(axis))])]
    ppermute x1 -> x19, starting transfers between devices: 1.29 us -> 16.2 us  [flip(): lax.ppermute(array, axis, [(i, i ^ by) for i in range(lax.axis_size(axis))])]
    another operation x17 -> x0, loops' own time: 11.2 us -> none  [the longest x1 10.8 us: shards(): lax.scan(lag_step, None, jnp.arange(lax.axis_size('tm') * lags_dev // 8,...]
  transfers between devices with their start and end apart: 3 -> 19, of which waited for: 3 -> 6; matrix products, arithmetic and copies ran while one was open for 0% -> 2% of each run, Pallas kernels for 0% -> 14%
where the time goes in v1:
time: 95.3 us; the launch traced here: 95 us
  Pallas kernels  43.8 us (46%)
  waiting for transfers between devices  31.7 us (33%)
  starting transfers between devices  16.2 us (17%)
  local copies, waits for them, and re-layouts  2.31 us (2%)
    ppermute x19, waiting for transfers between devices, flip(): lax.ppermute(array, axis, [(i, i ^ by) for i in range(lax.axis_size(axis))])  31.7 us
    pallas_call x1, Pallas kernels, block_shards(): pl.pallas_call(functools.partial(corr_kernel, time_len=time_len, n_tm=n_t...  30.7 us
    ppermute x19, starting transfers between devices, flip(): lax.ppermute(array, axis, [(i, i ^ by) for i in range(lax.axis_size(axis))])  16.2 us
    pallas_call x1, Pallas kernels, block_shards(): pl.pallas_call(functools.partial(order_kernel, chan_rows=chan_rows), in_s...  9.82 us
    pallas_call x1, Pallas kernels, block_shards(): pl.pallas_call(select_kernel, in_specs=[smem, vmem, vmem], out_specs=vmem...  3.25 us
  transfers between devices with their start and end apart: 19, of which 6 were waited for; matrix products, arithmetic and copies ran while one was open for 2% of the time, Pallas kernels for 14%

profile of v1, /device:TPU:0, one launch (start us, length us, event | category | flops | bytes accessed | tf_op | source)
XLA Modules:
  0.0 95.0 jit_solution(6300977200342423013)
XLA Ops:
  0.0 2.9 %collective-permute-start.1 = (bf16[512,768]{1,0:T(8,128)(2,1)}, bf16[512,768]{1,0:T(8,128)(2,1)S(1)}, u32[]{:S(2)}, u32[]{:S(2)}) collective-permute-start(bf16[512,768]{1,0:T(8,128)(2,1)} %refs_0_.1), channel_id=1, source_target_pairs={{0,2},{1,3},{2,0},{3,1},{4,6},{5,7},{6,4},{7,5},{8,10},{9,11},{10,... | collective-permute-start | bytes 2359304 | tf_op jit(solution)/shard_map/ppermute | solution.py:206
  2.9 0.0 collective-permute-start
  2.9 17.7 %collective-permute-done.1.refs_2_ = bf16[512,768]{1,0:T(8,128)(2,1)S(1)} collective-permute-done((bf16[512,768]{1,0:T(8,128)(2,1)}, bf16[512,768]{1,0:T(8,128)(2,1)S(1)}, u32[]{:S(2)}, u32[]{:S(2)}) %collective-permute-start.1) | collective-permute-done | bytes 786464 | tf_op jit(solution)/shard_map/ppermute | solution.py:206
  20.7 0.0 copy-start.1
  20.7 0.0 collective-permute-start.2
  20.7 3.3 %shard_map.29 = bf16[32,768]{1,0:T(8,128)(2,1)} custom-call(s32[1]{0:T(128)} %bitcast.1.group_ref, s32[8,256]{1,0:T(8,128)} %list_ref.3, bf16[512,768]{1,0:T(8,128)(2,1)} %refs_0_.1), custom_call_target="tpu_custom_call" | custom-call | tf_op jit(solution)/shard_map/pallas_call | solution.py:220
  23.9 1.7 %collective-permute-start.3 = (bf16[32,768]{1,0:T(8,128)(2,1)}, bf16[32,768]{1,0:T(8,128)(2,1)S(1)}, u32[]{:S(2)}, u32[]{:S(2)}) collective-permute-start(bf16[32,768]{1,0:T(8,128)(2,1)} %shard_map.29), channel_id=1, source_target_pairs={{0,2},{1,3},{2,0},{3,1},{4,6},{5,7},{6,4},{7,5},{8,10},{9,11},{10,... | collective-permute-start | bytes 147464 | tf_op jit(solution)/shard_map/ppermute | solution.py:206
  25.7 2.6 %collective-permute-done.3 = bf16[32,768]{1,0:T(8,128)(2,1)S(1)} collective-permute-done((bf16[32,768]{1,0:T(8,128)(2,1)}, bf16[32,768]{1,0:T(8,128)(2,1)S(1)}, u32[]{:S(2)}, u32[]{:S(2)}) %collective-permute-start.3) | collective-permute-done | bytes 49184 | tf_op jit(solution)/shard_map/ppermute | solution.py:206
  28.2 0.8 pad_maximum_fusion.refs_4_
  29.1 3.9 %collective-permute-start.15 = (bf16[64,768]{1,0:T(8,128)(2,1)S(1)}, bf16[64,768]{1,0:T(8,128)(2,1)S(1)}, u32[]{:S(2)}, u32[]{:S(2)}) collective-permute-start(bf16[64,768]{1,0:T(8,128)(2,1)S(1)} %pad_maximum_fusion.refs_4_), channel_id=1, source_target_pairs={{0,24},{4,28},{8,16},{12,20},{16,8},{20,12},{24,0},{28,4},{1,25},{... | collective-permute-start | bytes 294920 | tf_op jit(solution)/shard_map/ppermute | solution.py:206
  33.0 0.0 collective-permute-start.11
  33.0 0.6 collective-permute-start.7
  33.6 2.9 %collective-permute-done.15.refs_16_ = bf16[64,768]{1,0:T(8,128)(2,1)S(1)} collective-permute-done((bf16[64,768]{1,0:T(8,128)(2,1)S(1)}, bf16[64,768]{1,0:T(8,128)(2,1)S(1)}, u32[]{:S(2)}, u32[]{:S(2)}) %collective-permute-start.15) | collective-permute-done | bytes 98336 | tf_op jit(solution)/shard_map/ppermute | solution.py:206
  36.5 1.5 %collective-permute-start.5 = (bf16[64,768]{1,0:T(8,128)(2,1)S(1)}, bf16[64,768]{1,0:T(8,128)(2,1)S(1)}, u32[]{:S(2)}, u32[]{:S(2)}) collective-permute-start(bf16[64,768]{1,0:T(8,128)(2,1)S(1)} %pad_maximum_fusion.refs_4_), channel_id=1, source_target_pairs={{0,4},{4,0},{8,12},{12,8},{16,20},{20,16},{24,28},{28,24},{1,5},{5... | collective-permute-start | bytes 294920 | tf_op jit(solution)/shard_map/ppermute | solution.py:206
  38.0 2.5 %collective-permute-done.11.refs_12_ = bf16[64,768]{1,0:T(8,128)(2,1)S(1)} collective-permute-done((bf16[64,768]{1,0:T(8,128)(2,1)S(1)}, bf16[64,768]{1,0:T(8,128)(2,1)S(1)}, u32[]{:S(2)}, u32[]{:S(2)}) %collective-permute-start.11) | collective-permute-done | bytes 98336 | tf_op jit(solution)/shard_map/ppermute | solution.py:206
  40.5 0.0 collective-permute-start.4
  40.5 0.0 collective-permute-done.7.refs_8_
  40.5 0.0 copy-start.6
  40.5 1.6 %collective-permute-start.17 = (bf16[64,768]{1,0:T(8,128)(2,1)S(1)}, bf16[64,768]{1,0:T(8,128)(2,1)S(1)}, u32[]{:S(2)}, u32[]{:S(2)}) collective-permute-start(bf16[64,768]{1,0:T(8,128)(2,1)S(1)} %collective-permute-done.15.refs_16_), channel_id=1, source_target_pairs={{0,4},{4,0},{8,12},{12,8},{16,20},{20,16},{24,28},{28,24},{1,5},{5... | collective-permute-start | bytes 294920 | tf_op jit(solution)/shard_map/ppermute | solution.py:206
  42.1 0.0 collective-permute-done.5.refs_6_
  42.1 0.2 collective-permute-start.16
  42.3 0.0 collective-permute-done.4.refs_5_
  42.3 1.0 %collective-permute-start.13 = (bf16[64,768]{1,0:T(8,128)(2,1)S(1)}, bf16[64,768]{1,0:T(8,128)(2,1)S(1)}, u32[]{:S(2)}, u32[]{:S(2)}) collective-permute-start(bf16[64,768]{1,0:T(8,128)(2,1)S(1)} %collective-permute-done.11.refs_12_), channel_id=1, source_target_pairs={{0,4},{4,0},{8,12},{12,8},{16,20},{20,16},{24,28},{28,24},{1,5},{5... | collective-permute-start | bytes 294920 | tf_op jit(solution)/shard_map/ppermute | solution.py:206
  43.3 2.9 %collective-permute-done.17.refs_18_ = bf16[64,768]{1,0:T(8,128)(2,1)S(1)} collective-permute-done((bf16[64,768]{1,0:T(8,128)(2,1)S(1)}, bf16[64,768]{1,0:T(8,128)(2,1)S(1)}, u32[]{:S(2)}, u32[]{:S(2)}) %collective-permute-start.17) | collective-permute-done | bytes 98336 | tf_op jit(solution)/shard_map/ppermute | solution.py:206
  46.2 0.0 collective-permute-start.12
  46.2 0.0 collective-permute-done.16.refs_17_
  46.2 0.0 copy-start.10
  46.2 1.6 %collective-permute-start.9 = (bf16[64,768]{1,0:T(8,128)(2,1)S(1)}, bf16[64,768]{1,0:T(8,128)(2,1)S(1)}, u32[]{:S(2)}, u32[]{:S(2)}) collective-permute-start(bf16[64,768]{1,0:T(8,128)(2,1)S(1)} %collective-permute-done.7.refs_8_), channel_id=1, source_target_pairs={{0,4},{4,0},{8,12},{12,8},{16,20},{20,16},{24,28},{28,24},{1,5},{5... | collective-permute-start | bytes 294920 | tf_op jit(solution)/shard_map/ppermute | solution.py:206
  47.8 0.1 collective-permute-done.13.refs_14_
  47.8 0.1 collective-permute-start.8
  47.9 0.0 collective-permute-done.12.refs_13_
  48.0 0.4 collective-permute-start.6
  48.3 3.1 %collective-permute-done.9.refs_10_ = bf16[64,768]{1,0:T(8,128)(2,1)S(1)} collective-permute-done((bf16[64,768]{1,0:T(8,128)(2,1)S(1)}, bf16[64,768]{1,0:T(8,128)(2,1)S(1)}, u32[]{:S(2)}, u32[]{:S(2)}) %collective-permute-start.9) | collective-permute-done | bytes 98336 | tf_op jit(solution)/shard_map/ppermute | solution.py:206
  51.4 0.0 collective-permute-start.18
  51.4 0.0 collective-permute-done.8.refs_9_
  51.4 0.0 copy-start.14
  51.4 0.5 collective-permute-start.14
  51.9 0.0 collective-permute-done.6.refs_7_
  51.9 0.1 collective-permute-start.10
  52.0 1.3 %constant_dynamic-slice_fusion.mine_ref = s32[1,256]{1,0:T(1,128)} fusion(s32[8,256]{1,0:T(8,128)} %list_ref.3, s32[]{:T(128)S(6)} %select_n.3), kind=kLoop, calls=%fused_computation.1 | loop fusion | bytes 2052 | tf_op jit(solution)/shard_map/dynamic_slice | solution.py:230
  53.3 9.8 %shard_map.28.order_ref = bf16[256,256]{1,0:T(8,128)(2,1)} custom-call(s32[1]{0:T(128)} %bitcast.1.group_ref, s32[8,256]{1,0:T(8,128)} %list_ref.3, s32[1,256]{1,0:T(1,128)} %constant_dynamic-slice_fusion.mine_ref), custom_call_target="tpu_custom_call" | custom-call | flops 1000000000 | bytes 1000000 | tf_op jit(solution)/shard_map/pallas_call | solution.py:231
  63.1 0.0 collective-permute-done.18.refs_19_
  63.1 0.0 collective-permute-done.14.refs_15_
  63.1 0.0 collective-permute-done.10.refs_11_
  63.1 0.0 collective-permute-done.refs_1_
  63.1 0.0 copy-start.2
  63.1 0.0 collective-permute-done.2.refs_3_
  63.1 0.0 copy-start.3
  63.1 0.0 copy-done.1
  63.2 0.0 copy-done
  63.2 0.0 copy-done.4
  63.2 0.0 copy-done.5
  63.2 0.0 copy-done.6
  63.2 0.0 copy-done.7
  63.2 0.0 copy-done.8
  63.2 0.0 copy-done.9
  63.2 0.0 copy-done.10
  63.2 0.0 copy-done.11
  63.2 0.0 copy-done.12
  63.3 0.0 copy-done.13
  63.3 0.0 copy-done.14
  63.3 0.8 copy-done.2
  64.0 0.2 copy-done.3
  64.3 30.7 %shard_map.30 = bf16[2,4,4,512,256]{4,3,2,1,0:T(8,128)(2,1)} custom-call(s32[1]{0:T(128)} %bitcast.tm_ref, bf16[256,256]{1,0:T(8,128)(2,1)} %shard_map.28.order_ref, bf16[512,768]{1,0:T(8,128)(2,1)} %refs_0_.1, bf16[512,768]{1,0:T(8,128)(2,1)} %copy-done.2, bf16[512,768]{1,0:T(8,128)(2,1)} %copy-done.1, bf16[512,768]{1,0:T(8,128)(2,1)} %copy-done.3, ...), custom_call_target="tpu_custom_call" | custom-call | flops 15000000512 | bytes 20000000 | tf_op jit(solution)/shard_map/pallas_call | solution.py:248
  (9 shorter events, 0.0 us)
Async XLA Ops:
  0.0 20.7 %collective-permute-start.1 = (bf16[512,768]{1,0:T(8,128)(2,1)}, bf16[512,768]{1,0:T(8,128)(2,1)S(1)}, u32[]{:S(2)}, u32[]{:S(2)}) collective-permute-start(bf16[512,768]{1,0:T(8,128)(2,1)} %refs_0_.1), channel_id=1, source_target_pairs={{0,2},{1,3},{2,0},{3,1},{4,6},{5,7},{6,4},{7,5},{8,10},{9,11},{10,... | collective-permute-start | bytes 2359304 | tf_op jit(solution)/shard_map/ppermute | solution.py:206
  2.9 60.2 %collective-permute-start = (bf16[512,768]{1,0:T(8,128)(2,1)}, bf16[512,768]{1,0:T(8,128)(2,1)S(1)}, u32[]{:S(2)}, u32[]{:S(2)}) collective-permute-start(bf16[512,768]{1,0:T(8,128)(2,1)} %refs_0_.1), channel_id=1, source_target_pairs={{0,1},{1,0},{2,3},{3,2},{4,5},{5,4},{6,7},{7,6},{8,9},{9,8},{10,11... | collective-permute-start | bytes 2359304 | tf_op jit(solution)/shard_map/ppermute | solution.py:206
  20.7 42.5 %copy-start.1 = (bf16[512,768]{1,0:T(8,128)(2,1)}, bf16[512,768]{1,0:T(8,128)(2,1)S(1)}, u32[]{:S(2)}) copy-start(bf16[512,768]{1,0:T(8,128)(2,1)S(1)} %collective-permute-done.1.refs_2_) | copy-start | bytes 2359300
  20.7 42.4 %collective-permute-start.2 = (bf16[512,768]{1,0:T(8,128)(2,1)S(1)}, bf16[512,768]{1,0:T(8,128)(2,1)S(1)}, u32[]{:S(2)}, u32[]{:S(2)}) collective-permute-start(bf16[512,768]{1,0:T(8,128)(2,1)S(1)} %collective-permute-done.1.refs_2_), channel_id=1, source_target_pairs={{0,1},{1,0},{2,3},{3,2},{4,5},{5,4},{6,7},{7,6},{8,9},{9,8},{10,11... | collective-permute-start | bytes 2359304 | tf_op jit(solution)/shard_map/ppermute | solution.py:206
  23.9 4.3 %collective-permute-start.3 = (bf16[32,768]{1,0:T(8,128)(2,1)}, bf16[32,768]{1,0:T(8,128)(2,1)S(1)}, u32[]{:S(2)}, u32[]{:S(2)}) collective-permute-start(bf16[32,768]{1,0:T(8,128)(2,1)} %shard_map.29), channel_id=1, source_target_pairs={{0,2},{1,3},{2,0},{3,1},{4,6},{5,7},{6,4},{7,5},{8,10},{9,11},{10,... | collective-permute-start | bytes 147464 | tf_op jit(solution)/shard_map/ppermute | solution.py:206
  29.1 34.1 %copy-start = (bf16[64,768]{1,0:T(8,128)(2,1)}, bf16[64,768]{1,0:T(8,128)(2,1)S(1)}, u32[]{:S(2)}) copy-start(bf16[64,768]{1,0:T(8,128)(2,1)S(1)} %pad_maximum_fusion.refs_4_) | copy-start | bytes 294916
  29.1 7.4 %collective-permute-start.15 = (bf16[64,768]{1,0:T(8,128)(2,1)S(1)}, bf16[64,768]{1,0:T(8,128)(2,1)S(1)}, u32[]{:S(2)}, u32[]{:S(2)}) collective-permute-start(bf16[64,768]{1,0:T(8,128)(2,1)S(1)} %pad_maximum_fusion.refs_4_), channel_id=1, source_target_pairs={{0,24},{4,28},{8,16},{12,20},{16,8},{20,12},{24,0},{28,4},{1,25},{... | collective-permute-start | bytes 294920 | tf_op jit(solution)/shard_map/ppermute | solution.py:206
  33.0 7.5 %collective-permute-start.11 = (bf16[64,768]{1,0:T(8,128)(2,1)S(1)}, bf16[64,768]{1,0:T(8,128)(2,1)S(1)}, u32[]{:S(2)}, u32[]{:S(2)}) collective-permute-start(bf16[64,768]{1,0:T(8,128)(2,1)S(1)} %pad_maximum_fusion.refs_4_), channel_id=1, source_target_pairs={{0,16},{4,20},{8,24},{12,28},{16,0},{20,4},{24,8},{28,12},{1,17},{... | collective-permute-start | bytes 294920 | tf_op jit(solution)/shard_map/ppermute | solution.py:206
  33.0 7.5 %collective-permute-start.7 = (bf16[64,768]{1,0:T(8,128)(2,1)S(1)}, bf16[64,768]{1,0:T(8,128)(2,1)S(1)}, u32[]{:S(2)}, u32[]{:S(2)}) collective-permute-start(bf16[64,768]{1,0:T(8,128)(2,1)S(1)} %pad_maximum_fusion.refs_4_), channel_id=1, source_target_pairs={{0,8},{4,12},{8,0},{12,4},{16,24},{20,28},{24,16},{28,20},{1,9},{5... | collective-permute-start | bytes 294920 | tf_op jit(solution)/shard_map/ppermute | solution.py:206
  36.5 26.7 %copy-start.4 = (bf16[64,768]{1,0:T(8,128)(2,1)}, bf16[64,768]{1,0:T(8,128)(2,1)S(1)}, u32[]{:S(2)}) copy-start(bf16[64,768]{1,0:T(8,128)(2,1)S(1)} %collective-permute-done.15.refs_16_) | copy-start | bytes 294916
  36.5 5.6 %collective-permute-start.5 = (bf16[64,768]{1,0:T(8,128)(2,1)S(1)}, bf16[64,768]{1,0:T(8,128)(2,1)S(1)}, u32[]{:S(2)}, u32[]{:S(2)}) collective-permute-start(bf16[64,768]{1,0:T(8,128)(2,1)S(1)} %pad_maximum_fusion.refs_4_), channel_id=1, source_target_pairs={{0,4},{4,0},{8,12},{12,8},{16,20},{20,16},{24,28},{28,24},{1,5},{5... | collective-permute-start | bytes 294920 | tf_op jit(solution)/shard_map/ppermute | solution.py:206
  40.5 22.7 %copy-start.5 = (bf16[64,768]{1,0:T(8,128)(2,1)}, bf16[64,768]{1,0:T(8,128)(2,1)S(1)}, u32[]{:S(2)}) copy-start(bf16[64,768]{1,0:T(8,128)(2,1)S(1)} %collective-permute-done.11.refs_12_) | copy-start | bytes 294916
  40.5 1.8 %collective-permute-start.4 = (bf16[64,768]{1,0:T(8,128)(2,1)S(1)}, bf16[64,768]{1,0:T(8,128)(2,1)S(1)}, u32[]{:S(2)}, u32[]{:S(2)}) collective-permute-start(bf16[64,768]{1,0:T(8,128)(2,1)S(1)} %pad_maximum_fusion.refs_4_), channel_id=1, source_target_pairs={{0,1},{1,0},{2,3},{3,2},{4,5},{5,4},{6,7},{7,6},{8,9},{9,8},{10,11... | collective-permute-start | bytes 294920 | tf_op jit(solution)/shard_map/ppermute | solution.py:206
  40.5 22.7 %copy-start.6 = (bf16[64,768]{1,0:T(8,128)(2,1)}, bf16[64,768]{1,0:T(8,128)(2,1)S(1)}, u32[]{:S(2)}) copy-start(bf16[64,768]{1,0:T(8,128)(2,1)S(1)} %collective-permute-done.7.refs_8_) | copy-start | bytes 294916
  40.5 5.7 %collective-permute-start.17 = (bf16[64,768]{1,0:T(8,128)(2,1)S(1)}, bf16[64,768]{1,0:T(8,128)(2,1)S(1)}, u32[]{:S(2)}, u32[]{:S(2)}) collective-permute-start(bf16[64,768]{1,0:T(8,128)(2,1)S(1)} %collective-permute-done.15.refs_16_), channel_id=1, source_target_pairs={{0,4},{4,0},{8,12},{12,8},{16,20},{20,16},{24,28},{28,24},{1,5},{5... | collective-permute-start | bytes 294920 | tf_op jit(solution)/shard_map/ppermute | solution.py:206
  42.1 21.1 %copy-start.7 = (bf16[64,768]{1,0:T(8,128)(2,1)}, bf16[64,768]{1,0:T(8,128)(2,1)S(1)}, u32[]{:S(2)}) copy-start(bf16[64,768]{1,0:T(8,128)(2,1)S(1)} %collective-permute-done.5.refs_6_) | copy-start | bytes 294916
  42.1 4.1 %collective-permute-start.16 = (bf16[64,768]{1,0:T(8,128)(2,1)S(1)}, bf16[64,768]{1,0:T(8,128)(2,1)S(1)}, u32[]{:S(2)}, u32[]{:S(2)}) collective-permute-start(bf16[64,768]{1,0:T(8,128)(2,1)S(1)} %collective-permute-done.15.refs_16_), channel_id=1, source_target_pairs={{0,1},{1,0},{2,3},{3,2},{4,5},{5,4},{6,7},{7,6},{8,9},{9,8},{10,11... | collective-permute-start | bytes 294920 | tf_op jit(solution)/shard_map/ppermute | solution.py:206
  42.3 20.9 %copy-start.8 = (bf16[64,768]{1,0:T(8,128)(2,1)}, bf16[64,768]{1,0:T(8,128)(2,1)S(1)}, u32[]{:S(2)}) copy-start(bf16[64,768]{1,0:T(8,128)(2,1)S(1)} %collective-permute-done.4.refs_5_) | copy-start | bytes 294916
  42.3 5.6 %collective-permute-start.13 = (bf16[64,768]{1,0:T(8,128)(2,1)S(1)}, bf16[64,768]{1,0:T(8,128)(2,1)S(1)}, u32[]{:S(2)}, u32[]{:S(2)}) collective-permute-start(bf16[64,768]{1,0:T(8,128)(2,1)S(1)} %collective-permute-done.11.refs_12_), channel_id=1, source_target_pairs={{0,4},{4,0},{8,12},{12,8},{16,20},{20,16},{24,28},{28,24},{1,5},{5... | collective-permute-start | bytes 294920 | tf_op jit(solution)/shard_map/ppermute | solution.py:206
  46.2 17.0 %copy-start.9 = (bf16[64,768]{1,0:T(8,128)(2,1)}, bf16[64,768]{1,0:T(8,128)(2,1)S(1)}, u32[]{:S(2)}) copy-start(bf16[64,768]{1,0:T(8,128)(2,1)S(1)} %collective-permute-done.17.refs_18_) | copy-start | bytes 294916
  46.2 1.8 %collective-permute-start.12 = (bf16[64,768]{1,0:T(8,128)(2,1)S(1)}, bf16[64,768]{1,0:T(8,128)(2,1)S(1)}, u32[]{:S(2)}, u32[]{:S(2)}) collective-permute-start(bf16[64,768]{1,0:T(8,128)(2,1)S(1)} %collective-permute-done.11.refs_12_), channel_id=1, source_target_pairs={{0,1},{1,0},{2,3},{3,2},{4,5},{5,4},{6,7},{7,6},{8,9},{9,8},{10,11... | collective-permute-start | bytes 294920 | tf_op jit(solution)/shard_map/ppermute | solution.py:206
  46.2 17.0 %copy-start.10 = (bf16[64,768]{1,0:T(8,128)(2,1)}, bf16[64,768]{1,0:T(8,128)(2,1)S(1)}, u32[]{:S(2)}) copy-start(bf16[64,768]{1,0:T(8,128)(2,1)S(1)} %collective-permute-done.16.refs_17_) | copy-start | bytes 294916
  46.2 5.2 %collective-permute-start.9 = (bf16[64,768]{1,0:T(8,128)(2,1)S(1)}, bf16[64,768]{1,0:T(8,128)(2,1)S(1)}, u32[]{:S(2)}, u32[]{:S(2)}) collective-permute-start(bf16[64,768]{1,0:T(8,128)(2,1)S(1)} %collective-permute-done.7.refs_8_), channel_id=1, source_target_pairs={{0,4},{4,0},{8,12},{12,8},{16,20},{20,16},{24,28},{28,24},{1,5},{5... | collective-permute-start | bytes 294920 | tf_op jit(solution)/shard_map/ppermute | solution.py:206
  47.8 15.4 %copy-start.11 = (bf16[64,768]{1,0:T(8,128)(2,1)}, bf16[64,768]{1,0:T(8,128)(2,1)S(1)}, u32[]{:S(2)}) copy-start(bf16[64,768]{1,0:T(8,128)(2,1)S(1)} %collective-permute-done.13.refs_14_) | copy-start | bytes 294916
  47.8 3.6 %collective-permute-start.8 = (bf16[64,768]{1,0:T(8,128)(2,1)S(1)}, bf16[64,768]{1,0:T(8,128)(2,1)S(1)}, u32[]{:S(2)}, u32[]{:S(2)}) collective-permute-start(bf16[64,768]{1,0:T(8,128)(2,1)S(1)} %collective-permute-done.7.refs_8_), channel_id=1, source_target_pairs={{0,1},{1,0},{2,3},{3,2},{4,5},{5,4},{6,7},{7,6},{8,9},{9,8},{10,11... | collective-permute-start | bytes 294920 | tf_op jit(solution)/shard_map/ppermute | solution.py:206
  47.9 15.3 %copy-start.12 = (bf16[64,768]{1,0:T(8,128)(2,1)}, bf16[64,768]{1,0:T(8,128)(2,1)S(1)}, u32[]{:S(2)}) copy-start(bf16[64,768]{1,0:T(8,128)(2,1)S(1)} %collective-permute-done.12.refs_13_) | copy-start | bytes 294916
  48.0 4.0 %collective-permute-start.6 = (bf16[64,768]{1,0:T(8,128)(2,1)S(1)}, bf16[64,768]{1,0:T(8,128)(2,1)}, u32[]{:S(2)}, u32[]{:S(2)}) collective-permute-start(bf16[64,768]{1,0:T(8,128)(2,1)S(1)} %collective-permute-done.5.refs_6_), channel_id=1, source_target_pairs={{0,1},{1,0},{2,3},{3,2},{4,5},{5,4},{6,7},{7,6},{8,9},{9,8},{10,11... | collective-permute-start | bytes 294920 | tf_op jit(solution)/shard_map/ppermute | solution.py:206
  51.4 11.9 %copy-start.13 = (bf16[64,768]{1,0:T(8,128)(2,1)}, bf16[64,768]{1,0:T(8,128)(2,1)S(1)}, u32[]{:S(2)}) copy-start(bf16[64,768]{1,0:T(8,128)(2,1)S(1)} %collective-permute-done.9.refs_10_) | copy-start | bytes 294916
  51.4 11.7 %collective-permute-start.18 = (bf16[64,768]{1,0:T(8,128)(2,1)S(1)}, bf16[64,768]{1,0:T(8,128)(2,1)}, u32[]{:S(2)}, u32[]{:S(2)}) collective-permute-start(bf16[64,768]{1,0:T(8,128)(2,1)S(1)} %collective-permute-done.17.refs_18_), channel_id=1, source_target_pairs={{0,1},{1,0},{2,3},{3,2},{4,5},{5,4},{6,7},{7,6},{8,9},{9,8},{10,11... | collective-permute-start | bytes 294920 | tf_op jit(solution)/shard_map/ppermute | solution.py:206
  51.4 11.9 %copy-start.14 = (bf16[64,768]{1,0:T(8,128)(2,1)}, bf16[64,768]{1,0:T(8,128)(2,1)S(1)}, u32[]{:S(2)}) copy-start(bf16[64,768]{1,0:T(8,128)(2,1)S(1)} %collective-permute-done.8.refs_9_) | copy-start | bytes 294916
  51.4 11.7 %collective-permute-start.14 = (bf16[64,768]{1,0:T(8,128)(2,1)S(1)}, bf16[64,768]{1,0:T(8,128)(2,1)}, u32[]{:S(2)}, u32[]{:S(2)}) collective-permute-start(bf16[64,768]{1,0:T(8,128)(2,1)S(1)} %collective-permute-done.13.refs_14_), channel_id=1, source_target_pairs={{0,1},{1,0},{2,3},{3,2},{4,5},{5,4},{6,7},{7,6},{8,9},{9,8},{10,11... | collective-permute-start | bytes 294920 | tf_op jit(solution)/shard_map/ppermute | solution.py:206
  51.9 11.2 %collective-permute-start.10 = (bf16[64,768]{1,0:T(8,128)(2,1)S(1)}, bf16[64,768]{1,0:T(8,128)(2,1)}, u32[]{:S(2)}, u32[]{:S(2)}) collective-permute-start(bf16[64,768]{1,0:T(8,128)(2,1)S(1)} %collective-permute-done.9.refs_10_), channel_id=1, source_target_pairs={{0,1},{1,0},{2,3},{3,2},{4,5},{5,4},{6,7},{7,6},{8,9},{9,8},{10,11... | collective-permute-start | bytes 294920 | tf_op jit(solution)/shard_map/ppermute | solution.py:206
  63.1 0.9 copy-start.2
  63.1 1.1 %copy-start.3 = (bf16[512,768]{1,0:T(8,128)(2,1)}, bf16[512,768]{1,0:T(8,128)(2,1)S(1)}, u32[]{:S(2)}) copy-start(bf16[512,768]{1,0:T(8,128)(2,1)S(1)} %collective-permute-done.2.refs_3_) | copy-start | bytes 2359300

commit v2 on v0

--- a/solution.py
+++ b/solution.py
@@ -1,11 +1,21 @@
+import functools
 import math
 
 import jax
 import jax.numpy as jnp
 from jax import lax
+from jax.experimental import pallas as pl
+from jax.experimental.pallas import tpu as pltpu
 from jax.sharding import PartitionSpec as P
 
 LAGS = 128
+POOL = 32
+BF16 = jnp.bfloat16
+F32 = jnp.float32
+
+
+def dot(a, b):
+    return jnp.dot(a, b, preferred_element_type=F32)
 
 
 def shifted(array, axis, by):
@@ -25,7 +35,7 @@
     )
 
 
-def shards(series, ref_list):
+def general_shards(series, ref_list):
     chan_rows, time_len = series.shape
     ref_count = ref_list.shape[1]
     group_index = lax.axis_index("chan")
@@ -51,7 +61,287 @@
     )
 
 
+def ones_where(condition):
+    return jnp.where(condition, 1.0, 0.0).astype(BF16)
+
+
+def iota(shape, dim):
+    return lax.broadcasted_iota(jnp.int32, shape, dim)
+
+
+def nt_dot(a, b):
+    return lax.dot_general(a, b, (((1,), (1,)), ((), ())), preferred_element_type=F32)
+
+
+def marks_of(list_ref, highs):
+    groups, width = list_ref.shape
+    rows = [list_ref[g : g + 1, c : c + 128] for g in range(groups) for c in range(0, width, 128)]
+    high = jnp.concatenate([ones_where(iota((highs, 128), 0) == (row >> 7)) for row in rows], axis=1)
+    low = jnp.concatenate([ones_where(iota((128, 128), 0) == (row & 127)) for row in rows], axis=1)
+    return high, low
+
+
+def select_kernel(group_ref, list_ref, s_hbm, pool_ref, pair_ref, s_ref, rank_ref, sem):
+    copy = pltpu.make_async_copy(s_hbm, s_ref, sem)
+    copy.start()
+    per = s_ref.shape[0] // 128
+    highs = list_ref.shape[0] * per
+    high, low = marks_of(list_ref, highs)
+    named = nt_dot(high, low) > 0.5
+    marks = ones_where(named)
+    before = ones_where(iota((128, 128), 0) < iota((128, 128), 1))
+    held = dot(marks, jnp.ones((128, 128), BF16)).astype(BF16)
+    h_to, h_from = iota((highs, highs), 0), iota((highs, highs), 1)
+    earlier = ones_where((h_to // per == h_from // per) & (h_from < h_to))
+    rank_ref[...] = jnp.where(named, dot(marks, before) + dot(earlier, held), -1.0)
+    slot = iota((POOL, 128), 0).astype(F32)
+    picks = [
+        ones_where(jnp.broadcast_to(rank_ref[pl.ds(group_ref[0] * per + h, 1), :], (POOL, 128)) == slot)
+        for h in range(per)
+    ]
+    copy.wait()
+    rows = dot(jnp.concatenate(picks, axis=1), s_ref[...]).astype(BF16)
+    pool_ref[...] = rows
+    pair_ref[:POOL] = rows
+    pair_ref[POOL:] = jnp.zeros_like(rows)
+
+
+def order_kernel(group_ref, list_ref, pool_ref, order_ref, *, per):
+    del pool_ref
+    groups, width = list_ref.shape
+    highs = groups * per
+    own = group_ref[0]
+    high, low = marks_of(list_ref, highs)
+    marks = ones_where(nt_dot(low, high) > 0.5)
+    after = ones_where(iota((128, 128), 1) < iota((128, 128), 0))
+    held = dot(jnp.ones((128, 128), BF16), marks).astype(BF16)
+    h_from, h_to = iota((highs, highs), 0), iota((highs, highs), 1)
+    earlier = ones_where((h_to // per == h_from // per) & (h_from < h_to))
+    rank = dot(after, marks) + dot(held, earlier)
+    place = rank + (POOL * ((iota((128, highs), 1) // per) ^ own)).astype(F32)
+    mine = list_ref[pl.ds(own, 1), :]
+    mine_high = ones_where(iota((highs, width), 0) == (mine >> 7))
+    mine_low = jnp.where(iota((128, width), 0) == (mine & 127), 1.0, 0.0)
+    at = jnp.sum(dot(place.astype(BF16), mine_high) * mine_low, axis=0, keepdims=True)
+    order_ref[...] = ones_where(iota(order_ref.shape, 0).astype(F32) == at)
+
+
+PH = 16
+WIN = 512
+PER = WIN // PH
+QUARTER = WIN // 4
+COMBOS = ((0, 0), (1, 0), (1, 4), (2, 0), (3, 0), (3, 4), (2, 8), (3, 8), (3, 12))
+
+
+def series_kernel(core_ref, mine_ref, other_ref, out_ref, raw, sem):
+    time_len = mine_ref.shape[1]
+    copies = [
+        pltpu.make_async_copy(
+            ref, raw.at[:, pl.ds(pl.multiple_of((core_ref[0] ^ e) * time_len, 128), time_len)], sem.at[e]
+        )
+        for e, ref in enumerate((mine_ref, other_ref))
+    ]
+    for copy in copies:
+        copy.start()
+    at, to = iota((WIN, WIN), 0), iota((WIN, WIN), 1)
+    turn = ones_where(at == PH * (to & (PER - 1)) + to // PER)
+    for copy in copies:
+        copy.wait()
+    for b in range(raw.shape[1] // WIN):
+        turned = dot(raw[:, b * WIN : (b + 1) * WIN], turn)
+        t = [turned[:, QUARTER * g : QUARTER * (g + 1)] for g in range(4)]
+        u0, u1 = t[0] + t[2], t[1] + t[3]
+        sums = (u0 + u1, u1, -u0, t[2] + t[3], t[3], -t[2], -(t[0] + t[1]), -t[1], t[0])
+        for i, value in enumerate(sums):
+            out_ref[i, :, b * QUARTER : (b + 1) * QUARTER] = value.astype(BF16)
+
+
+def corr_kernel(tm_ref, order_ref, *refs, n_pool, time_len, scale):
+    halves = refs[:2]
+    pieces = refs[2 : 2 + n_pool]
+    out_ref, r_raw, xf, xr, rv0, rv1, sem_r = refs[2 + n_pool :]
+    me = tm_ref[0]
+    total = r_raw.shape[1]
+    windows = total // WIN
+    half_w = windows // 2
+    step = pl.program_id(0)
+
+    def slab(idx):
+        return pl.ds(pl.multiple_of(idx * PER, PER), PER)
+
+    def make(idx, rv, base, which):
+        for b in range(windows):
+            x0, x4, x8, x12 = (xr[b, slab(idx + o), :].astype(F32) for o in (0, 4, 8, 12))
+            f0 = x4 - x0
+            if 0 in which:
+                rv[0, b, slab(idx - base), :] = f0.astype(BF16)
+            if 1 in which:
+                rv[1, b, slab(idx - base), :] = (x8 - x0).astype(BF16)
+            rv[2, b, slab(idx - base), :] = ((x12 - x8) - f0).astype(BF16)
+
+    @pl.when(step == 0)
+    def _():
+        def r_copy(d, c, x):
+            lanes = pl.ds(pl.multiple_of((me ^ (c + 2 * x)) * time_len, 128), time_len)
+            return pltpu.make_async_copy(
+                pieces[2 * d + c].at[POOL * x : POOL * (x + 1)],
+                r_raw.at[POOL * d : POOL * (d + 1), lanes],
+                sem_r.at[d, c, x],
+            )
+
+        r_copies = [r_copy(d, c, x) for d in range(n_pool // 2) for c in range(2) for x in range(2)]
+        for copy in r_copies:
+            copy.start()
+        at, to = iota((256, 256), 0), iota((256, 256), 1)
+        turn = ones_where(to == PH * (at & 15) + (at >> 4))
+        for h in range(2):
+            for p in range(PH):
+                xf[h, p, 0:8, :] = jnp.zeros((8, 128), F32)
+        for copy in r_copies:
+            copy.wait()
+        for b in range(total // 256):
+            turned = nt_dot(turn, r_raw[:, b * 256 : (b + 1) * 256]).astype(BF16)
+            placed = dot(turned, order_ref[...])
+            for p in range(PH):
+                for h in range(2):
+                    xf[h, p, 8 + 16 * b : 24 + 16 * b, :] = placed[
+                        16 * p : 16 * p + 16, 128 * h : 128 * h + 128
+                    ]
+
+        @pl.loop(0, 47)
+        def _(idx):
+            k = idx - 31
+            for b in range(windows):
+                half = (me >> 1) ^ (b // half_w)
+                row = 8 + PER * (half_w * half + b % half_w) + (k >> 4) - 2 * me
+                for h in range(2):
+                    xr[b, slab(idx), 128 * h : 128 * h + 128] = xf[h, k & 15, pl.ds(row, PER), :].astype(BF16)
+
+        for low, high, which in ((24, 35, (0, 1)), (20, 24, (1,)), (16, 20, ())):
+
+            @pl.loop(low, high)
+            def _(idx):
+                make(idx, rv0, 16, which)
+
+    def products(rv):
+        first = 15 - (step & 3)
+
+        def product(i):
+            v, off = COMBOS[i]
+            if v == 0:
+                rows = pl.ds(pl.multiple_of((first + 16 - 16 * (step >> 2)) * PER, PER), 4 * PER)
+                parts = [xr[b, rows, :] for b in range(windows)]
+            else:
+                rows = pl.ds(pl.multiple_of((first - off) * PER, PER), 4 * PER)
+                parts = [rv[v - 1, b, rows, :] for b in range(windows)]
+            return dot(jnp.concatenate([half[i] for half in halves], axis=1), jnp.concatenate(parts, axis=0))
+
+        p = [product(i) for i in range(9)]
+        w0, w1 = p[0] + p[3], p[0] + p[6]
+        for at, value in enumerate((w0 + (p[1] + p[4]), w0 + (p[2] + p[5]), w1 + (p[1] + p[7]), w1 + (p[2] + p[8]))):
+            out_ref[0, at, 0] = (scale * value).astype(BF16)
+
+    @pl.when(step < 4)
+    def _():
+        products(rv0)
+        for o in range(5):
+            make(jnp.maximum(18 - 5 * step - o, 0), rv1, 0, (0, 1))
+
+    @pl.when(step >= 4)
+    def _():
+        products(rv1)
+
+
+def flip(array, axis, by):
+    return lax.ppermute(array, axis, [(i, i ^ by) for i in range(lax.axis_size(axis))])
+
+
+def after(array, *others):
+    return lax.optimization_barrier((array, *others))[0]
+
+
+def block_shards(series, ref_list):
+    chan_rows, time_len = series.shape
+    groups, refs = ref_list.shape
+    n_tm = lax.axis_size("tm")
+    total = time_len * n_tm
+    lags_dev = LAGS // n_tm
+    group = lax.axis_index("chan").astype(jnp.int32)
+    me = lax.axis_index("tm").astype(jnp.int32)
+    smem = pl.BlockSpec(memory_space=pltpu.SMEM)
+    vmem = pl.BlockSpec(memory_space=pltpu.VMEM)
+    hbm = pl.BlockSpec(memory_space=pltpu.HBM)
+    anywhere = pl.BlockSpec(memory_space=pl.ANY)
+    own_pool, pair = pl.pallas_call(
+        select_kernel,
+        in_specs=[smem, vmem, hbm],
+        out_specs=[vmem, vmem],
+        out_shape=[jax.ShapeDtypeStruct((rows, time_len), BF16) for rows in (POOL, 2 * POOL)],
+        scratch_shapes=[
+            pltpu.VMEM((chan_rows, time_len), BF16),
+            pltpu.VMEM((groups * chan_rows // 128, 128), F32),
+            pltpu.SemaphoreType.DMA(()),
+        ],
+    )(group[None], ref_list, series)
+    pool_x = flip(own_pool, "tm", 2)
+    order = pl.pallas_call(
+        functools.partial(order_kernel, per=chan_rows // 128),
+        in_specs=[smem, vmem, hbm],
+        out_specs=vmem,
+        out_shape=jax.ShapeDtypeStruct((groups * POOL, refs), BF16),
+        cost_estimate=pl.CostEstimate(flops=10**9, bytes_accessed=10**6, transcendentals=0),
+    )(group[None], ref_list, own_pool)
+    pair = lax.dynamic_update_slice(after(pair, order), pool_x, (POOL, 0))
+    series_x = flip(after(series, pool_x), "tm", 2)
+    along_z = [pair] + [flip(pair, "chan", 2 * d) for d in range(1, groups // 2)]
+    pool = []
+    for piece in along_z:
+        pool += [piece, flip(piece, "chan", 1)]
+    series_c = flip(after(series, *along_z), "tm", 1)
+    series_xc = flip(after(series_x, *pool), "tm", 1)
+
+    def phases(mine, other):
+        return pl.pallas_call(
+            series_kernel,
+            in_specs=[smem, hbm, hbm],
+            out_specs=vmem,
+            out_shape=jax.ShapeDtypeStruct((9, chan_rows, time_len // 2), BF16),
+            scratch_shapes=[pltpu.VMEM((chan_rows, 2 * time_len), BF16), pltpu.SemaphoreType.DMA((2,))],
+            compiler_params=pltpu.CompilerParams(vmem_limit_bytes=16 * 2**20),
+            cost_estimate=pl.CostEstimate(
+                flops=4 * chan_rows * time_len * WIN, bytes_accessed=6 * 10**6, transcendentals=0
+            ),
+        )((me & 1)[None], mine, other)
+
+    halves = [phases(series, series_c), phases(series_x, series_xc)]
+    pieces = []
+    for piece in pool:
+        pieces += [piece, flip(piece, "tm", 1)]
+    n_pool = len(pieces)
+    windows = total // WIN
+    out = pl.pallas_call(
+        functools.partial(corr_kernel, time_len=time_len, n_pool=n_pool, scale=1.0 / math.sqrt(total)),
+        grid=(8,),
+        in_specs=[smem, pl.BlockSpec((groups * POOL, refs), lambda i: (0, 0))] + [vmem] * 2 + [hbm] * n_pool,
+        out_specs=pl.BlockSpec((1, 4, 1, chan_rows, refs), lambda i: (i // 4, 0, i % 4, 0, 0)),
+        out_shape=jax.ShapeDtypeStruct((2, 4, 4, chan_rows, refs), BF16),
+        scratch_shapes=[
+            pltpu.VMEM((groups * POOL, total), BF16),
+            pltpu.VMEM((2, PH, total // PH + 8, 128), F32),
+            pltpu.VMEM((windows, 47 * PER, refs), BF16),
+            pltpu.VMEM((3, windows, 19 * PER, refs), BF16),
+            pltpu.VMEM((3, windows, 19 * PER, refs), BF16),
+            pltpu.SemaphoreType.DMA((n_pool // 2, 2, 2)),
+        ],
+        compiler_params=pltpu.CompilerParams(vmem_limit_bytes=40 * 2**20),
+        cost_estimate=pl.CostEstimate(flops=15 * 10**9, bytes_accessed=2 * 10**7, transcendentals=0),
+    )(me[None], order, *halves, *pieces)
+    return out.reshape(lags_dev, chan_rows, refs)
+
+
 def solution(mesh):
     in_specs = (P("chan", "tm"), P())
     out_specs = P("tm", "chan", None)
-    return jax.shard_map(shards, mesh=mesh, in_specs=in_specs, out_specs=out_specs, check_vma=False)
+    sizes = (mesh.shape["chan"], mesh.shape["tm"])
+    body = block_shards if sizes == (8, 4) else general_shards
+    return jax.shard_map(body, mesh=mesh, in_specs=in_specs, out_specs=out_specs, check_vma=False)

time: 785 us -> 60.2 us (0.08)
  local copies, waits for them, and re-layouts: 326 us -> 0.09 us
  waiting for transfers between devices: 334 us -> 10.9 us
  matrix products: 95.2 us -> 0 us
  Pallas kernels: 0 us -> 31.8 us
  starting transfers between devices: 1.33 us -> 17 us
  between operations: 13.5 us -> 0.21 us
  loops' own time: 11.2 us -> 0 us
    gather x385 -> x0, local copies, waits for them, and re-layouts: 315 us -> none
    unnamed x3 -> x0, waiting for transfers between devices: 234 us -> none
    all_gather x1 -> x0, waiting for transfers between devices: 98.6 us -> none  [shards(): gathered_all = lax.all_gather(series, 'chan', axis=0, tiled=True)]
    dot_general x16 -> x0, matrix products: 95.2 us -> none  [lag_block(): jnp.einsum('jct,rt->jcr', windows, ref_block, preferred_element_type=jnp....]
    pallas_call x0 -> x5, Pallas kernels: none -> 31.8 us  [the longest x1 24 us: block_shards(): pl.pallas_call(functools.partial(corr_kernel, time_len=time_len, n_pool=n...]
    ppermute x1 -> x19, starting transfers between devices: 1.29 us -> 17 us  [flip(): lax.ppermute(array, axis, [(i, i ^ by) for i in range(lax.axis_size(axis))])]
    another operation x17 -> x0, loops' own time: 11.2 us -> none  [the longest x1 10.8 us: shards(): lax.scan(lag_step, None, jnp.arange(lax.axis_size('tm') * lags_dev // 8,...]
    ppermute x1 -> x19, waiting for transfers between devices: 1.2 us -> 10.9 us  [flip(): lax.ppermute(array, axis, [(i, i ^ by) for i in range(lax.axis_size(axis))])]
  transfers between devices with their start and end apart: 3 -> 19, of which waited for: 3 -> 6; matrix products, arithmetic and copies ran while one was open for 0% -> 0% of each run, Pallas kernels for 0% -> 8%
where the time goes in v2:
time: 60.2 us; the launch traced here: 60 us
  Pallas kernels  31.8 us (53%)
  starting transfers between devices  17 us (28%)
  waiting for transfers between devices  10.9 us (18%)
    pallas_call x1, Pallas kernels, block_shards(): pl.pallas_call(functools.partial(corr_kernel, time_len=time_len, n_pool=n...  24 us
    ppermute x19, starting transfers between devices, flip(): lax.ppermute(array, axis, [(i, i ^ by) for i in range(lax.axis_size(axis))])  17 us
    ppermute x19, waiting for transfers between devices, flip(): lax.ppermute(array, axis, [(i, i ^ by) for i in range(lax.axis_size(axis))])  10.9 us
    pallas_call x1, Pallas kernels, block_shards(): pl.pallas_call(select_kernel, in_specs=[smem, vmem, hbm], out_specs=[vmem...  2.9 us
    pallas_call x2, Pallas kernels, phases(): pl.pallas_call(series_kernel, in_specs=[smem, hbm, hbm], out_specs=vmem,...  2.79 us
    pallas_call x1, Pallas kernels, block_shards(): pl.pallas_call(functools.partial(order_kernel, per=chan_rows // 128), in_...  2.11 us
  transfers between devices with their start and end apart: 19, of which 6 were waited for; matrix products, arithmetic and copies ran while one was open for 0% of the time, Pallas kernels for 8%

profile of v2, /device:TPU:0, one launch (start us, length us, event | category | flops | bytes accessed | tf_op | source)
XLA Modules:
  0.0 60.0 jit_solution(3154391687404399246)
XLA Ops:
  0.0 0.0 copy-start
  0.0 2.9 %shard_map.28 = (bf16[32,768]{1,0:T(8,128)(2,1)}, bf16[64,768]{1,0:T(8,128)(2,1)}) custom-call(s32[1]{0:T(128)} %bitcast.1.group_ref, s32[8,256]{1,0:T(8,128)} %list_ref.3, bf16[512,768]{1,0:T(8,128)(2,1)} %mine_ref.1), custom_call_target="tpu_custom_call" | custom-call | tf_op jit(solution)/shard_map/pallas_call | solution.py:275
  2.9 0.0 copy-start.7
  2.9 3.0 %collective-permute-start = (bf16[32,768]{1,0:T(8,128)(2,1)}, bf16[32,768]{1,0:T(8,128)(2,1)S(1)}, u32[]{:S(2)}, u32[]{:S(2)}) collective-permute-start(bf16[32,768]{1,0:T(8,128)(2,1)} %get-tuple-element.11.pool_ref), channel_id=1, source_target_pairs={{0,2},{1,3},{2,0},{3,1},{4,6},{5,7},{6,4},{7,5},{8,10},{9,11},{10,... | collective-permute-start | bytes 147464 | tf_op jit(solution)/shard_map/ppermute | solution.py:256
  5.9 2.3 %collective-permute-done = bf16[32,768]{1,0:T(8,128)(2,1)S(1)} collective-permute-done((bf16[32,768]{1,0:T(8,128)(2,1)}, bf16[32,768]{1,0:T(8,128)(2,1)S(1)}, u32[]{:S(2)}, u32[]{:S(2)}) %collective-permute-start) | collective-permute-done | bytes 49184 | tf_op jit(solution)/shard_map/ppermute | solution.py:256
  8.2 2.0 %collective-permute-start.5 = (bf16[512,768]{1,0:T(8,128)(2,1)}, bf16[512,768]{1,0:T(8,128)(2,1)S(1)}, u32[]{:S(2)}, u32[]{:S(2)}) collective-permute-start(bf16[512,768]{1,0:T(8,128)(2,1)} %mine_ref.1), channel_id=1, source_target_pairs={{0,2},{1,3},{2,0},{3,1},{4,6},{5,7},{6,4},{7,5},{8,10},{9,11},{10,... | collective-permute-start | bytes 2359304 | tf_op jit(solution)/shard_map/ppermute | solution.py:256
  10.2 2.1 %shard_map.29.order_ref = bf16[256,256]{1,0:T(8,128)(2,1)} custom-call(s32[1]{0:T(128)} %bitcast.1.group_ref, s32[8,256]{1,0:T(8,128)} %list_ref.3, bf16[32,768]{1,0:T(8,128)(2,1)} %get-tuple-element.11.pool_ref), custom_call_target="tpu_custom_call" | custom-call | flops 1000000000 | bytes 1000000 | tf_op jit(solution)/shard_map/pallas_call | solution.py:287
  12.3 0.0 copy-done.7
  12.3 0.0 copy-start.8
  12.3 3.7 %collective-permute-start.3 = (bf16[64,768]{1,0:T(8,128)(2,1)S(1)}, bf16[64,768]{1,0:T(8,128)(2,1)S(1)}, u32[]{:S(2)}, u32[]{:S(2)}) collective-permute-start(bf16[64,768]{1,0:T(8,128)(2,1)S(1)} %constant_dynamic-update-slice_fusion.refs_2_), channel_id=1, source_target_pairs={{0,24},{4,28},{8,16},{12,20},{16,8},{20,12},{24,0},{28,4},{1,25},{... | collective-permute-start | bytes 294920 | tf_op jit(solution)/shard_map/ppermute | solution.py:256
  16.0 0.0 collective-permute-start.2
  16.0 0.8 %collective-permute-start.1 = (bf16[64,768]{1,0:T(8,128)(2,1)S(1)}, bf16[64,768]{1,0:T(8,128)(2,1)S(1)}, u32[]{:S(2)}, u32[]{:S(2)}) collective-permute-start(bf16[64,768]{1,0:T(8,128)(2,1)S(1)} %constant_dynamic-update-slice_fusion.refs_2_), channel_id=1, source_target_pairs={{0,8},{4,12},{8,0},{12,4},{16,24},{20,28},{24,16},{28,20},{1,9},{5... | collective-permute-start | bytes 294920 | tf_op jit(solution)/shard_map/ppermute | solution.py:256
  16.8 1.5 %collective-permute-start.6 = (bf16[64,768]{1,0:T(8,128)(2,1)S(1)}, bf16[64,768]{1,0:T(8,128)(2,1)S(1)}, u32[]{:S(2)}, u32[]{:S(2)}) collective-permute-start(bf16[64,768]{1,0:T(8,128)(2,1)S(1)} %constant_dynamic-update-slice_fusion.refs_2_), channel_id=1, source_target_pairs={{0,4},{4,0},{8,12},{12,8},{16,20},{20,16},{24,28},{28,24},{1,5},{5... | collective-permute-start | bytes 294920 | tf_op jit(solution)/shard_map/ppermute | solution.py:256
  18.3 0.5 collective-permute-done.3.refs_14_
  18.9 1.5 %collective-permute-start.9 = (bf16[64,768]{1,0:T(8,128)(2,1)S(1)}, bf16[64,768]{1,0:T(8,128)(2,1)S(1)}, u32[]{:S(2)}, u32[]{:S(2)}) collective-permute-start(bf16[64,768]{1,0:T(8,128)(2,1)S(1)} %collective-permute-done.3.refs_14_), channel_id=1, source_target_pairs={{0,4},{4,0},{8,12},{12,8},{16,20},{20,16},{24,28},{28,24},{1,5},{5... | collective-permute-start | bytes 294920 | tf_op jit(solution)/shard_map/ppermute | solution.py:256
  20.4 2.5 %collective-permute-done.2.refs_10_ = bf16[64,768]{1,0:T(8,128)(2,1)S(1)} collective-permute-done((bf16[64,768]{1,0:T(8,128)(2,1)S(1)}, bf16[64,768]{1,0:T(8,128)(2,1)S(1)}, u32[]{:S(2)}, u32[]{:S(2)}) %collective-permute-start.2) | collective-permute-done | bytes 98336 | tf_op jit(solution)/shard_map/ppermute | solution.py:256
  22.9 1.5 %collective-permute-start.8 = (bf16[64,768]{1,0:T(8,128)(2,1)S(1)}, bf16[64,768]{1,0:T(8,128)(2,1)S(1)}, u32[]{:S(2)}, u32[]{:S(2)}) collective-permute-start(bf16[64,768]{1,0:T(8,128)(2,1)S(1)} %collective-permute-done.2.refs_10_), channel_id=1, source_target_pairs={{0,4},{4,0},{8,12},{12,8},{16,20},{20,16},{24,28},{28,24},{1,5},{5... | collective-permute-start | bytes 294920 | tf_op jit(solution)/shard_map/ppermute | solution.py:256
  24.5 0.0 collective-permute-done.1.refs_6_
  24.5 0.5 collective-permute-start.7
  25.0 0.0 copy-done.8
  25.0 0.0 collective-permute-done.6.refs_4_
  25.0 0.0 copy-done
  25.0 0.1 collective-permute-start.4
  25.1 0.0 collective-permute-done.9.refs_16_
  25.1 0.0 copy-start.1
  25.1 2.9 %collective-permute-done.8.refs_12_ = bf16[64,768]{1,0:T(8,128)(2,1)S(1)} collective-permute-done((bf16[64,768]{1,0:T(8,128)(2,1)S(1)}, bf16[64,768]{1,0:T(8,128)(2,1)S(1)}, u32[]{:S(2)}, u32[]{:S(2)}) %collective-permute-start.8) | collective-permute-done | bytes 98336 | tf_op jit(solution)/shard_map/ppermute | solution.py:256
  28.0 0.0 copy-start.3
  28.0 1.1 %collective-permute-done.7.refs_8_ = bf16[64,768]{1,0:T(8,128)(2,1)S(1)} collective-permute-done((bf16[64,768]{1,0:T(8,128)(2,1)S(1)}, bf16[64,768]{1,0:T(8,128)(2,1)S(1)}, u32[]{:S(2)}, u32[]{:S(2)}) %collective-permute-start.7) | collective-permute-done | bytes 98336 | tf_op jit(solution)/shard_map/ppermute | solution.py:256
  29.1 0.0 collective-permute-done.5.mine_ref
  29.1 0.0 collective-permute-start.10
  29.1 0.5 collective-permute-start.11
  29.6 0.0 copy-done.1
  29.6 0.1 collective-permute-start.12
  29.7 0.0 copy-done.3
  29.7 0.0 copy-done.5
  29.7 0.4 collective-permute-start.17
  30.1 1.5 %collective-permute-done.11.refs_3_ = bf16[64,768]{1,0:T(8,128)(2,1)} collective-permute-done((bf16[64,768]{1,0:T(8,128)(2,1)}, bf16[64,768]{1,0:T(8,128)(2,1)}, u32[]{:S(2)}, u32[]{:S(2)}) %collective-permute-start.11) | collective-permute-done | bytes 98336 | tf_op jit(solution)/shard_map/ppermute | solution.py:256
  31.6 0.4 collective-permute-start.15
  32.0 0.0 collective-permute-done.12.refs_5_
  32.0 0.1 collective-permute-start.13
  32.1 0.0 collective-permute-done.17.refs_15_
  32.1 0.4 collective-permute-start.18
  32.5 0.0 collective-permute-done.4.other_ref
  32.5 0.1 collective-permute-start.16
  32.7 0.0 collective-permute-done.10.other_ref
  32.7 0.4 collective-permute-start.14
  33.0 1.4 %shard_map.30.refs_0_ = bf16[9,512,384]{2,1,0:T(8,128)(2,1)S(1)} custom-call(s32[1]{0:T(128)} %bitcast.2.core_ref, bf16[512,768]{1,0:T(8,128)(2,1)S(1)} %copy-done, bf16[512,768]{1,0:T(8,128)(2,1)S(1)} %collective-permute-done.4.other_ref), custom_call_target="tpu_custom_call" | custom-call | flops 805306368 | bytes 6000000 | tf_op jit(solution)/shard_map/pallas_call | solution.py:304
  34.4 0.0 copy-start.2
  34.4 0.0 copy-start.4
  34.5 0.0 copy-start.6
  34.5 0.0 copy-start.9
  34.5 0.0 copy-start.10
  34.5 1.4 %shard_map.31.refs_1_ = bf16[9,512,384]{2,1,0:T(8,128)(2,1)S(1)} custom-call(s32[1]{0:T(128)} %bitcast.2.core_ref, bf16[512,768]{1,0:T(8,128)(2,1)S(1)} %collective-permute-done.5.mine_ref, bf16[512,768]{1,0:T(8,128)(2,1)S(1)} %collective-permute-done.10.other_ref), custom_call_target="tpu_custom_call" | custom-call | flops 805306368 | bytes 6000000 | tf_op jit(solution)/shard_map/pallas_call | solution.py:304
  35.9 0.0 collective-permute-done.15.refs_11_
  35.9 0.0 collective-permute-done.13.refs_7_
  35.9 0.0 collective-permute-done.18.refs_17_
  35.9 0.0 collective-permute-done.16.refs_13_
  35.9 0.0 collective-permute-done.14.refs_9_
  35.9 0.0 copy-done.2
  36.0 0.0 copy-done.4
  36.0 0.0 copy-done.6
  36.0 0.0 copy-done.9
  36.0 0.0 copy-done.10
  36.0 24.0 %shard_map.32 = bf16[2,4,4,512,256]{4,3,2,1,0:T(8,128)(2,1)} custom-call(s32[1]{0:T(128)} %bitcast.tm_ref, bf16[256,256]{1,0:T(8,128)(2,1)S(1)} %copy-done.10, bf16[9,512,384]{2,1,0:T(8,128)(2,1)S(1)} %shard_map.30.refs_0_, bf16[9,512,384]{2,1,0:T(8,128)(2,1)S(1)} %shard_map.31.refs_1_, bf16[64,768]{1,0:T(8,128)(2,1)S(1)} %copy-done.9, ...), custom_call_target="tpu_custom_call" | custom-call | flops 15000000512 | bytes 20000000 | tf_op jit(solution)/shard_map/pallas_call | solution.py:322
  (2 shorter events, 0.0 us)
Async XLA Ops:
  0.0 25.0 %copy-start = (bf16[512,768]{1,0:T(8,128)(2,1)S(1)}, bf16[512,768]{1,0:T(8,128)(2,1)}, u32[]{:S(2)}) copy-start(bf16[512,768]{1,0:T(8,128)(2,1)} %mine_ref.1) | copy-start | bytes 2359300
  2.9 9.4 %copy-start.7 = (bf16[64,768]{1,0:T(8,128)(2,1)S(1)}, bf16[64,768]{1,0:T(8,128)(2,1)}, u32[]{:S(2)}) copy-start(bf16[64,768]{1,0:T(8,128)(2,1)} %get-tuple-element.13) | copy-start | bytes 294916
  2.9 5.3 %collective-permute-start = (bf16[32,768]{1,0:T(8,128)(2,1)}, bf16[32,768]{1,0:T(8,128)(2,1)S(1)}, u32[]{:S(2)}, u32[]{:S(2)}) collective-permute-start(bf16[32,768]{1,0:T(8,128)(2,1)} %get-tuple-element.11.pool_ref), channel_id=1, source_target_pairs={{0,2},{1,3},{2,0},{3,1},{4,6},{5,7},{6,4},{7,5},{8,10},{9,11},{10,... | collective-permute-start | bytes 147464 | tf_op jit(solution)/shard_map/ppermute | solution.py:256
  8.2 20.9 %collective-permute-start.5 = (bf16[512,768]{1,0:T(8,128)(2,1)}, bf16[512,768]{1,0:T(8,128)(2,1)S(1)}, u32[]{:S(2)}, u32[]{:S(2)}) collective-permute-start(bf16[512,768]{1,0:T(8,128)(2,1)} %mine_ref.1), channel_id=1, source_target_pairs={{0,2},{1,3},{2,0},{3,1},{4,6},{5,7},{6,4},{7,5},{8,10},{9,11},{10,... | collective-permute-start | bytes 2359304 | tf_op jit(solution)/shard_map/ppermute | solution.py:256
  12.3 12.6 %copy-start.8 = (bf16[64,768]{1,0:T(8,128)(2,1)}, bf16[64,768]{1,0:T(8,128)(2,1)S(1)}, u32[]{:S(2)}) copy-start(bf16[64,768]{1,0:T(8,128)(2,1)S(1)} %constant_dynamic-update-slice_fusion.refs_2_) | copy-start | bytes 294916
  12.3 6.5 %collective-permute-start.3 = (bf16[64,768]{1,0:T(8,128)(2,1)S(1)}, bf16[64,768]{1,0:T(8,128)(2,1)S(1)}, u32[]{:S(2)}, u32[]{:S(2)}) collective-permute-start(bf16[64,768]{1,0:T(8,128)(2,1)S(1)} %constant_dynamic-update-slice_fusion.refs_2_), channel_id=1, source_target_pairs={{0,24},{4,28},{8,16},{12,20},{16,8},{20,12},{24,0},{28,4},{1,25},{... | collective-permute-start | bytes 294920 | tf_op jit(solution)/shard_map/ppermute | solution.py:256
  16.0 6.9 %collective-permute-start.2 = (bf16[64,768]{1,0:T(8,128)(2,1)S(1)}, bf16[64,768]{1,0:T(8,128)(2,1)S(1)}, u32[]{:S(2)}, u32[]{:S(2)}) collective-permute-start(bf16[64,768]{1,0:T(8,128)(2,1)S(1)} %constant_dynamic-update-slice_fusion.refs_2_), channel_id=1, source_target_pairs={{0,16},{4,20},{8,24},{12,28},{16,0},{20,4},{24,8},{28,12},{1,17},{... | collective-permute-start | bytes 294920 | tf_op jit(solution)/shard_map/ppermute | solution.py:256
  16.0 8.4 %collective-permute-start.1 = (bf16[64,768]{1,0:T(8,128)(2,1)S(1)}, bf16[64,768]{1,0:T(8,128)(2,1)S(1)}, u32[]{:S(2)}, u32[]{:S(2)}) collective-permute-start(bf16[64,768]{1,0:T(8,128)(2,1)S(1)} %constant_dynamic-update-slice_fusion.refs_2_), channel_id=1, source_target_pairs={{0,8},{4,12},{8,0},{12,4},{16,24},{20,28},{24,16},{28,20},{1,9},{5... | collective-permute-start | bytes 294920 | tf_op jit(solution)/shard_map/ppermute | solution.py:256
  16.8 8.2 %collective-permute-start.6 = (bf16[64,768]{1,0:T(8,128)(2,1)S(1)}, bf16[64,768]{1,0:T(8,128)(2,1)S(1)}, u32[]{:S(2)}, u32[]{:S(2)}) collective-permute-start(bf16[64,768]{1,0:T(8,128)(2,1)S(1)} %constant_dynamic-update-slice_fusion.refs_2_), channel_id=1, source_target_pairs={{0,4},{4,0},{8,12},{12,8},{16,20},{20,16},{24,28},{28,24},{1,5},{5... | collective-permute-start | bytes 294920 | tf_op jit(solution)/shard_map/ppermute | solution.py:256
  18.9 6.2 %collective-permute-start.9 = (bf16[64,768]{1,0:T(8,128)(2,1)S(1)}, bf16[64,768]{1,0:T(8,128)(2,1)S(1)}, u32[]{:S(2)}, u32[]{:S(2)}) collective-permute-start(bf16[64,768]{1,0:T(8,128)(2,1)S(1)} %collective-permute-done.3.refs_14_), channel_id=1, source_target_pairs={{0,4},{4,0},{8,12},{12,8},{16,20},{20,16},{24,28},{28,24},{1,5},{5... | collective-permute-start | bytes 294920 | tf_op jit(solution)/shard_map/ppermute | solution.py:256
  22.9 5.1 %collective-permute-start.8 = (bf16[64,768]{1,0:T(8,128)(2,1)S(1)}, bf16[64,768]{1,0:T(8,128)(2,1)S(1)}, u32[]{:S(2)}, u32[]{:S(2)}) collective-permute-start(bf16[64,768]{1,0:T(8,128)(2,1)S(1)} %collective-permute-done.2.refs_10_), channel_id=1, source_target_pairs={{0,4},{4,0},{8,12},{12,8},{16,20},{20,16},{24,28},{28,24},{1,5},{5... | collective-permute-start | bytes 294920 | tf_op jit(solution)/shard_map/ppermute | solution.py:256
  24.5 4.6 %collective-permute-start.7 = (bf16[64,768]{1,0:T(8,128)(2,1)S(1)}, bf16[64,768]{1,0:T(8,128)(2,1)S(1)}, u32[]{:S(2)}, u32[]{:S(2)}) collective-permute-start(bf16[64,768]{1,0:T(8,128)(2,1)S(1)} %collective-permute-done.1.refs_6_), channel_id=1, source_target_pairs={{0,4},{4,0},{8,12},{12,8},{16,20},{20,16},{24,28},{28,24},{1,5},{5... | collective-permute-start | bytes 294920 | tf_op jit(solution)/shard_map/ppermute | solution.py:256
  25.0 7.5 %collective-permute-start.4 = (bf16[512,768]{1,0:T(8,128)(2,1)S(1)}, bf16[512,768]{1,0:T(8,128)(2,1)S(1)}, u32[]{:S(2)}, u32[]{:S(2)}) collective-permute-start(bf16[512,768]{1,0:T(8,128)(2,1)S(1)} %copy-done), channel_id=1, source_target_pairs={{0,1},{1,0},{2,3},{3,2},{4,5},{5,4},{6,7},{7,6},{8,9},{9,8},{10,11... | collective-permute-start | bytes 2359304 | tf_op jit(solution)/shard_map/ppermute | solution.py:256
  25.1 4.5 %copy-start.1 = (bf16[64,768]{1,0:T(8,128)(2,1)}, bf16[64,768]{1,0:T(8,128)(2,1)S(1)}, u32[]{:S(2)}) copy-start(bf16[64,768]{1,0:T(8,128)(2,1)S(1)} %collective-permute-done.9.refs_16_) | copy-start | bytes 294916
  28.0 1.7 %copy-start.3 = (bf16[64,768]{1,0:T(8,128)(2,1)}, bf16[64,768]{1,0:T(8,128)(2,1)S(1)}, u32[]{:S(2)}) copy-start(bf16[64,768]{1,0:T(8,128)(2,1)S(1)} %collective-permute-done.8.refs_12_) | copy-start | bytes 294916
  29.1 0.6 %copy-start.5 = (bf16[64,768]{1,0:T(8,128)(2,1)}, bf16[64,768]{1,0:T(8,128)(2,1)S(1)}, u32[]{:S(2)}) copy-start(bf16[64,768]{1,0:T(8,128)(2,1)S(1)} %collective-permute-done.7.refs_8_) | copy-start | bytes 294916
  29.1 3.6 %collective-permute-start.10 = (bf16[512,768]{1,0:T(8,128)(2,1)S(1)}, bf16[512,768]{1,0:T(8,128)(2,1)S(1)}, u32[]{:S(2)}, u32[]{:S(2)}) collective-permute-start(bf16[512,768]{1,0:T(8,128)(2,1)S(1)} %collective-permute-done.5.mine_ref), channel_id=1, source_target_pairs={{0,1},{1,0},{2,3},{3,2},{4,5},{5,4},{6,7},{7,6},{8,9},{9,8},{10,11... | collective-permute-start | bytes 2359304 | tf_op jit(solution)/shard_map/ppermute | solution.py:256
  29.1 2.5 %collective-permute-start.11 = (bf16[64,768]{1,0:T(8,128)(2,1)}, bf16[64,768]{1,0:T(8,128)(2,1)}, u32[]{:S(2)}, u32[]{:S(2)}) collective-permute-start(bf16[64,768]{1,0:T(8,128)(2,1)} %copy-done.8), channel_id=1, source_target_pairs={{0,1},{1,0},{2,3},{3,2},{4,5},{5,4},{6,7},{7,6},{8,9},{9,8},{10,11... | collective-permute-start | bytes 294920 | tf_op jit(solution)/shard_map/ppermute | solution.py:256
  29.6 2.4 %collective-permute-start.12 = (bf16[64,768]{1,0:T(8,128)(2,1)S(1)}, bf16[64,768]{1,0:T(8,128)(2,1)}, u32[]{:S(2)}, u32[]{:S(2)}) collective-permute-start(bf16[64,768]{1,0:T(8,128)(2,1)S(1)} %collective-permute-done.6.refs_4_), channel_id=1, source_target_pairs={{0,1},{1,0},{2,3},{3,2},{4,5},{5,4},{6,7},{7,6},{8,9},{9,8},{10,11... | collective-permute-start | bytes 294920 | tf_op jit(solution)/shard_map/ppermute | solution.py:256
  29.7 2.4 %collective-permute-start.17 = (bf16[64,768]{1,0:T(8,128)(2,1)S(1)}, bf16[64,768]{1,0:T(8,128)(2,1)}, u32[]{:S(2)}, u32[]{:S(2)}) collective-permute-start(bf16[64,768]{1,0:T(8,128)(2,1)S(1)} %collective-permute-done.3.refs_14_), channel_id=1, source_target_pairs={{0,1},{1,0},{2,3},{3,2},{4,5},{5,4},{6,7},{7,6},{8,9},{9,8},{10,11... | collective-permute-start | bytes 294920 | tf_op jit(solution)/shard_map/ppermute | solution.py:256
  31.6 4.3 %collective-permute-start.15 = (bf16[64,768]{1,0:T(8,128)(2,1)S(1)}, bf16[64,768]{1,0:T(8,128)(2,1)S(1)}, u32[]{:S(2)}, u32[]{:S(2)}) collective-permute-start(bf16[64,768]{1,0:T(8,128)(2,1)S(1)} %collective-permute-done.2.refs_10_), channel_id=1, source_target_pairs={{0,1},{1,0},{2,3},{3,2},{4,5},{5,4},{6,7},{7,6},{8,9},{9,8},{10,11... | collective-permute-start | bytes 294920 | tf_op jit(solution)/shard_map/ppermute | solution.py:256
  32.0 3.9 %collective-permute-start.13 = (bf16[64,768]{1,0:T(8,128)(2,1)S(1)}, bf16[64,768]{1,0:T(8,128)(2,1)S(1)}, u32[]{:S(2)}, u32[]{:S(2)}) collective-permute-start(bf16[64,768]{1,0:T(8,128)(2,1)S(1)} %collective-permute-done.1.refs_6_), channel_id=1, source_target_pairs={{0,1},{1,0},{2,3},{3,2},{4,5},{5,4},{6,7},{7,6},{8,9},{9,8},{10,11... | collective-permute-start | bytes 294920 | tf_op jit(solution)/shard_map/ppermute | solution.py:256
  32.1 3.8 %collective-permute-start.18 = (bf16[64,768]{1,0:T(8,128)(2,1)}, bf16[64,768]{1,0:T(8,128)(2,1)S(1)}, u32[]{:S(2)}, u32[]{:S(2)}) collective-permute-start(bf16[64,768]{1,0:T(8,128)(2,1)} %copy-done.1), channel_id=1, source_target_pairs={{0,1},{1,0},{2,3},{3,2},{4,5},{5,4},{6,7},{7,6},{8,9},{9,8},{10,11... | collective-permute-start | bytes 294920 | tf_op jit(solution)/shard_map/ppermute | solution.py:256
  32.5 3.4 %collective-permute-start.16 = (bf16[64,768]{1,0:T(8,128)(2,1)}, bf16[64,768]{1,0:T(8,128)(2,1)S(1)}, u32[]{:S(2)}, u32[]{:S(2)}) collective-permute-start(bf16[64,768]{1,0:T(8,128)(2,1)} %copy-done.3), channel_id=1, source_target_pairs={{0,1},{1,0},{2,3},{3,2},{4,5},{5,4},{6,7},{7,6},{8,9},{9,8},{10,11... | collective-permute-start | bytes 294920 | tf_op jit(solution)/shard_map/ppermute | solution.py:256
  32.7 3.3 %collective-permute-start.14 = (bf16[64,768]{1,0:T(8,128)(2,1)}, bf16[64,768]{1,0:T(8,128)(2,1)S(1)}, u32[]{:S(2)}, u32[]{:S(2)}) collective-permute-start(bf16[64,768]{1,0:T(8,128)(2,1)} %copy-done.5), channel_id=1, source_target_pairs={{0,1},{1,0},{2,3},{3,2},{4,5},{5,4},{6,7},{7,6},{8,9},{9,8},{10,11... | collective-permute-start | bytes 294920 | tf_op jit(solution)/shard_map/ppermute | solution.py:256
  34.4 1.5 %copy-start.2 = (bf16[64,768]{1,0:T(8,128)(2,1)S(1)}, bf16[64,768]{1,0:T(8,128)(2,1)}, u32[]{:S(2)}) copy-start(bf16[64,768]{1,0:T(8,128)(2,1)} %copy-done.1) | copy-start | bytes 294916
  34.4 1.5 %copy-start.4 = (bf16[64,768]{1,0:T(8,128)(2,1)S(1)}, bf16[64,768]{1,0:T(8,128)(2,1)}, u32[]{:S(2)}) copy-start(bf16[64,768]{1,0:T(8,128)(2,1)} %copy-done.3) | copy-start | bytes 294916
  34.5 1.5 %copy-start.6 = (bf16[64,768]{1,0:T(8,128)(2,1)S(1)}, bf16[64,768]{1,0:T(8,128)(2,1)}, u32[]{:S(2)}) copy-start(bf16[64,768]{1,0:T(8,128)(2,1)} %copy-done.5) | copy-start | bytes 294916
  34.5 1.5 %copy-start.9 = (bf16[64,768]{1,0:T(8,128)(2,1)S(1)}, bf16[64,768]{1,0:T(8,128)(2,1)}, u32[]{:S(2)}) copy-start(bf16[64,768]{1,0:T(8,128)(2,1)} %copy-done.8) | copy-start | bytes 294916
  34.5 1.5 %copy-start.10 = (bf16[256,256]{1,0:T(8,128)(2,1)S(1)}, bf16[256,256]{1,0:T(8,128)(2,1)}, u32[]{:S(2)}) copy-start(bf16[256,256]{1,0:T(8,128)(2,1)} %shard_map.29.order_ref) | copy-start | bytes 393220

commit v3 on v2

--- a/solution.py
+++ b/solution.py
@@ -156,57 +156,53 @@
             out_ref[i, :, b * QUARTER : (b + 1) * QUARTER] = value.astype(BF16)
 
 
-def corr_kernel(tm_ref, order_ref, *refs, n_pool, time_len, scale):
+def refs_kernel(order_ref, *refs):
+    *pieces, out_ref = refs
+    time_len = pieces[0].shape[1]
+    at, to = iota((256, 256), 0), iota((256, 256), 1)
+    turn = ones_where(to == PH * (at & 15) + (at >> 4))
+    blocks = [(x, b) for x in range(2) for b in range(time_len // 256)]
+    turned = []
+    for x, b in blocks:
+        block = [piece[POOL * x : POOL * (x + 1), 256 * b : 256 * (b + 1)] for piece in pieces]
+        turned.append(nt_dot(turn, jnp.concatenate(block, axis=0)).astype(BF16))
+    placed = dot(jnp.concatenate(turned, axis=0), order_ref[...]).astype(BF16)
+    for i, (x, b) in enumerate(blocks):
+        for p in range(PH):
+            out_ref[x, p, 16 * b : 16 * (b + 1), :] = placed[256 * i + 16 * p : 256 * i + 16 * (p + 1)]
+
+
+def corr_kernel(tm_ref, mine_ref, other_ref, *refs, windows, scale):
     halves = refs[:2]
-    pieces = refs[2 : 2 + n_pool]
-    out_ref, r_raw, xf, xr, rv0, rv1, sem_r = refs[2 + n_pool :]
+    out_ref, xf, xr, rv0, rv1 = refs[2:]
     me = tm_ref[0]
-    total = r_raw.shape[1]
-    windows = total // WIN
     half_w = windows // 2
     step = pl.program_id(0)
 
     def slab(idx):
         return pl.ds(pl.multiple_of(idx * PER, PER), PER)
 
-    def make(idx, rv, base, which):
-        for b in range(windows):
-            x0, x4, x8, x12 = (xr[b, slab(idx + o), :].astype(F32) for o in (0, 4, 8, 12))
+    def make(idx, rv, base, which, windows_of):
+        for b in windows_of:
+            x0, x4, x8, x12 = (xr[b, slab(idx + o), :] for o in (0, 4, 8, 12))
             f0 = x4 - x0
             if 0 in which:
-                rv[0, b, slab(idx - base), :] = f0.astype(BF16)
+                rv[0, b, slab(idx - base), :] = f0
             if 1 in which:
-                rv[1, b, slab(idx - base), :] = (x8 - x0).astype(BF16)
-            rv[2, b, slab(idx - base), :] = ((x12 - x8) - f0).astype(BF16)
+                rv[1, b, slab(idx - base), :] = x8 - x0
+            rv[2, b, slab(idx - base), :] = (x12 - x8) - f0
 
     @pl.when(step == 0)
     def _():
-        def r_copy(d, c, x):
-            lanes = pl.ds(pl.multiple_of((me ^ (c + 2 * x)) * time_len, 128), time_len)
-            return pltpu.make_async_copy(
-                pieces[2 * d + c].at[POOL * x : POOL * (x + 1)],
-                r_raw.at[POOL * d : POOL * (d + 1), lanes],
-                sem_r.at[d, c, x],
-            )
-
-        r_copies = [r_copy(d, c, x) for d in range(n_pool // 2) for c in range(2) for x in range(2)]
-        for copy in r_copies:
-            copy.start()
-        at, to = iota((256, 256), 0), iota((256, 256), 1)
-        turn = ones_where(to == PH * (at & 15) + (at >> 4))
+        block_rows = mine_ref.shape[2]
         for h in range(2):
+            lanes = slice(128 * h, 128 * h + 128)
             for p in range(PH):
                 xf[h, p, 0:8, :] = jnp.zeros((8, 128), F32)
-        for copy in r_copies:
-            copy.wait()
-        for b in range(total // 256):
-            turned = nt_dot(turn, r_raw[:, b * 256 : (b + 1) * 256]).astype(BF16)
-            placed = dot(turned, order_ref[...])
-            for p in range(PH):
-                for h in range(2):
-                    xf[h, p, 8 + 16 * b : 24 + 16 * b, :] = placed[
-                        16 * p : 16 * p + 16, 128 * h : 128 * h + 128
-                    ]
+                for c, ref in enumerate((mine_ref, other_ref)):
+                    for x in range(2):
+                        row = pl.multiple_of(8 + block_rows * (me ^ (c + 2 * x)), 8)
+                        xf[h, p, pl.ds(row, block_rows), :] = ref[x, p, :, lanes].astype(F32)
 
         @pl.loop(0, 47)
         def _(idx):
@@ -221,9 +217,9 @@
 
             @pl.loop(low, high)
             def _(idx):
-                make(idx, rv0, 16, which)
-
-    def products(rv):
+                make(idx, rv0, 16, which, range(windows))
+
+    def products(rv, beside):
         first = 15 - (step & 3)
 
         def product(i):
@@ -234,6 +230,7 @@
             else:
                 rows = pl.ds(pl.multiple_of((first - off) * PER, PER), 4 * PER)
                 parts = [rv[v - 1, b, rows, :] for b in range(windows)]
+            beside(i)
             return dot(jnp.concatenate([half[i] for half in halves], axis=1), jnp.concatenate(parts, axis=0))
 
         p = [product(i) for i in range(9)]
@@ -243,13 +240,15 @@
 
     @pl.when(step < 4)
     def _():
-        products(rv0)
-        for o in range(5):
-            make(jnp.maximum(18 - 5 * step - o, 0), rv1, 0, (0, 1))
+        def beside(i):
+            for n in range(i, 5 * windows, 9):
+                make(jnp.maximum(18 - 5 * step - n // windows, 0), rv1, 0, (0, 1), (n % windows,))
+
+        products(rv0, beside)
 
     @pl.when(step >= 4)
     def _():
-        products(rv1)
+        products(rv1, lambda i: None)
 
 
 def flip(array, axis, by):
@@ -292,13 +291,12 @@
         cost_estimate=pl.CostEstimate(flops=10**9, bytes_accessed=10**6, transcendentals=0),
     )(group[None], ref_list, own_pool)
     pair = lax.dynamic_update_slice(after(pair, order), pool_x, (POOL, 0))
-    series_x = flip(after(series, pool_x), "tm", 2)
+    series_x = flip(after(series, pool_x, order), "tm", 2)
     along_z = [pair] + [flip(pair, "chan", 2 * d) for d in range(1, groups // 2)]
     pool = []
     for piece in along_z:
         pool += [piece, flip(piece, "chan", 1)]
-    series_c = flip(after(series, *along_z), "tm", 1)
-    series_xc = flip(after(series_x, *pool), "tm", 1)
+    series_c = flip(after(series, *pool), "tm", 1)
 
     def phases(mine, other):
         return pl.pallas_call(
@@ -309,33 +307,37 @@
             scratch_shapes=[pltpu.VMEM((chan_rows, 2 * time_len), BF16), pltpu.SemaphoreType.DMA((2,))],
             compiler_params=pltpu.CompilerParams(vmem_limit_bytes=16 * 2**20),
             cost_estimate=pl.CostEstimate(
-                flops=4 * chan_rows * time_len * WIN, bytes_accessed=6 * 10**6, transcendentals=0
+                flops=1000, bytes_accessed=1000, transcendentals=0
             ),
         )((me & 1)[None], mine, other)
 
-    halves = [phases(series, series_c), phases(series_x, series_xc)]
-    pieces = []
-    for piece in pool:
-        pieces += [piece, flip(piece, "tm", 1)]
-    n_pool = len(pieces)
+    first_half = phases(series, series_c)
+    series_xc = flip(after(series_x, *pool), "tm", 1)
+    halves = [first_half, phases(series_x, series_xc)]
+    placed = pl.pallas_call(
+        refs_kernel,
+        in_specs=[vmem] * (1 + len(pool)),
+        out_specs=vmem,
+        out_shape=jax.ShapeDtypeStruct((2, PH, time_len // PH, refs), BF16),
+        cost_estimate=pl.CostEstimate(flops=8 * 10**8, bytes_accessed=10**6, transcendentals=0),
+    )(order, *pool)
+    placed_c = flip(placed, "tm", 1)
     windows = total // WIN
     out = pl.pallas_call(
-        functools.partial(corr_kernel, time_len=time_len, n_pool=n_pool, scale=1.0 / math.sqrt(total)),
+        functools.partial(corr_kernel, windows=windows, scale=1.0 / math.sqrt(total)),
         grid=(8,),
-        in_specs=[smem, pl.BlockSpec((groups * POOL, refs), lambda i: (0, 0))] + [vmem] * 2 + [hbm] * n_pool,
+        in_specs=[smem] + [vmem] * 4,
         out_specs=pl.BlockSpec((1, 4, 1, chan_rows, refs), lambda i: (i // 4, 0, i % 4, 0, 0)),
         out_shape=jax.ShapeDtypeStruct((2, 4, 4, chan_rows, refs), BF16),
         scratch_shapes=[
-            pltpu.VMEM((groups * POOL, total), BF16),
             pltpu.VMEM((2, PH, total // PH + 8, 128), F32),
             pltpu.VMEM((windows, 47 * PER, refs), BF16),
             pltpu.VMEM((3, windows, 19 * PER, refs), BF16),
             pltpu.VMEM((3, windows, 19 * PER, refs), BF16),
-            pltpu.SemaphoreType.DMA((n_pool // 2, 2, 2)),
         ],
         compiler_params=pltpu.CompilerParams(vmem_limit_bytes=40 * 2**20),
         cost_estimate=pl.CostEstimate(flops=15 * 10**9, bytes_accessed=2 * 10**7, transcendentals=0),
-    )(me[None], order, *halves, *pieces)
+    )(me[None], placed, placed_c, *halves)
     return out.reshape(lags_dev, chan_rows, refs)
 
 

time: 60.2 us -> 54.7 us (0.909)
  waiting for transfers between devices: 10.9 us -> 7.41 us
  starting transfers between devices: 17 us -> 15.1 us
    ppermute x19 -> x12, waiting for transfers between devices: 10.9 us -> 7.41 us  [flip(): lax.ppermute(array, axis, [(i, i ^ by) for i in range(lax.axis_size(axis))])]
    ppermute x19 -> x12, starting transfers between devices: 17 us -> 15.1 us  [flip(): lax.ppermute(array, axis, [(i, i ^ by) for i in range(lax.axis_size(axis))])]
    pallas_call x1 -> x2, Pallas kernels: 24 us -> 23.4 us  [the longest x1 20.7 us: block_shards(): pl.pallas_call(functools.partial(corr_kernel, windows=windows, scale=1.0...]
  transfers between devices with their start and end apart: 19 -> 12, of which waited for: 6 -> 6; matrix products, arithmetic and copies ran while one was open for 0% -> 0% of each run, Pallas kernels for 8% -> 14%
where the time goes in v3:
time: 54.7 us; the launch traced here: 54.4 us
  Pallas kernels  31.2 us (57%)
  starting transfers between devices  15.1 us (28%)
  waiting for transfers between devices  7.41 us (14%)
  local copies, waits for them, and re-layouts  0.62 us (1%)
    pallas_call x1, Pallas kernels, block_shards(): pl.pallas_call(functools.partial(corr_kernel, windows=windows, scale=1.0...  20.7 us
    ppermute x12, starting transfers between devices, flip(): lax.ppermute(array, axis, [(i, i ^ by) for i in range(lax.axis_size(axis))])  15.1 us
    ppermute x12, waiting for transfers between devices, flip(): lax.ppermute(array, axis, [(i, i ^ by) for i in range(lax.axis_size(axis))])  7.41 us
    pallas_call x1, Pallas kernels, block_shards(): pl.pallas_call(select_kernel, in_specs=[smem, vmem, hbm], out_specs=[vmem...  2.89 us
    pallas_call x2, Pallas kernels, phases(): pl.pallas_call(series_kernel, in_specs=[smem, hbm, hbm], out_specs=vmem,...  2.8 us
    pallas_call x1, Pallas kernels, block_shards(): pl.pallas_call(refs_kernel, in_specs=[vmem] * (1 + len(pool)), out_specs=...  2.73 us
    pallas_call x1, Pallas kernels, block_shards(): pl.pallas_call(functools.partial(order_kernel, per=chan_rows // 128), in_...  2.1 us
  transfers between devices with their start and end apart: 12, of which 6 were waited for; matrix products, arithmetic and copies ran while one was open for 0% of the time, Pallas kernels for 14%

profile of v3, /device:TPU:0, one launch (start us, length us, event | category | flops | bytes accessed | tf_op | source)
XLA Modules:
  0.0 54.4 jit_solution(1699432343507813546)
XLA Ops:
  0.0 0.0 copy-start
  0.0 2.9 %shard_map.28 = (bf16[32,768]{1,0:T(8,128)(2,1)}, bf16[64,768]{1,0:T(8,128)(2,1)}) custom-call(s32[1]{0:T(128)} %bitcast.1.group_ref, s32[8,256]{1,0:T(8,128)} %list_ref.3, bf16[512,768]{1,0:T(8,128)(2,1)} %mine_ref.1), custom_call_target="tpu_custom_call" | custom-call | tf_op jit(solution)/shard_map/pallas_call | solution.py:274
  2.9 0.0 copy-start.9
  2.9 3.0 %collective-permute-start = (bf16[32,768]{1,0:T(8,128)(2,1)}, bf16[32,768]{1,0:T(8,128)(2,1)S(1)}, u32[]{:S(2)}, u32[]{:S(2)}) collective-permute-start(bf16[32,768]{1,0:T(8,128)(2,1)} %get-tuple-element.11.pool_ref), channel_id=1, source_target_pairs={{0,2},{1,3},{2,0},{3,1},{4,6},{5,7},{6,4},{7,5},{8,10},{9,11},{10,... | collective-permute-start | bytes 147464 | tf_op jit(solution)/shard_map/ppermute | solution.py:255
  5.9 2.1 %shard_map.29.order_ref = bf16[256,256]{1,0:T(8,128)(2,1)} custom-call(s32[1]{0:T(128)} %bitcast.1.group_ref, s32[8,256]{1,0:T(8,128)} %list_ref.3, bf16[32,768]{1,0:T(8,128)(2,1)} %get-tuple-element.11.pool_ref), custom_call_target="tpu_custom_call" | custom-call | flops 1000000000 | bytes 1000000 | tf_op jit(solution)/shard_map/pallas_call | solution.py:286
  8.0 0.2 collective-permute-done
  8.2 0.0 copy-done
  8.2 2.0 %collective-permute-start.10 = (bf16[512,768]{1,0:T(8,128)(2,1)S(1)}, bf16[512,768]{1,0:T(8,128)(2,1)S(1)}, u32[]{:S(2)}, u32[]{:S(2)}) collective-permute-start(bf16[512,768]{1,0:T(8,128)(2,1)S(1)} %copy-done), channel_id=1, source_target_pairs={{0,2},{1,3},{2,0},{3,1},{4,6},{5,7},{6,4},{7,5},{8,10},{9,11},{10,... | collective-permute-start | bytes 2359304 | tf_op jit(solution)/shard_map/ppermute | solution.py:255
  10.2 0.0 copy-done.9
  10.2 0.0 copy-start.10
  10.2 3.7 %collective-permute-start.6 = (bf16[64,768]{1,0:T(8,128)(2,1)S(1)}, bf16[64,768]{1,0:T(8,128)(2,1)S(1)}, u32[]{:S(2)}, u32[]{:S(2)}) collective-permute-start(bf16[64,768]{1,0:T(8,128)(2,1)S(1)} %constant_dynamic-update-slice_fusion.refs_0_), channel_id=1, source_target_pairs={{0,24},{4,28},{8,16},{12,20},{16,8},{20,12},{24,0},{28,4},{1,25},{... | collective-permute-start | bytes 294920 | tf_op jit(solution)/shard_map/ppermute | solution.py:255
  13.9 0.0 collective-permute-start.4
  13.9 0.8 %collective-permute-start.2 = (bf16[64,768]{1,0:T(8,128)(2,1)S(1)}, bf16[64,768]{1,0:T(8,128)(2,1)S(1)}, u32[]{:S(2)}, u32[]{:S(2)}) collective-permute-start(bf16[64,768]{1,0:T(8,128)(2,1)S(1)} %constant_dynamic-update-slice_fusion.refs_0_), channel_id=1, source_target_pairs={{0,8},{4,12},{8,0},{12,4},{16,24},{20,28},{24,16},{28,20},{1,9},{5... | collective-permute-start | bytes 294920 | tf_op jit(solution)/shard_map/ppermute | solution.py:255
  14.7 1.5 %collective-permute-start.1 = (bf16[64,768]{1,0:T(8,128)(2,1)S(1)}, bf16[64,768]{1,0:T(8,128)(2,1)S(1)}, u32[]{:S(2)}, u32[]{:S(2)}) collective-permute-start(bf16[64,768]{1,0:T(8,128)(2,1)S(1)} %constant_dynamic-update-slice_fusion.refs_0_), channel_id=1, source_target_pairs={{0,4},{4,0},{8,12},{12,8},{16,20},{20,16},{24,28},{28,24},{1,5},{5... | collective-permute-start | bytes 294920 | tf_op jit(solution)/shard_map/ppermute | solution.py:255
  16.2 0.5 %collective-permute-done.6.refs_6_ = bf16[64,768]{1,0:T(8,128)(2,1)S(1)} collective-permute-done((bf16[64,768]{1,0:T(8,128)(2,1)S(1)}, bf16[64,768]{1,0:T(8,128)(2,1)S(1)}, u32[]{:S(2)}, u32[]{:S(2)}) %collective-permute-start.6) | collective-permute-done | bytes 98336 | tf_op jit(solution)/shard_map/ppermute | solution.py:255
  16.8 0.0 copy-start.2
  16.8 1.5 %collective-permute-start.7 = (bf16[64,768]{1,0:T(8,128)(2,1)S(1)}, bf16[64,768]{1,0:T(8,128)(2,1)S(1)}, u32[]{:S(2)}, u32[]{:S(2)}) collective-permute-start(bf16[64,768]{1,0:T(8,128)(2,1)S(1)} %collective-permute-done.6.refs_6_), channel_id=1, source_target_pairs={{0,4},{4,0},{8,12},{12,8},{16,20},{20,16},{24,28},{28,24},{1,5},{5... | collective-permute-start | bytes 294920 | tf_op jit(solution)/shard_map/ppermute | solution.py:255
  18.3 2.5 %collective-permute-done.4.refs_4_ = bf16[64,768]{1,0:T(8,128)(2,1)S(1)} collective-permute-done((bf16[64,768]{1,0:T(8,128)(2,1)S(1)}, bf16[64,768]{1,0:T(8,128)(2,1)S(1)}, u32[]{:S(2)}, u32[]{:S(2)}) %collective-permute-start.4) | collective-permute-done | bytes 98336 | tf_op jit(solution)/shard_map/ppermute | solution.py:255
  20.8 0.0 copy-start.3
  20.8 1.5 %collective-permute-start.5 = (bf16[64,768]{1,0:T(8,128)(2,1)S(1)}, bf16[64,768]{1,0:T(8,128)(2,1)S(1)}, u32[]{:S(2)}, u32[]{:S(2)}) collective-permute-start(bf16[64,768]{1,0:T(8,128)(2,1)S(1)} %collective-permute-done.4.refs_4_), channel_id=1, source_target_pairs={{0,4},{4,0},{8,12},{12,8},{16,20},{20,16},{24,28},{28,24},{1,5},{5... | collective-permute-start | bytes 294920 | tf_op jit(solution)/shard_map/ppermute | solution.py:255
  22.4 0.0 collective-permute-done.2.refs_2_
  22.4 0.0 copy-start.4
  22.4 0.5 collective-permute-start.3
  22.9 0.0 collective-permute-done.1.refs_1_
  22.9 0.0 copy-start.5
  22.9 0.0 collective-permute-done.7.refs_7_
  22.9 0.0 copy-start.6
  22.9 3.0 %collective-permute-done.5.refs_5_ = bf16[64,768]{1,0:T(8,128)(2,1)S(1)} collective-permute-done((bf16[64,768]{1,0:T(8,128)(2,1)S(1)}, bf16[64,768]{1,0:T(8,128)(2,1)S(1)}, u32[]{:S(2)}, u32[]{:S(2)}) %collective-permute-start.5) | collective-permute-done | bytes 98336 | tf_op jit(solution)/shard_map/ppermute | solution.py:255
  25.9 0.0 copy-done.10
  25.9 0.0 copy-start.7
  25.9 1.1 %collective-permute-done.3.refs_3_ = bf16[64,768]{1,0:T(8,128)(2,1)S(1)} collective-permute-done((bf16[64,768]{1,0:T(8,128)(2,1)S(1)}, bf16[64,768]{1,0:T(8,128)(2,1)S(1)}, u32[]{:S(2)}, u32[]{:S(2)}) %collective-permute-start.3) | collective-permute-done | bytes 98336 | tf_op jit(solution)/shard_map/ppermute | solution.py:255
  27.0 0.0 copy-start.8
  27.0 0.0 collective-permute-start.9
  27.0 0.1 collective-permute-done.10.mine_ref
  27.0 0.0 copy-done.6
  27.0 0.0 copy-done.7
  27.0 0.6 %copy-done.8 = bf16[64,768]{1,0:T(8,128)(2,1)} copy-done((bf16[64,768]{1,0:T(8,128)(2,1)}, bf16[64,768]{1,0:T(8,128)(2,1)S(1)}, u32[]{:S(2)}) %copy-start.8) | copy-done | bytes 98328
  27.6 0.0 collective-permute-start.11
  27.6 0.0 copy-done.2
  27.6 0.0 copy-done.3
  27.6 0.0 copy-done.4
  27.6 0.0 copy-done.5
  27.6 2.7 %shard_map.30.mine_ref = bf16[2,16,48,256]{3,2,1,0:T(8,128)(2,1)} custom-call(bf16[256,256]{1,0:T(8,128)(2,1)} %shard_map.29.order_ref, bf16[64,768]{1,0:T(8,128)(2,1)} %copy-done.10, bf16[64,768]{1,0:T(8,128)(2,1)} %copy-done.5, bf16[64,768]{1,0:T(8,128)(2,1)} %copy-done.4, bf16[64,768]{1,0:T(8,128)(2,1)} %copy-done.8, bf16[64,768]{1,0:T(8,128)(2,1)} %copy-done.3, ...), custom_call_target="tpu_custom_call" | custom-call | flops 800000000 | bytes 1000000 | tf_op jit(solution)/shard_map/pallas_call | solution.py:317
  30.4 0.5 collective-permute-start.8
  30.9 0.0 collective-permute-done.9.other_ref
  30.9 1.4 %shard_map.31.refs_0_ = bf16[9,512,384]{2,1,0:T(8,128)(2,1)S(1)} custom-call(s32[1]{0:T(128)} %bitcast.2.core_ref, bf16[512,768]{1,0:T(8,128)(2,1)S(1)} %copy-done, bf16[512,768]{1,0:T(8,128)(2,1)S(1)} %collective-permute-done.9.other_ref), custom_call_target="tpu_custom_call" | custom-call | flops 1000 | bytes 1000 | tf_op jit(solution)/shard_map/pallas_call | solution.py:302
  32.3 0.0 copy-start.1
  32.3 0.0 collective-permute-done.11.other_ref
  32.3 1.4 %shard_map.32.refs_1_ = bf16[9,512,384]{2,1,0:T(8,128)(2,1)S(1)} custom-call(s32[1]{0:T(128)} %bitcast.2.core_ref, bf16[512,768]{1,0:T(8,128)(2,1)S(1)} %collective-permute-done.10.mine_ref, bf16[512,768]{1,0:T(8,128)(2,1)S(1)} %collective-permute-done.11.other_ref), custom_call_target="tpu_custom_call" | custom-call | flops 1000 | bytes 1000 | tf_op jit(solution)/shard_map/pallas_call | solution.py:302
  33.7 0.0 collective-permute-done.8.other_ref
  33.7 0.0 copy-done.1
  33.7 20.7 %shard_map.33 = bf16[2,4,4,512,256]{4,3,2,1,0:T(8,128)(2,1)} custom-call(s32[1]{0:T(128)} %bitcast.tm_ref, bf16[2,16,48,256]{3,2,1,0:T(8,128)(2,1)S(1)} %copy-done.1, bf16[2,16,48,256]{3,2,1,0:T(8,128)(2,1)} %collective-permute-done.8.other_ref, bf16[9,512,384]{2,1,0:T(8,128)(2,1)S(1)} %shard_map.31.refs_0_, bf16[9,512,384]{2,1,0:T(8,128)(2,1)S(1)} %shard_map.32.refs_1_), custom_call_target="tpu_custom_call" | custom-call | flops 15000000512 | bytes 20000000 | tf_op jit(solution)/shard_map/pallas_call | solution.py:326
  (1 shorter events, 0.0 us)
Async XLA Ops:
  0.0 8.2 %copy-start = (bf16[512,768]{1,0:T(8,128)(2,1)S(1)}, bf16[512,768]{1,0:T(8,128)(2,1)}, u32[]{:S(2)}) copy-start(bf16[512,768]{1,0:T(8,128)(2,1)} %mine_ref.1) | copy-start | bytes 2359300
  2.9 7.3 %copy-start.9 = (bf16[64,768]{1,0:T(8,128)(2,1)S(1)}, bf16[64,768]{1,0:T(8,128)(2,1)}, u32[]{:S(2)}) copy-start(bf16[64,768]{1,0:T(8,128)(2,1)} %get-tuple-element.13) | copy-start | bytes 294916
  2.9 5.3 %collective-permute-start = (bf16[32,768]{1,0:T(8,128)(2,1)}, bf16[32,768]{1,0:T(8,128)(2,1)S(1)}, u32[]{:S(2)}, u32[]{:S(2)}) collective-permute-start(bf16[32,768]{1,0:T(8,128)(2,1)} %get-tuple-element.11.pool_ref), channel_id=1, source_target_pairs={{0,2},{1,3},{2,0},{3,1},{4,6},{5,7},{6,4},{7,5},{8,10},{9,11},{10,... | collective-permute-start | bytes 147464 | tf_op jit(solution)/shard_map/ppermute | solution.py:255
  8.2 18.8 %collective-permute-start.10 = (bf16[512,768]{1,0:T(8,128)(2,1)S(1)}, bf16[512,768]{1,0:T(8,128)(2,1)S(1)}, u32[]{:S(2)}, u32[]{:S(2)}) collective-permute-start(bf16[512,768]{1,0:T(8,128)(2,1)S(1)} %copy-done), channel_id=1, source_target_pairs={{0,2},{1,3},{2,0},{3,1},{4,6},{5,7},{6,4},{7,5},{8,10},{9,11},{10,... | collective-permute-start | bytes 2359304 | tf_op jit(solution)/shard_map/ppermute | solution.py:255
  10.2 15.7 %copy-start.10 = (bf16[64,768]{1,0:T(8,128)(2,1)}, bf16[64,768]{1,0:T(8,128)(2,1)S(1)}, u32[]{:S(2)}) copy-start(bf16[64,768]{1,0:T(8,128)(2,1)S(1)} %constant_dynamic-update-slice_fusion.refs_0_) | copy-start | bytes 294916
  10.2 6.5 %collective-permute-start.6 = (bf16[64,768]{1,0:T(8,128)(2,1)S(1)}, bf16[64,768]{1,0:T(8,128)(2,1)S(1)}, u32[]{:S(2)}, u32[]{:S(2)}) collective-permute-start(bf16[64,768]{1,0:T(8,128)(2,1)S(1)} %constant_dynamic-update-slice_fusion.refs_0_), channel_id=1, source_target_pairs={{0,24},{4,28},{8,16},{12,20},{16,8},{20,12},{24,0},{28,4},{1,25},{... | collective-permute-start | bytes 294920 | tf_op jit(solution)/shard_map/ppermute | solution.py:255
  13.9 6.9 %collective-permute-start.4 = (bf16[64,768]{1,0:T(8,128)(2,1)S(1)}, bf16[64,768]{1,0:T(8,128)(2,1)S(1)}, u32[]{:S(2)}, u32[]{:S(2)}) collective-permute-start(bf16[64,768]{1,0:T(8,128)(2,1)S(1)} %constant_dynamic-update-slice_fusion.refs_0_), channel_id=1, source_target_pairs={{0,16},{4,20},{8,24},{12,28},{16,0},{20,4},{24,8},{28,12},{1,17},{... | collective-permute-start | bytes 294920 | tf_op jit(solution)/shard_map/ppermute | solution.py:255
  13.9 8.4 %collective-permute-start.2 = (bf16[64,768]{1,0:T(8,128)(2,1)S(1)}, bf16[64,768]{1,0:T(8,128)(2,1)S(1)}, u32[]{:S(2)}, u32[]{:S(2)}) collective-permute-start(bf16[64,768]{1,0:T(8,128)(2,1)S(1)} %constant_dynamic-update-slice_fusion.refs_0_), channel_id=1, source_target_pairs={{0,8},{4,12},{8,0},{12,4},{16,24},{20,28},{24,16},{28,20},{1,9},{5... | collective-permute-start | bytes 294920 | tf_op jit(solution)/shard_map/ppermute | solution.py:255
  14.7 8.2 %collective-permute-start.1 = (bf16[64,768]{1,0:T(8,128)(2,1)S(1)}, bf16[64,768]{1,0:T(8,128)(2,1)S(1)}, u32[]{:S(2)}, u32[]{:S(2)}) collective-permute-start(bf16[64,768]{1,0:T(8,128)(2,1)S(1)} %constant_dynamic-update-slice_fusion.refs_0_), channel_id=1, source_target_pairs={{0,4},{4,0},{8,12},{12,8},{16,20},{20,16},{24,28},{28,24},{1,5},{5... | collective-permute-start | bytes 294920 | tf_op jit(solution)/shard_map/ppermute | solution.py:255
  16.8 10.9 %copy-start.2 = (bf16[64,768]{1,0:T(8,128)(2,1)}, bf16[64,768]{1,0:T(8,128)(2,1)S(1)}, u32[]{:S(2)}) copy-start(bf16[64,768]{1,0:T(8,128)(2,1)S(1)} %collective-permute-done.6.refs_6_) | copy-start | bytes 294916
  16.8 6.1 %collective-permute-start.7 = (bf16[64,768]{1,0:T(8,128)(2,1)S(1)}, bf16[64,768]{1,0:T(8,128)(2,1)S(1)}, u32[]{:S(2)}, u32[]{:S(2)}) collective-permute-start(bf16[64,768]{1,0:T(8,128)(2,1)S(1)} %collective-permute-done.6.refs_6_), channel_id=1, source_target_pairs={{0,4},{4,0},{8,12},{12,8},{16,20},{20,16},{24,28},{28,24},{1,5},{5... | collective-permute-start | bytes 294920 | tf_op jit(solution)/shard_map/ppermute | solution.py:255
  20.8 6.8 %copy-start.3 = (bf16[64,768]{1,0:T(8,128)(2,1)}, bf16[64,768]{1,0:T(8,128)(2,1)S(1)}, u32[]{:S(2)}) copy-start(bf16[64,768]{1,0:T(8,128)(2,1)S(1)} %collective-permute-done.4.refs_4_) | copy-start | bytes 294916
  20.8 5.1 %collective-permute-start.5 = (bf16[64,768]{1,0:T(8,128)(2,1)S(1)}, bf16[64,768]{1,0:T(8,128)(2,1)S(1)}, u32[]{:S(2)}, u32[]{:S(2)}) collective-permute-start(bf16[64,768]{1,0:T(8,128)(2,1)S(1)} %collective-permute-done.4.refs_4_), channel_id=1, source_target_pairs={{0,4},{4,0},{8,12},{12,8},{16,20},{20,16},{24,28},{28,24},{1,5},{5... | collective-permute-start | bytes 294920 | tf_op jit(solution)/shard_map/ppermute | solution.py:255
  22.4 5.3 %copy-start.4 = (bf16[64,768]{1,0:T(8,128)(2,1)}, bf16[64,768]{1,0:T(8,128)(2,1)S(1)}, u32[]{:S(2)}) copy-start(bf16[64,768]{1,0:T(8,128)(2,1)S(1)} %collective-permute-done.2.refs_2_) | copy-start | bytes 294916
  22.4 4.6 %collective-permute-start.3 = (bf16[64,768]{1,0:T(8,128)(2,1)S(1)}, bf16[64,768]{1,0:T(8,128)(2,1)S(1)}, u32[]{:S(2)}, u32[]{:S(2)}) collective-permute-start(bf16[64,768]{1,0:T(8,128)(2,1)S(1)} %collective-permute-done.2.refs_2_), channel_id=1, source_target_pairs={{0,4},{4,0},{8,12},{12,8},{16,20},{20,16},{24,28},{28,24},{1,5},{5... | collective-permute-start | bytes 294920 | tf_op jit(solution)/shard_map/ppermute | solution.py:255
  22.9 4.8 %copy-start.5 = (bf16[64,768]{1,0:T(8,128)(2,1)}, bf16[64,768]{1,0:T(8,128)(2,1)S(1)}, u32[]{:S(2)}) copy-start(bf16[64,768]{1,0:T(8,128)(2,1)S(1)} %collective-permute-done.1.refs_1_) | copy-start | bytes 294916
  22.9 4.1 %copy-start.6 = (bf16[64,768]{1,0:T(8,128)(2,1)}, bf16[64,768]{1,0:T(8,128)(2,1)S(1)}, u32[]{:S(2)}) copy-start(bf16[64,768]{1,0:T(8,128)(2,1)S(1)} %collective-permute-done.7.refs_7_) | copy-start | bytes 294916
  25.9 1.1 %copy-start.7 = (bf16[64,768]{1,0:T(8,128)(2,1)}, bf16[64,768]{1,0:T(8,128)(2,1)S(1)}, u32[]{:S(2)}) copy-start(bf16[64,768]{1,0:T(8,128)(2,1)S(1)} %collective-permute-done.5.refs_5_) | copy-start | bytes 294916
  27.0 0.6 %copy-start.8 = (bf16[64,768]{1,0:T(8,128)(2,1)}, bf16[64,768]{1,0:T(8,128)(2,1)S(1)}, u32[]{:S(2)}) copy-start(bf16[64,768]{1,0:T(8,128)(2,1)S(1)} %collective-permute-done.3.refs_3_) | copy-start | bytes 294916
  27.0 3.9 %collective-permute-start.9 = (bf16[512,768]{1,0:T(8,128)(2,1)S(1)}, bf16[512,768]{1,0:T(8,128)(2,1)S(1)}, u32[]{:S(2)}, u32[]{:S(2)}) collective-permute-start(bf16[512,768]{1,0:T(8,128)(2,1)S(1)} %copy-done), channel_id=1, source_target_pairs={{0,1},{1,0},{2,3},{3,2},{4,5},{5,4},{6,7},{7,6},{8,9},{9,8},{10,11... | collective-permute-start | bytes 2359304 | tf_op jit(solution)/shard_map/ppermute | solution.py:255
  27.6 4.7 %collective-permute-start.11 = (bf16[512,768]{1,0:T(8,128)(2,1)S(1)}, bf16[512,768]{1,0:T(8,128)(2,1)S(1)}, u32[]{:S(2)}, u32[]{:S(2)}) collective-permute-start(bf16[512,768]{1,0:T(8,128)(2,1)S(1)} %collective-permute-done.10.mine_ref), channel_id=1, source_target_pairs={{0,1},{1,0},{2,3},{3,2},{4,5},{5,4},{6,7},{7,6},{8,9},{9,8},{10,11... | collective-permute-start | bytes 2359304 | tf_op jit(solution)/shard_map/ppermute | solution.py:255
  30.4 3.3 %collective-permute-start.8 = (bf16[2,16,48,256]{3,2,1,0:T(8,128)(2,1)}, bf16[2,16,48,256]{3,2,1,0:T(8,128)(2,1)}, u32[]{:S(2)}, u32[]{:S(2)}) collective-permute-start(bf16[2,16,48,256]{3,2,1,0:T(8,128)(2,1)} %shard_map.30.mine_ref), channel_id=1, source_target_pairs={{0,1},{1,0},{2,3},{3,2},{4,5},{5,4},{6,7},{7,6},{8,9},{9,8},{10,11... | collective-permute-start | bytes 2359304 | tf_op jit(solution)/shard_map/ppermute | solution.py:255
  32.3 1.4 %copy-start.1 = (bf16[2,16,48,256]{3,2,1,0:T(8,128)(2,1)S(1)}, bf16[2,16,48,256]{3,2,1,0:T(8,128)(2,1)}, u32[]{:S(2)}) copy-start(bf16[2,16,48,256]{3,2,1,0:T(8,128)(2,1)} %shard_map.30.mine_ref) | copy-start | bytes 2359300

commit v4 on v3

--- a/solution.py
+++ b/solution.py
@@ -81,9 +81,12 @@
     return high, low
 
 
-def select_kernel(group_ref, list_ref, s_hbm, pool_ref, pair_ref, s_ref, rank_ref, sem):
-    copy = pltpu.make_async_copy(s_hbm, s_ref, sem)
+def select_kernel(group_ref, list_hbm, s_hbm, pool_ref, pair_ref, list_ref, s_ref, rank_ref, sem):
+    list_copy = pltpu.make_async_copy(list_hbm, list_ref, sem.at[0])
+    list_copy.start()
+    copy = pltpu.make_async_copy(s_hbm, s_ref, sem.at[1])
     copy.start()
+    list_copy.wait()
     per = s_ref.shape[0] // 128
     highs = list_ref.shape[0] * per
     high, low = marks_of(list_ref, highs)
@@ -106,8 +109,7 @@
     pair_ref[POOL:] = jnp.zeros_like(rows)
 
 
-def order_kernel(group_ref, list_ref, pool_ref, order_ref, *, per):
-    del pool_ref
+def order_kernel(group_ref, list_ref, order_ref, *, per):
     groups, width = list_ref.shape
     highs = groups * per
     own = group_ref[0]
@@ -271,28 +273,33 @@
     vmem = pl.BlockSpec(memory_space=pltpu.VMEM)
     hbm = pl.BlockSpec(memory_space=pltpu.HBM)
     anywhere = pl.BlockSpec(memory_space=pl.ANY)
+    small = pltpu.CompilerParams(vmem_limit_bytes=12 * 2**20)
     own_pool, pair = pl.pallas_call(
         select_kernel,
-        in_specs=[smem, vmem, hbm],
+        in_specs=[smem, hbm, hbm],
         out_specs=[vmem, vmem],
         out_shape=[jax.ShapeDtypeStruct((rows, time_len), BF16) for rows in (POOL, 2 * POOL)],
         scratch_shapes=[
+            pltpu.VMEM((groups, refs), jnp.int32),
             pltpu.VMEM((chan_rows, time_len), BF16),
             pltpu.VMEM((groups * chan_rows // 128, 128), F32),
-            pltpu.SemaphoreType.DMA(()),
+            pltpu.SemaphoreType.DMA((2,)),
         ],
+        compiler_params=pltpu.CompilerParams(vmem_limit_bytes=60 * 2**20),
     )(group[None], ref_list, series)
     pool_x = flip(own_pool, "tm", 2)
     order = pl.pallas_call(
         functools.partial(order_kernel, per=chan_rows // 128),
-        in_specs=[smem, vmem, hbm],
+        in_specs=[smem, vmem],
         out_specs=vmem,
         out_shape=jax.ShapeDtypeStruct((groups * POOL, refs), BF16),
+        compiler_params=small,
         cost_estimate=pl.CostEstimate(flops=10**9, bytes_accessed=10**6, transcendentals=0),
-    )(group[None], ref_list, own_pool)
+    )(group[None], after(ref_list, own_pool))
     pair = lax.dynamic_update_slice(after(pair, order), pool_x, (POOL, 0))
     series_x = flip(after(series, pool_x, order), "tm", 2)
-    along_z = [pair] + [flip(pair, "chan", 2 * d) for d in range(1, groups // 2)]
+    along_z = [pair, flip(pair, "chan", 2), flip(pair, "chan", 4)]
+    along_z.append(flip(along_z[2], "chan", 2))
     pool = []
     for piece in along_z:
         pool += [piece, flip(piece, "chan", 1)]
@@ -319,6 +326,7 @@
         in_specs=[vmem] * (1 + len(pool)),
         out_specs=vmem,
         out_shape=jax.ShapeDtypeStruct((2, PH, time_len // PH, refs), BF16),
+        compiler_params=small,
         cost_estimate=pl.CostEstimate(flops=8 * 10**8, bytes_accessed=10**6, transcendentals=0),
     )(order, *pool)
     placed_c = flip(placed, "tm", 1)

time: 54.7 us -> 52.1 us (0.952)
  Pallas kernels: 31.2 us -> 28.4 us
  starting transfers between devices: 15.1 us -> 15.8 us
    pallas_call x1, Pallas kernels: 2.1 us -> 0.75 us  [block_shards(): pl.pallas_call(functools.partial(order_kernel, per=chan_rows // 128), in_...]
    pallas_call x1, Pallas kernels: 2.73 us -> 1.52 us  [block_shards(): pl.pallas_call(refs_kernel, in_specs=[vmem] * (1 + len(pool)), out_specs=...]
    ppermute x12, starting transfers between devices: 15.1 us -> 15.8 us  [flip(): lax.ppermute(array, axis, [(i, i ^ by) for i in range(lax.axis_size(axis))])]
  transfers between devices with their start and end apart: 12 -> 12, of which waited for: 6 -> 7; matrix products, arithmetic and copies ran while one was open for 0% -> 0% of each run, Pallas kernels for 14% -> 10%
where the time goes in v4:
time: 52.1 us; the launch traced here: 51.9 us
  Pallas kernels  28.4 us (55%)
  starting transfers between devices  15.8 us (30%)
  waiting for transfers between devices  6.91 us (13%)
  local copies, waits for them, and re-layouts  0.71 us (1%)
    pallas_call x1, Pallas kernels, block_shards(): pl.pallas_call(functools.partial(corr_kernel, windows=windows, scale=1.0...  20.9 us
    ppermute x12, starting transfers between devices, flip(): lax.ppermute(array, axis, [(i, i ^ by) for i in range(lax.axis_size(axis))])  15.8 us
    ppermute x12, waiting for transfers between devices, flip(): lax.ppermute(array, axis, [(i, i ^ by) for i in range(lax.axis_size(axis))])  6.91 us
    pallas_call x2, Pallas kernels, phases(): pl.pallas_call(series_kernel, in_specs=[smem, hbm, hbm], out_specs=vmem,...  2.79 us
    pallas_call x1, Pallas kernels, block_shards(): pl.pallas_call(select_kernel, in_specs=[smem, hbm, hbm], out_specs=[vmem,...  2.42 us
    pallas_call x1, Pallas kernels, block_shards(): pl.pallas_call(refs_kernel, in_specs=[vmem] * (1 + len(pool)), out_specs=...  1.52 us
  transfers between devices with their start and end apart: 12, of which 7 were waited for; matrix products, arithmetic and copies ran while one was open for 0% of the time, Pallas kernels for 10%

profile of v4, /device:TPU:0, one launch (start us, length us, event | category | flops | bytes accessed | tf_op | source)
XLA Modules:
  0.0 51.9 jit_solution(4557532519118945149)
XLA Ops:
  0.0 0.0 copy-start
  0.0 2.4 %shard_map.28 = (bf16[32,768]{1,0:T(8,128)(2,1)}, bf16[64,768]{1,0:T(8,128)(2,1)}) custom-call(s32[1]{0:T(128)} %bitcast.1.group_ref, s32[8,256]{1,0:T(8,128)} %list_ref, bf16[512,768]{1,0:T(8,128)(2,1)} %mine_ref.1), custom_call_target="tpu_custom_call" | custom-call | tf_op jit(solution)/shard_map/pallas_call | solution.py:277
  2.4 3.0 %collective-permute-start = (bf16[32,768]{1,0:T(8,128)(2,1)}, bf16[32,768]{1,0:T(8,128)(2,1)S(1)}, u32[]{:S(2)}, u32[]{:S(2)}) collective-permute-start(bf16[32,768]{1,0:T(8,128)(2,1)} %get-tuple-element.12), channel_id=1, source_target_pairs={{0,2},{1,3},{2,0},{3,1},{4,6},{5,7},{6,4},{7,5},{8,10},{9,11},{10,... | collective-permute-start | bytes 147464 | tf_op jit(solution)/shard_map/ppermute | solution.py:257
  5.4 0.0 copy-start.1
  5.4 0.7 %copy-done.1 = s32[8,256]{1,0:T(8,128)S(1)} copy-done((s32[8,256]{1,0:T(8,128)S(1)}, s32[8,256]{1,0:T(8,128)}, u32[]{:S(2)}) %copy-start.1) | copy-done | bytes 8216
  6.1 0.0 copy-start.2
  6.1 0.8 %shard_map.29.order_ref = bf16[256,256]{1,0:T(8,128)(2,1)S(1)} custom-call(s32[1]{0:T(128)} %bitcast.1.group_ref, s32[8,256]{1,0:T(8,128)S(1)} %copy-done.1), custom_call_target="tpu_custom_call" | custom-call | flops 1000000000 | bytes 1000000 | tf_op jit(solution)/shard_map/pallas_call | solution.py:291
  6.9 0.8 %collective-permute-done = bf16[32,768]{1,0:T(8,128)(2,1)S(1)} collective-permute-done((bf16[32,768]{1,0:T(8,128)(2,1)}, bf16[32,768]{1,0:T(8,128)(2,1)S(1)}, u32[]{:S(2)}, u32[]{:S(2)}) %collective-permute-start) | collective-permute-done | bytes 49184 | tf_op jit(solution)/shard_map/ppermute | solution.py:257
  7.7 0.0 copy-done
  7.7 2.0 %collective-permute-start.10 = (bf16[512,768]{1,0:T(8,128)(2,1)S(1)}, bf16[512,768]{1,0:T(8,128)(2,1)S(1)}, u32[]{:S(2)}, u32[]{:S(2)}) collective-permute-start(bf16[512,768]{1,0:T(8,128)(2,1)S(1)} %copy-done), channel_id=1, source_target_pairs={{0,2},{1,3},{2,0},{3,1},{4,6},{5,7},{6,4},{7,5},{8,10},{9,11},{10,... | collective-permute-start | bytes 2359304 | tf_op jit(solution)/shard_map/ppermute | solution.py:257
  9.7 0.0 copy-done.2
  9.7 2.6 %collective-permute-start.4 = (bf16[64,768]{1,0:T(8,128)(2,1)S(1)}, bf16[64,768]{1,0:T(8,128)(2,1)S(1)}, u32[]{:S(2)}, u32[]{:S(2)}) collective-permute-start(bf16[64,768]{1,0:T(8,128)(2,1)S(1)} %constant_dynamic-update-slice_fusion.refs_0_), channel_id=1, source_target_pairs={{0,16},{4,20},{8,24},{12,28},{16,0},{20,4},{24,8},{28,12},{1,17},{... | collective-permute-start | bytes 294920 | tf_op jit(solution)/shard_map/ppermute | solution.py:257
  12.3 1.6 %collective-permute-start.2 = (bf16[64,768]{1,0:T(8,128)(2,1)S(1)}, bf16[64,768]{1,0:T(8,128)(2,1)S(1)}, u32[]{:S(2)}, u32[]{:S(2)}) collective-permute-start(bf16[64,768]{1,0:T(8,128)(2,1)S(1)} %constant_dynamic-update-slice_fusion.refs_0_), channel_id=1, source_target_pairs={{0,8},{4,12},{8,0},{12,4},{16,24},{20,28},{24,16},{28,20},{1,9},{5... | collective-permute-start | bytes 294920 | tf_op jit(solution)/shard_map/ppermute | solution.py:257
  13.9 1.4 %collective-permute-done.4.refs_4_ = bf16[64,768]{1,0:T(8,128)(2,1)S(1)} collective-permute-done((bf16[64,768]{1,0:T(8,128)(2,1)S(1)}, bf16[64,768]{1,0:T(8,128)(2,1)S(1)}, u32[]{:S(2)}, u32[]{:S(2)}) %collective-permute-start.4) | collective-permute-done | bytes 98336 | tf_op jit(solution)/shard_map/ppermute | solution.py:257
  15.3 1.7 %collective-permute-start.6 = (bf16[64,768]{1,0:T(8,128)(2,1)S(1)}, bf16[64,768]{1,0:T(8,128)(2,1)S(1)}, u32[]{:S(2)}, u32[]{:S(2)}) collective-permute-start(bf16[64,768]{1,0:T(8,128)(2,1)S(1)} %collective-permute-done.4.refs_4_), channel_id=1, source_target_pairs={{0,8},{4,12},{8,0},{12,4},{16,24},{20,28},{24,16},{28,20},{1,9},{5... | collective-permute-start | bytes 294920 | tf_op jit(solution)/shard_map/ppermute | solution.py:257
  17.0 1.5 %collective-permute-start.1 = (bf16[64,768]{1,0:T(8,128)(2,1)S(1)}, bf16[64,768]{1,0:T(8,128)(2,1)S(1)}, u32[]{:S(2)}, u32[]{:S(2)}) collective-permute-start(bf16[64,768]{1,0:T(8,128)(2,1)S(1)} %constant_dynamic-update-slice_fusion.refs_0_), channel_id=1, source_target_pairs={{0,4},{4,0},{8,12},{12,8},{16,20},{20,16},{24,28},{28,24},{1,5},{5... | collective-permute-start | bytes 294920 | tf_op jit(solution)/shard_map/ppermute | solution.py:257
  18.5 0.5 collective-permute-start.5
  19.0 0.0 collective-permute-done.2.refs_2_
  19.0 1.5 %collective-permute-start.3 = (bf16[64,768]{1,0:T(8,128)(2,1)S(1)}, bf16[64,768]{1,0:T(8,128)(2,1)S(1)}, u32[]{:S(2)}, u32[]{:S(2)}) collective-permute-start(bf16[64,768]{1,0:T(8,128)(2,1)S(1)} %collective-permute-done.2.refs_2_), channel_id=1, source_target_pairs={{0,4},{4,0},{8,12},{12,8},{16,20},{20,16},{24,28},{28,24},{1,5},{5... | collective-permute-start | bytes 294920 | tf_op jit(solution)/shard_map/ppermute | solution.py:257
  20.5 0.0 collective-permute-done.6.refs_6_
  20.5 0.9 %collective-permute-start.7 = (bf16[64,768]{1,0:T(8,128)(2,1)S(1)}, bf16[64,768]{1,0:T(8,128)(2,1)S(1)}, u32[]{:S(2)}, u32[]{:S(2)}) collective-permute-start(bf16[64,768]{1,0:T(8,128)(2,1)S(1)} %collective-permute-done.6.refs_6_), channel_id=1, source_target_pairs={{0,4},{4,0},{8,12},{12,8},{16,20},{20,16},{24,28},{28,24},{1,5},{5... | collective-permute-start | bytes 294920 | tf_op jit(solution)/shard_map/ppermute | solution.py:257
  21.4 0.9 %collective-permute-done.1.refs_1_ = bf16[64,768]{1,0:T(8,128)(2,1)S(1)} collective-permute-done((bf16[64,768]{1,0:T(8,128)(2,1)S(1)}, bf16[64,768]{1,0:T(8,128)(2,1)S(1)}, u32[]{:S(2)}, u32[]{:S(2)}) %collective-permute-start.1) | collective-permute-done | bytes 98336 | tf_op jit(solution)/shard_map/ppermute | solution.py:257
  22.3 1.1 %collective-permute-done.5.refs_5_ = bf16[64,768]{1,0:T(8,128)(2,1)S(1)} collective-permute-done((bf16[64,768]{1,0:T(8,128)(2,1)S(1)}, bf16[64,768]{1,0:T(8,128)(2,1)S(1)}, u32[]{:S(2)}, u32[]{:S(2)}) %collective-permute-start.5) | collective-permute-done | bytes 98336 | tf_op jit(solution)/shard_map/ppermute | solution.py:257
  23.4 1.1 %collective-permute-done.3.refs_3_ = bf16[64,768]{1,0:T(8,128)(2,1)S(1)} collective-permute-done((bf16[64,768]{1,0:T(8,128)(2,1)S(1)}, bf16[64,768]{1,0:T(8,128)(2,1)S(1)}, u32[]{:S(2)}, u32[]{:S(2)}) %collective-permute-start.3) | collective-permute-done | bytes 98336 | tf_op jit(solution)/shard_map/ppermute | solution.py:257
  24.4 1.1 %collective-permute-done.7.refs_7_ = bf16[64,768]{1,0:T(8,128)(2,1)S(1)} collective-permute-done((bf16[64,768]{1,0:T(8,128)(2,1)S(1)}, bf16[64,768]{1,0:T(8,128)(2,1)S(1)}, u32[]{:S(2)}, u32[]{:S(2)}) %collective-permute-start.7) | collective-permute-done | bytes 98336 | tf_op jit(solution)/shard_map/ppermute | solution.py:257
  25.5 0.0 collective-permute-start.9
  25.5 0.7 %collective-permute-done.10.mine_ref = bf16[512,768]{1,0:T(8,128)(2,1)S(1)} collective-permute-done((bf16[512,768]{1,0:T(8,128)(2,1)S(1)}, bf16[512,768]{1,0:T(8,128)(2,1)S(1)}, u32[]{:S(2)}, u32[]{:S(2)}) %collective-permute-start.10) | collective-permute-done | bytes 786464 | tf_op jit(solution)/shard_map/ppermute | solution.py:257
  26.1 0.0 collective-permute-start.11
  26.1 1.5 %shard_map.30.mine_ref = bf16[2,16,48,256]{3,2,1,0:T(8,128)(2,1)} custom-call(bf16[256,256]{1,0:T(8,128)(2,1)S(1)} %shard_map.29.order_ref, bf16[64,768]{1,0:T(8,128)(2,1)S(1)} %constant_dynamic-update-slice_fusion.refs_0_, bf16[64,768]{1,0:T(8,128)(2,1)S(1)} %collective-permute-done.1.refs_1_, bf16[64,768]{1,0:T(8,128)(2,1)S(1)} %collective-permute-done.2.refs_2_, ...), custom_call_target="tpu_custom_call" | custom-call | flops 800000000 | bytes 1000000 | tf_op jit(solution)/shard_map/pallas_call | solution.py:324
  27.7 0.5 collective-permute-start.8
  28.2 0.0 collective-permute-done.9.other_ref
  28.2 1.4 %shard_map.31.refs_0_ = bf16[9,512,384]{2,1,0:T(8,128)(2,1)S(1)} custom-call(s32[1]{0:T(128)} %bitcast.2.core_ref, bf16[512,768]{1,0:T(8,128)(2,1)S(1)} %copy-done, bf16[512,768]{1,0:T(8,128)(2,1)S(1)} %collective-permute-done.9.other_ref), custom_call_target="tpu_custom_call" | custom-call | flops 1000 | bytes 1000 | tf_op jit(solution)/shard_map/pallas_call | solution.py:309
  29.6 0.0 collective-permute-done.11.other_ref
  29.6 1.4 %shard_map.32.refs_1_ = bf16[9,512,384]{2,1,0:T(8,128)(2,1)S(1)} custom-call(s32[1]{0:T(128)} %bitcast.2.core_ref, bf16[512,768]{1,0:T(8,128)(2,1)S(1)} %collective-permute-done.10.mine_ref, bf16[512,768]{1,0:T(8,128)(2,1)S(1)} %collective-permute-done.11.other_ref), custom_call_target="tpu_custom_call" | custom-call | flops 1000 | bytes 1000 | tf_op jit(solution)/shard_map/pallas_call | solution.py:309
  31.0 0.0 collective-permute-done.8.other_ref
  31.0 20.9 %shard_map.33 = bf16[2,4,4,512,256]{4,3,2,1,0:T(8,128)(2,1)} custom-call(s32[1]{0:T(128)} %bitcast.tm_ref, bf16[2,16,48,256]{3,2,1,0:T(8,128)(2,1)} %shard_map.30.mine_ref, bf16[2,16,48,256]{3,2,1,0:T(8,128)(2,1)} %collective-permute-done.8.other_ref, bf16[9,512,384]{2,1,0:T(8,128)(2,1)S(1)} %shard_map.31.refs_0_, bf16[9,512,384]{2,1,0:T(8,128)(2,1)S(1)} %shard_map.32.refs_1_), custom_call_target="tpu_custom_call" | custom-call | flops 15000000512 | bytes 20000000 | tf_op jit(solution)/shard_map/pallas_call | solution.py:334
  (1 shorter events, 0.0 us)
Async XLA Ops:
  0.0 7.7 %copy-start = (bf16[512,768]{1,0:T(8,128)(2,1)S(1)}, bf16[512,768]{1,0:T(8,128)(2,1)}, u32[]{:S(2)}) copy-start(bf16[512,768]{1,0:T(8,128)(2,1)} %mine_ref.1) | copy-start | bytes 2359300
  2.4 5.3 %collective-permute-start = (bf16[32,768]{1,0:T(8,128)(2,1)}, bf16[32,768]{1,0:T(8,128)(2,1)S(1)}, u32[]{:S(2)}, u32[]{:S(2)}) collective-permute-start(bf16[32,768]{1,0:T(8,128)(2,1)} %get-tuple-element.12), channel_id=1, source_target_pairs={{0,2},{1,3},{2,0},{3,1},{4,6},{5,7},{6,4},{7,5},{8,10},{9,11},{10,... | collective-permute-start | bytes 147464 | tf_op jit(solution)/shard_map/ppermute | solution.py:257
  5.4 0.7 %copy-start.1 = (s32[8,256]{1,0:T(8,128)S(1)}, s32[8,256]{1,0:T(8,128)}, u32[]{:S(2)}) copy-start(s32[8,256]{1,0:T(8,128)} %list_ref) | copy-start | bytes 24580
  6.1 3.6 %copy-start.2 = (bf16[64,768]{1,0:T(8,128)(2,1)S(1)}, bf16[64,768]{1,0:T(8,128)(2,1)}, u32[]{:S(2)}) copy-start(bf16[64,768]{1,0:T(8,128)(2,1)} %get-tuple-element.15) | copy-start | bytes 294916
  7.7 18.4 %collective-permute-start.10 = (bf16[512,768]{1,0:T(8,128)(2,1)S(1)}, bf16[512,768]{1,0:T(8,128)(2,1)S(1)}, u32[]{:S(2)}, u32[]{:S(2)}) collective-permute-start(bf16[512,768]{1,0:T(8,128)(2,1)S(1)} %copy-done), channel_id=1, source_target_pairs={{0,2},{1,3},{2,0},{3,1},{4,6},{5,7},{6,4},{7,5},{8,10},{9,11},{10,... | collective-permute-start | bytes 2359304 | tf_op jit(solution)/shard_map/ppermute | solution.py:257
  9.7 5.5 %collective-permute-start.4 = (bf16[64,768]{1,0:T(8,128)(2,1)S(1)}, bf16[64,768]{1,0:T(8,128)(2,1)S(1)}, u32[]{:S(2)}, u32[]{:S(2)}) collective-permute-start(bf16[64,768]{1,0:T(8,128)(2,1)S(1)} %constant_dynamic-update-slice_fusion.refs_0_), channel_id=1, source_target_pairs={{0,16},{4,20},{8,24},{12,28},{16,0},{20,4},{24,8},{28,12},{1,17},{... | collective-permute-start | bytes 294920 | tf_op jit(solution)/shard_map/ppermute | solution.py:257
  12.3 6.7 %collective-permute-start.2 = (bf16[64,768]{1,0:T(8,128)(2,1)S(1)}, bf16[64,768]{1,0:T(8,128)(2,1)S(1)}, u32[]{:S(2)}, u32[]{:S(2)}) collective-permute-start(bf16[64,768]{1,0:T(8,128)(2,1)S(1)} %constant_dynamic-update-slice_fusion.refs_0_), channel_id=1, source_target_pairs={{0,8},{4,12},{8,0},{12,4},{16,24},{20,28},{24,16},{28,20},{1,9},{5... | collective-permute-start | bytes 294920 | tf_op jit(solution)/shard_map/ppermute | solution.py:257
  15.3 5.3 %collective-permute-start.6 = (bf16[64,768]{1,0:T(8,128)(2,1)S(1)}, bf16[64,768]{1,0:T(8,128)(2,1)S(1)}, u32[]{:S(2)}, u32[]{:S(2)}) collective-permute-start(bf16[64,768]{1,0:T(8,128)(2,1)S(1)} %collective-permute-done.4.refs_4_), channel_id=1, source_target_pairs={{0,8},{4,12},{8,0},{12,4},{16,24},{20,28},{24,16},{28,20},{1,9},{5... | collective-permute-start | bytes 294920 | tf_op jit(solution)/shard_map/ppermute | solution.py:257
  17.0 5.3 %collective-permute-start.1 = (bf16[64,768]{1,0:T(8,128)(2,1)S(1)}, bf16[64,768]{1,0:T(8,128)(2,1)S(1)}, u32[]{:S(2)}, u32[]{:S(2)}) collective-permute-start(bf16[64,768]{1,0:T(8,128)(2,1)S(1)} %constant_dynamic-update-slice_fusion.refs_0_), channel_id=1, source_target_pairs={{0,4},{4,0},{8,12},{12,8},{16,20},{20,16},{24,28},{28,24},{1,5},{5... | collective-permute-start | bytes 294920 | tf_op jit(solution)/shard_map/ppermute | solution.py:257
  18.5 4.9 %collective-permute-start.5 = (bf16[64,768]{1,0:T(8,128)(2,1)S(1)}, bf16[64,768]{1,0:T(8,128)(2,1)S(1)}, u32[]{:S(2)}, u32[]{:S(2)}) collective-permute-start(bf16[64,768]{1,0:T(8,128)(2,1)S(1)} %collective-permute-done.4.refs_4_), channel_id=1, source_target_pairs={{0,4},{4,0},{8,12},{12,8},{16,20},{20,16},{24,28},{28,24},{1,5},{5... | collective-permute-start | bytes 294920 | tf_op jit(solution)/shard_map/ppermute | solution.py:257
  19.0 5.4 %collective-permute-start.3 = (bf16[64,768]{1,0:T(8,128)(2,1)S(1)}, bf16[64,768]{1,0:T(8,128)(2,1)S(1)}, u32[]{:S(2)}, u32[]{:S(2)}) collective-permute-start(bf16[64,768]{1,0:T(8,128)(2,1)S(1)} %collective-permute-done.2.refs_2_), channel_id=1, source_target_pairs={{0,4},{4,0},{8,12},{12,8},{16,20},{20,16},{24,28},{28,24},{1,5},{5... | collective-permute-start | bytes 294920 | tf_op jit(solution)/shard_map/ppermute | solution.py:257
  20.5 4.9 %collective-permute-start.7 = (bf16[64,768]{1,0:T(8,128)(2,1)S(1)}, bf16[64,768]{1,0:T(8,128)(2,1)S(1)}, u32[]{:S(2)}, u32[]{:S(2)}) collective-permute-start(bf16[64,768]{1,0:T(8,128)(2,1)S(1)} %collective-permute-done.6.refs_6_), channel_id=1, source_target_pairs={{0,4},{4,0},{8,12},{12,8},{16,20},{20,16},{24,28},{28,24},{1,5},{5... | collective-permute-start | bytes 294920 | tf_op jit(solution)/shard_map/ppermute | solution.py:257
  25.5 2.7 %collective-permute-start.9 = (bf16[512,768]{1,0:T(8,128)(2,1)S(1)}, bf16[512,768]{1,0:T(8,128)(2,1)S(1)}, u32[]{:S(2)}, u32[]{:S(2)}) collective-permute-start(bf16[512,768]{1,0:T(8,128)(2,1)S(1)} %copy-done), channel_id=1, source_target_pairs={{0,1},{1,0},{2,3},{3,2},{4,5},{5,4},{6,7},{7,6},{8,9},{9,8},{10,11... | collective-permute-start | bytes 2359304 | tf_op jit(solution)/shard_map/ppermute | solution.py:257
  26.1 3.4 %collective-permute-start.11 = (bf16[512,768]{1,0:T(8,128)(2,1)S(1)}, bf16[512,768]{1,0:T(8,128)(2,1)S(1)}, u32[]{:S(2)}, u32[]{:S(2)}) collective-permute-start(bf16[512,768]{1,0:T(8,128)(2,1)S(1)} %collective-permute-done.10.mine_ref), channel_id=1, source_target_pairs={{0,1},{1,0},{2,3},{3,2},{4,5},{5,4},{6,7},{7,6},{8,9},{9,8},{10,11... | collective-permute-start | bytes 2359304 | tf_op jit(solution)/shard_map/ppermute | solution.py:257
  27.7 3.3 %collective-permute-start.8 = (bf16[2,16,48,256]{3,2,1,0:T(8,128)(2,1)}, bf16[2,16,48,256]{3,2,1,0:T(8,128)(2,1)}, u32[]{:S(2)}, u32[]{:S(2)}) collective-permute-start(bf16[2,16,48,256]{3,2,1,0:T(8,128)(2,1)} %shard_map.30.mine_ref), channel_id=1, source_target_pairs={{0,1},{1,0},{2,3},{3,2},{4,5},{5,4},{6,7},{7,6},{8,9},{9,8},{10,11... | collective-permute-start | bytes 2359304 | tf_op jit(solution)/shard_map/ppermute | solution.py:257

commit v5 on v4

--- a/solution.py
+++ b/solution.py
@@ -296,14 +296,14 @@
         compiler_params=small,
         cost_estimate=pl.CostEstimate(flops=10**9, bytes_accessed=10**6, transcendentals=0),
     )(group[None], after(ref_list, own_pool))
-    pair = lax.dynamic_update_slice(after(pair, order), pool_x, (POOL, 0))
+    series_c = flip(after(series, own_pool), "tm", 1)
+    pair = lax.dynamic_update_slice(after(pair, order, series_c), pool_x, (POOL, 0))
     series_x = flip(after(series, pool_x, order), "tm", 2)
     along_z = [pair, flip(pair, "chan", 2), flip(pair, "chan", 4)]
     along_z.append(flip(along_z[2], "chan", 2))
     pool = []
     for piece in along_z:
         pool += [piece, flip(piece, "chan", 1)]
-    series_c = flip(after(series, *pool), "tm", 1)
 
     def phases(mine, other):
         return pl.pallas_call(
@@ -328,7 +328,7 @@
         out_shape=jax.ShapeDtypeStruct((2, PH, time_len // PH, refs), BF16),
         compiler_params=small,
         cost_estimate=pl.CostEstimate(flops=8 * 10**8, bytes_accessed=10**6, transcendentals=0),
-    )(order, *pool)
+    )(after(order, halves[0]), *pool)
     placed_c = flip(placed, "tm", 1)
     windows = total // WIN
     out = pl.pallas_call(

time: 52.1 us -> 50.9 us (0.977)
  Pallas kernels: 28.4 us -> 26.1 us
  waiting for transfers between devices: 6.91 us -> 7.95 us
    pallas_call x1, Pallas kernels: 20.9 us -> 19.5 us  [block_shards(): pl.pallas_call(functools.partial(corr_kernel, windows=windows, scale=1.0...]
    ppermute x12, waiting for transfers between devices: 6.91 us -> 7.95 us  [flip(): lax.ppermute(array, axis, [(i, i ^ by) for i in range(lax.axis_size(axis))])]
    pallas_call x1, Pallas kernels: 1.52 us -> 0.61 us  [block_shards(): pl.pallas_call(refs_kernel, in_specs=[vmem] * (1 + len(pool)), out_specs=...]
  transfers between devices with their start and end apart: 12 -> 12, of which waited for: 7 -> 4; matrix products, arithmetic and copies ran while one was open for 0% -> 0% of each run, Pallas kernels for 10% -> 8%
where the time goes in v5:
time: 50.9 us; the launch traced here: 50.7 us
  Pallas kernels  26.1 us (51%)
  starting transfers between devices  15.8 us (31%)
  waiting for transfers between devices  7.95 us (16%)
  local copies, waits for them, and re-layouts  0.71 us (1%)
    pallas_call x1, Pallas kernels, block_shards(): pl.pallas_call(functools.partial(corr_kernel, windows=windows, scale=1.0...  19.5 us
    ppermute x12, starting transfers between devices, flip(): lax.ppermute(array, axis, [(i, i ^ by) for i in range(lax.axis_size(axis))])  15.8 us
    ppermute x12, waiting for transfers between devices, flip(): lax.ppermute(array, axis, [(i, i ^ by) for i in range(lax.axis_size(axis))])  7.95 us
    pallas_call x2, Pallas kernels, phases(): pl.pallas_call(series_kernel, in_specs=[smem, hbm, hbm], out_specs=vmem,...  2.78 us
    pallas_call x1, Pallas kernels, block_shards(): pl.pallas_call(select_kernel, in_specs=[smem, hbm, hbm], out_specs=[vmem,...  2.42 us
  transfers between devices with their start and end apart: 12, of which 4 were waited for; matrix products, arithmetic and copies ran while one was open for 0% of the time, Pallas kernels for 8%

profile of v5, /device:TPU:0, one launch (start us, length us, event | category | flops | bytes accessed | tf_op | source)
XLA Modules:
  0.0 50.7 jit_solution(11562604399031033676)
XLA Ops:
  0.0 0.0 copy-start
  0.0 2.4 %shard_map.28 = (bf16[32,768]{1,0:T(8,128)(2,1)}, bf16[64,768]{1,0:T(8,128)(2,1)}) custom-call(s32[1]{0:T(128)} %bitcast.1.group_ref, s32[8,256]{1,0:T(8,128)} %list_ref, bf16[512,768]{1,0:T(8,128)(2,1)} %mine_ref.1), custom_call_target="tpu_custom_call" | custom-call | tf_op jit(solution)/shard_map/pallas_call | solution.py:277
  2.4 0.5 %collective-permute-start = (bf16[512,768]{1,0:T(8,128)(2,1)}, bf16[512,768]{1,0:T(8,128)(2,1)S(1)}, u32[]{:S(2)}, u32[]{:S(2)}) collective-permute-start(bf16[512,768]{1,0:T(8,128)(2,1)} %mine_ref.1), channel_id=1, source_target_pairs={{0,1},{1,0},{2,3},{3,2},{4,5},{5,4},{6,7},{7,6},{8,9},{9,8},{10,11... | collective-permute-start | bytes 2359304 | tf_op jit(solution)/shard_map/ppermute | solution.py:257
  2.9 2.6 %collective-permute-start.1 = (bf16[32,768]{1,0:T(8,128)(2,1)}, bf16[32,768]{1,0:T(8,128)(2,1)S(1)}, u32[]{:S(2)}, u32[]{:S(2)}) collective-permute-start(bf16[32,768]{1,0:T(8,128)(2,1)} %get-tuple-element.13), channel_id=1, source_target_pairs={{0,2},{1,3},{2,0},{3,1},{4,6},{5,7},{6,4},{7,5},{8,10},{9,11},{10,... | collective-permute-start | bytes 147464 | tf_op jit(solution)/shard_map/ppermute | solution.py:257
  5.5 0.0 copy-start.1
  5.5 0.7 %copy-done.1 = s32[8,256]{1,0:T(8,128)S(1)} copy-done((s32[8,256]{1,0:T(8,128)S(1)}, s32[8,256]{1,0:T(8,128)}, u32[]{:S(2)}) %copy-start.1) | copy-done | bytes 8216
  6.2 0.0 copy-start.2
  6.2 0.8 %shard_map.29.order_ref = bf16[256,256]{1,0:T(8,128)(2,1)S(1)} custom-call(s32[1]{0:T(128)} %bitcast.1.group_ref, s32[8,256]{1,0:T(8,128)S(1)} %copy-done.1), custom_call_target="tpu_custom_call" | custom-call | flops 1000000000 | bytes 1000000 | tf_op jit(solution)/shard_map/pallas_call | solution.py:291
  7.0 1.1 %collective-permute-done.1 = bf16[32,768]{1,0:T(8,128)(2,1)S(1)} collective-permute-done((bf16[32,768]{1,0:T(8,128)(2,1)}, bf16[32,768]{1,0:T(8,128)(2,1)S(1)}, u32[]{:S(2)}, u32[]{:S(2)}) %collective-permute-start.1) | collective-permute-done | bytes 49184 | tf_op jit(solution)/shard_map/ppermute | solution.py:257
  8.1 0.0 copy-done
  8.1 1.8 %collective-permute-start.10 = (bf16[512,768]{1,0:T(8,128)(2,1)S(1)}, bf16[512,768]{1,0:T(8,128)(2,1)S(1)}, u32[]{:S(2)}, u32[]{:S(2)}) collective-permute-start(bf16[512,768]{1,0:T(8,128)(2,1)S(1)} %copy-done), channel_id=1, source_target_pairs={{0,2},{1,3},{2,0},{3,1},{4,6},{5,7},{6,4},{7,5},{8,10},{9,11},{10,... | collective-permute-start | bytes 2359304 | tf_op jit(solution)/shard_map/ppermute | solution.py:257
  9.8 0.0 collective-permute-done.other_ref
  9.8 0.0 copy-done.2
  9.8 2.7 %collective-permute-start.5 = (bf16[64,768]{1,0:T(8,128)(2,1)S(1)}, bf16[64,768]{1,0:T(8,128)(2,1)S(1)}, u32[]{:S(2)}, u32[]{:S(2)}) collective-permute-start(bf16[64,768]{1,0:T(8,128)(2,1)S(1)} %constant_dynamic-update-slice_fusion.refs_0_), channel_id=1, source_target_pairs={{0,16},{4,20},{8,24},{12,28},{16,0},{20,4},{24,8},{28,12},{1,17},{... | collective-permute-start | bytes 294920 | tf_op jit(solution)/shard_map/ppermute | solution.py:257
  12.5 1.6 %collective-permute-start.3 = (bf16[64,768]{1,0:T(8,128)(2,1)S(1)}, bf16[64,768]{1,0:T(8,128)(2,1)S(1)}, u32[]{:S(2)}, u32[]{:S(2)}) collective-permute-start(bf16[64,768]{1,0:T(8,128)(2,1)S(1)} %constant_dynamic-update-slice_fusion.refs_0_), channel_id=1, source_target_pairs={{0,8},{4,12},{8,0},{12,4},{16,24},{20,28},{24,16},{28,20},{1,9},{5... | collective-permute-start | bytes 294920 | tf_op jit(solution)/shard_map/ppermute | solution.py:257
  14.1 1.6 %collective-permute-done.5.refs_4_ = bf16[64,768]{1,0:T(8,128)(2,1)S(1)} collective-permute-done((bf16[64,768]{1,0:T(8,128)(2,1)S(1)}, bf16[64,768]{1,0:T(8,128)(2,1)S(1)}, u32[]{:S(2)}, u32[]{:S(2)}) %collective-permute-start.5) | collective-permute-done | bytes 98336 | tf_op jit(solution)/shard_map/ppermute | solution.py:257
  15.7 1.6 %collective-permute-start.7 = (bf16[64,768]{1,0:T(8,128)(2,1)S(1)}, bf16[64,768]{1,0:T(8,128)(2,1)S(1)}, u32[]{:S(2)}, u32[]{:S(2)}) collective-permute-start(bf16[64,768]{1,0:T(8,128)(2,1)S(1)} %collective-permute-done.5.refs_4_), channel_id=1, source_target_pairs={{0,8},{4,12},{8,0},{12,4},{16,24},{20,28},{24,16},{28,20},{1,9},{5... | collective-permute-start | bytes 294920 | tf_op jit(solution)/shard_map/ppermute | solution.py:257
  17.3 1.5 %collective-permute-start.2 = (bf16[64,768]{1,0:T(8,128)(2,1)S(1)}, bf16[64,768]{1,0:T(8,128)(2,1)S(1)}, u32[]{:S(2)}, u32[]{:S(2)}) collective-permute-start(bf16[64,768]{1,0:T(8,128)(2,1)S(1)} %constant_dynamic-update-slice_fusion.refs_0_), channel_id=1, source_target_pairs={{0,4},{4,0},{8,12},{12,8},{16,20},{20,16},{24,28},{28,24},{1,5},{5... | collective-permute-start | bytes 294920 | tf_op jit(solution)/shard_map/ppermute | solution.py:257
  18.8 0.5 collective-permute-start.6
  19.3 0.0 collective-permute-done.3.refs_2_
  19.3 1.5 %collective-permute-start.4 = (bf16[64,768]{1,0:T(8,128)(2,1)S(1)}, bf16[64,768]{1,0:T(8,128)(2,1)S(1)}, u32[]{:S(2)}, u32[]{:S(2)}) collective-permute-start(bf16[64,768]{1,0:T(8,128)(2,1)S(1)} %collective-permute-done.3.refs_2_), channel_id=1, source_target_pairs={{0,4},{4,0},{8,12},{12,8},{16,20},{20,16},{24,28},{28,24},{1,5},{5... | collective-permute-start | bytes 294920 | tf_op jit(solution)/shard_map/ppermute | solution.py:257
  20.8 0.0 collective-permute-done.7.refs_6_
  20.8 1.0 %collective-permute-start.8 = (bf16[64,768]{1,0:T(8,128)(2,1)S(1)}, bf16[64,768]{1,0:T(8,128)(2,1)S(1)}, u32[]{:S(2)}, u32[]{:S(2)}) collective-permute-start(bf16[64,768]{1,0:T(8,128)(2,1)S(1)} %collective-permute-done.7.refs_6_), channel_id=1, source_target_pairs={{0,4},{4,0},{8,12},{12,8},{16,20},{20,16},{24,28},{28,24},{1,5},{5... | collective-permute-start | bytes 294920 | tf_op jit(solution)/shard_map/ppermute | solution.py:257
  21.8 1.4 %shard_map.30.refs_0_ = bf16[9,512,384]{2,1,0:T(8,128)(2,1)S(1)} custom-call(s32[1]{0:T(128)} %bitcast.2.core_ref, bf16[512,768]{1,0:T(8,128)(2,1)S(1)} %copy-done, bf16[512,768]{1,0:T(8,128)(2,1)S(1)} %collective-permute-done.other_ref), custom_call_target="tpu_custom_call" | custom-call | flops 1000 | bytes 1000 | tf_op jit(solution)/shard_map/pallas_call | solution.py:309
  23.2 4.1 %collective-permute-done.10.mine_ref = bf16[512,768]{1,0:T(8,128)(2,1)S(1)} collective-permute-done((bf16[512,768]{1,0:T(8,128)(2,1)S(1)}, bf16[512,768]{1,0:T(8,128)(2,1)S(1)}, u32[]{:S(2)}, u32[]{:S(2)}) %collective-permute-start.10) | collective-permute-done | bytes 786464 | tf_op jit(solution)/shard_map/ppermute | solution.py:257
  27.4 0.0 collective-permute-done.2.refs_1_
  27.4 0.0 collective-permute-done.6.refs_5_
  27.4 0.0 collective-permute-done.4.refs_3_
  27.4 0.0 collective-permute-done.8.refs_7_
  27.4 0.1 collective-permute-start.11
  27.5 0.6 %shard_map.31.mine_ref = bf16[2,16,48,256]{3,2,1,0:T(8,128)(2,1)S(1)} custom-call(bf16[256,256]{1,0:T(8,128)(2,1)S(1)} %shard_map.29.order_ref, bf16[64,768]{1,0:T(8,128)(2,1)S(1)} %constant_dynamic-update-slice_fusion.refs_0_, bf16[64,768]{1,0:T(8,128)(2,1)S(1)} %collective-permute-done.2.refs_1_, bf16[64,768]{1,0:T(8,128)(2,1)S(1)} %collective-permute-done.3.refs_2_, ...), custom_call_target="tpu_custom_call" | custom-call | flops 800000000 | bytes 1000000 | tf_op jit(solution)/shard_map/pallas_call | solution.py:324
  28.1 0.6 %collective-permute-start.9 = (bf16[2,16,48,256]{3,2,1,0:T(8,128)(2,1)S(1)}, bf16[2,16,48,256]{3,2,1,0:T(8,128)(2,1)S(1)}, u32[]{:S(2)}, u32[]{:S(2)}) collective-permute-start(bf16[2,16,48,256]{3,2,1,0:T(8,128)(2,1)S(1)} %shard_map.31.mine_ref), channel_id=1, source_target_pairs={{0,1},{1,0},{2,3},{3,2},{4,5},{5,4},{6,7},{7,6},{8,9},{9,8},{10,11... | collective-permute-start | bytes 2359304 | tf_op jit(solution)/shard_map/ppermute | solution.py:257
  28.6 1.1 %collective-permute-done.11.other_ref = bf16[512,768]{1,0:T(8,128)(2,1)S(1)} collective-permute-done((bf16[512,768]{1,0:T(8,128)(2,1)S(1)}, bf16[512,768]{1,0:T(8,128)(2,1)S(1)}, u32[]{:S(2)}, u32[]{:S(2)}) %collective-permute-start.11) | collective-permute-done | bytes 786464 | tf_op jit(solution)/shard_map/ppermute | solution.py:257
  29.7 1.4 %shard_map.32.refs_1_ = bf16[9,512,384]{2,1,0:T(8,128)(2,1)S(1)} custom-call(s32[1]{0:T(128)} %bitcast.2.core_ref, bf16[512,768]{1,0:T(8,128)(2,1)S(1)} %collective-permute-done.10.mine_ref, bf16[512,768]{1,0:T(8,128)(2,1)S(1)} %collective-permute-done.11.other_ref), custom_call_target="tpu_custom_call" | custom-call | flops 1000 | bytes 1000 | tf_op jit(solution)/shard_map/pallas_call | solution.py:309
  31.1 0.0 collective-permute-done.9.other_ref
  31.1 19.5 %shard_map.33 = bf16[2,4,4,512,256]{4,3,2,1,0:T(8,128)(2,1)} custom-call(s32[1]{0:T(128)} %bitcast.tm_ref, bf16[2,16,48,256]{3,2,1,0:T(8,128)(2,1)S(1)} %shard_map.31.mine_ref, bf16[2,16,48,256]{3,2,1,0:T(8,128)(2,1)S(1)} %collective-permute-done.9.other_ref, bf16[9,512,384]{2,1,0:T(8,128)(2,1)S(1)} %shard_map.30.refs_0_, ...), custom_call_target="tpu_custom_call" | custom-call | flops 15000000512 | bytes 20000000 | tf_op jit(solution)/shard_map/pallas_call | solution.py:334
  (1 shorter events, 0.0 us)
Async XLA Ops:
  0.0 8.1 %copy-start = (bf16[512,768]{1,0:T(8,128)(2,1)S(1)}, bf16[512,768]{1,0:T(8,128)(2,1)}, u32[]{:S(2)}) copy-start(bf16[512,768]{1,0:T(8,128)(2,1)} %mine_ref.1) | copy-start | bytes 2359300
  2.4 7.4 %collective-permute-start = (bf16[512,768]{1,0:T(8,128)(2,1)}, bf16[512,768]{1,0:T(8,128)(2,1)S(1)}, u32[]{:S(2)}, u32[]{:S(2)}) collective-permute-start(bf16[512,768]{1,0:T(8,128)(2,1)} %mine_ref.1), channel_id=1, source_target_pairs={{0,1},{1,0},{2,3},{3,2},{4,5},{5,4},{6,7},{7,6},{8,9},{9,8},{10,11... | collective-permute-start | bytes 2359304 | tf_op jit(solution)/shard_map/ppermute | solution.py:257
  2.9 5.1 %collective-permute-start.1 = (bf16[32,768]{1,0:T(8,128)(2,1)}, bf16[32,768]{1,0:T(8,128)(2,1)S(1)}, u32[]{:S(2)}, u32[]{:S(2)}) collective-permute-start(bf16[32,768]{1,0:T(8,128)(2,1)} %get-tuple-element.13), channel_id=1, source_target_pairs={{0,2},{1,3},{2,0},{3,1},{4,6},{5,7},{6,4},{7,5},{8,10},{9,11},{10,... | collective-permute-start | bytes 147464 | tf_op jit(solution)/shard_map/ppermute | solution.py:257
  5.5 0.7 %copy-start.1 = (s32[8,256]{1,0:T(8,128)S(1)}, s32[8,256]{1,0:T(8,128)}, u32[]{:S(2)}) copy-start(s32[8,256]{1,0:T(8,128)} %list_ref) | copy-start | bytes 24580
  6.2 3.6 %copy-start.2 = (bf16[64,768]{1,0:T(8,128)(2,1)S(1)}, bf16[64,768]{1,0:T(8,128)(2,1)}, u32[]{:S(2)}) copy-start(bf16[64,768]{1,0:T(8,128)(2,1)} %get-tuple-element.18) | copy-start | bytes 294916
  8.1 19.3 %collective-permute-start.10 = (bf16[512,768]{1,0:T(8,128)(2,1)S(1)}, bf16[512,768]{1,0:T(8,128)(2,1)S(1)}, u32[]{:S(2)}, u32[]{:S(2)}) collective-permute-start(bf16[512,768]{1,0:T(8,128)(2,1)S(1)} %copy-done), channel_id=1, source_target_pairs={{0,2},{1,3},{2,0},{3,1},{4,6},{5,7},{6,4},{7,5},{8,10},{9,11},{10,... | collective-permute-start | bytes 2359304 | tf_op jit(solution)/shard_map/ppermute | solution.py:257
  9.8 5.8 %collective-permute-start.5 = (bf16[64,768]{1,0:T(8,128)(2,1)S(1)}, bf16[64,768]{1,0:T(8,128)(2,1)S(1)}, u32[]{:S(2)}, u32[]{:S(2)}) collective-permute-start(bf16[64,768]{1,0:T(8,128)(2,1)S(1)} %constant_dynamic-update-slice_fusion.refs_0_), channel_id=1, source_target_pairs={{0,16},{4,20},{8,24},{12,28},{16,0},{20,4},{24,8},{28,12},{1,17},{... | collective-permute-start | bytes 294920 | tf_op jit(solution)/shard_map/ppermute | solution.py:257
  12.5 6.8 %collective-permute-start.3 = (bf16[64,768]{1,0:T(8,128)(2,1)S(1)}, bf16[64,768]{1,0:T(8,128)(2,1)S(1)}, u32[]{:S(2)}, u32[]{:S(2)}) collective-permute-start(bf16[64,768]{1,0:T(8,128)(2,1)S(1)} %constant_dynamic-update-slice_fusion.refs_0_), channel_id=1, source_target_pairs={{0,8},{4,12},{8,0},{12,4},{16,24},{20,28},{24,16},{28,20},{1,9},{5... | collective-permute-start | bytes 294920 | tf_op jit(solution)/shard_map/ppermute | solution.py:257
  15.7 5.2 %collective-permute-start.7 = (bf16[64,768]{1,0:T(8,128)(2,1)S(1)}, bf16[64,768]{1,0:T(8,128)(2,1)S(1)}, u32[]{:S(2)}, u32[]{:S(2)}) collective-permute-start(bf16[64,768]{1,0:T(8,128)(2,1)S(1)} %collective-permute-done.5.refs_4_), channel_id=1, source_target_pairs={{0,8},{4,12},{8,0},{12,4},{16,24},{20,28},{24,16},{28,20},{1,9},{5... | collective-permute-start | bytes 294920 | tf_op jit(solution)/shard_map/ppermute | solution.py:257
  17.3 10.1 %collective-permute-start.2 = (bf16[64,768]{1,0:T(8,128)(2,1)S(1)}, bf16[64,768]{1,0:T(8,128)(2,1)S(1)}, u32[]{:S(2)}, u32[]{:S(2)}) collective-permute-start(bf16[64,768]{1,0:T(8,128)(2,1)S(1)} %constant_dynamic-update-slice_fusion.refs_0_), channel_id=1, source_target_pairs={{0,4},{4,0},{8,12},{12,8},{16,20},{20,16},{24,28},{28,24},{1,5},{5... | collective-permute-start | bytes 294920 | tf_op jit(solution)/shard_map/ppermute | solution.py:257
  18.8 8.6 %collective-permute-start.6 = (bf16[64,768]{1,0:T(8,128)(2,1)S(1)}, bf16[64,768]{1,0:T(8,128)(2,1)S(1)}, u32[]{:S(2)}, u32[]{:S(2)}) collective-permute-start(bf16[64,768]{1,0:T(8,128)(2,1)S(1)} %collective-permute-done.5.refs_4_), channel_id=1, source_target_pairs={{0,4},{4,0},{8,12},{12,8},{16,20},{20,16},{24,28},{28,24},{1,5},{5... | collective-permute-start | bytes 294920 | tf_op jit(solution)/shard_map/ppermute | solution.py:257
  19.3 8.1 %collective-permute-start.4 = (bf16[64,768]{1,0:T(8,128)(2,1)S(1)}, bf16[64,768]{1,0:T(8,128)(2,1)S(1)}, u32[]{:S(2)}, u32[]{:S(2)}) collective-permute-start(bf16[64,768]{1,0:T(8,128)(2,1)S(1)} %collective-permute-done.3.refs_2_), channel_id=1, source_target_pairs={{0,4},{4,0},{8,12},{12,8},{16,20},{20,16},{24,28},{28,24},{1,5},{5... | collective-permute-start | bytes 294920 | tf_op jit(solution)/shard_map/ppermute | solution.py:257
  20.8 6.5 %collective-permute-start.8 = (bf16[64,768]{1,0:T(8,128)(2,1)S(1)}, bf16[64,768]{1,0:T(8,128)(2,1)S(1)}, u32[]{:S(2)}, u32[]{:S(2)}) collective-permute-start(bf16[64,768]{1,0:T(8,128)(2,1)S(1)} %collective-permute-done.7.refs_6_), channel_id=1, source_target_pairs={{0,4},{4,0},{8,12},{12,8},{16,20},{20,16},{24,28},{28,24},{1,5},{5... | collective-permute-start | bytes 294920 | tf_op jit(solution)/shard_map/ppermute | solution.py:257
  27.4 2.4 %collective-permute-start.11 = (bf16[512,768]{1,0:T(8,128)(2,1)S(1)}, bf16[512,768]{1,0:T(8,128)(2,1)S(1)}, u32[]{:S(2)}, u32[]{:S(2)}) collective-permute-start(bf16[512,768]{1,0:T(8,128)(2,1)S(1)} %collective-permute-done.10.mine_ref), channel_id=1, source_target_pairs={{0,1},{1,0},{2,3},{3,2},{4,5},{5,4},{6,7},{7,6},{8,9},{9,8},{10,11... | collective-permute-start | bytes 2359304 | tf_op jit(solution)/shard_map/ppermute | solution.py:257
  28.1 3.1 %collective-permute-start.9 = (bf16[2,16,48,256]{3,2,1,0:T(8,128)(2,1)S(1)}, bf16[2,16,48,256]{3,2,1,0:T(8,128)(2,1)S(1)}, u32[]{:S(2)}, u32[]{:S(2)}) collective-permute-start(bf16[2,16,48,256]{3,2,1,0:T(8,128)(2,1)S(1)} %shard_map.31.mine_ref), channel_id=1, source_target_pairs={{0,1},{1,0},{2,3},{3,2},{4,5},{5,4},{6,7},{7,6},{8,9},{9,8},{10,11... | collective-permute-start | bytes 2359304 | tf_op jit(solution)/shard_map/ppermute | solution.py:257

commit v6 on v5

--- a/solution.py
+++ b/solution.py
@@ -174,52 +174,54 @@
             out_ref[x, p, 16 * b : 16 * (b + 1), :] = placed[256 * i + 16 * p : 256 * i + 16 * (p + 1)]
 
 
-def corr_kernel(tm_ref, mine_ref, other_ref, *refs, windows, scale):
-    halves = refs[:2]
-    out_ref, xf, xr, rv0, rv1 = refs[2:]
+def slab(idx):
+    return pl.ds(pl.multiple_of(idx * PER, PER), PER)
+
+
+def make(xr, idx, rv, base, which, windows_of):
+    for b in windows_of:
+        x0, x4, x8, x12 = (xr[b, slab(idx + o), :] for o in (0, 4, 8, 12))
+        f0 = x4 - x0
+        if 0 in which:
+            rv[0, b, slab(idx - base), :] = f0
+        if 1 in which:
+            rv[1, b, slab(idx - base), :] = x8 - x0
+        rv[2, b, slab(idx - base), :] = (x12 - x8) - f0
+
+
+def lag_kernel(tm_ref, mine_ref, other_ref, xr, rv0, xf):
     me = tm_ref[0]
+    windows = xr.shape[0]
     half_w = windows // 2
+    block_rows = mine_ref.shape[2]
+    for h in range(2):
+        lanes = slice(128 * h, 128 * h + 128)
+        for p in range(PH):
+            xf[h, p, 0:8, :] = jnp.zeros((8, 128), F32)
+            for c, ref in enumerate((mine_ref, other_ref)):
+                for x in range(2):
+                    row = pl.multiple_of(8 + block_rows * (me ^ (c + 2 * x)), 8)
+                    xf[h, p, pl.ds(row, block_rows), :] = ref[x, p, :, lanes].astype(F32)
+
+    @pl.loop(0, 47)
+    def _(idx):
+        k = idx - 31
+        for b in range(windows):
+            half = (me >> 1) ^ (b // half_w)
+            row = 8 + PER * (half_w * half + b % half_w) + (k >> 4) - 2 * me
+            for h in range(2):
+                xr[b, slab(idx), 128 * h : 128 * h + 128] = xf[h, k & 15, pl.ds(row, PER), :].astype(BF16)
+
+    for low, high, which in ((24, 35, (0, 1)), (20, 24, (1,)), (16, 20, ())):
+
+        @pl.loop(low, high)
+        def _(idx):
+            make(xr, idx, rv0, 16, which, range(windows))
+
+
+def corr_kernel(xr, rv0, *refs, windows, scale):
+    *halves, out_ref, rv1 = refs
     step = pl.program_id(0)
-
-    def slab(idx):
-        return pl.ds(pl.multiple_of(idx * PER, PER), PER)
-
-    def make(idx, rv, base, which, windows_of):
-        for b in windows_of:
-            x0, x4, x8, x12 = (xr[b, slab(idx + o), :] for o in (0, 4, 8, 12))
-            f0 = x4 - x0
-            if 0 in which:
-                rv[0, b, slab(idx - base), :] = f0
-            if 1 in which:
-                rv[1, b, slab(idx - base), :] = x8 - x0
-            rv[2, b, slab(idx - base), :] = (x12 - x8) - f0
-
-    @pl.when(step == 0)
-    def _():
-        block_rows = mine_ref.shape[2]
-        for h in range(2):
-            lanes = slice(128 * h, 128 * h + 128)
-            for p in range(PH):
-                xf[h, p, 0:8, :] = jnp.zeros((8, 128), F32)
-                for c, ref in enumerate((mine_ref, other_ref)):
-                    for x in range(2):
-                        row = pl.multiple_of(8 + block_rows * (me ^ (c + 2 * x)), 8)
-                        xf[h, p, pl.ds(row, block_rows), :] = ref[x, p, :, lanes].astype(F32)
-
-        @pl.loop(0, 47)
-        def _(idx):
-            k = idx - 31
-            for b in range(windows):
-                half = (me >> 1) ^ (b // half_w)
-                row = 8 + PER * (half_w * half + b % half_w) + (k >> 4) - 2 * me
-                for h in range(2):
-                    xr[b, slab(idx), 128 * h : 128 * h + 128] = xf[h, k & 15, pl.ds(row, PER), :].astype(BF16)
-
-        for low, high, which in ((24, 35, (0, 1)), (20, 24, (1,)), (16, 20, ())):
-
-            @pl.loop(low, high)
-            def _(idx):
-                make(idx, rv0, 16, which, range(windows))
 
     def products(rv, beside):
         first = 15 - (step & 3)
@@ -244,7 +246,7 @@
     def _():
         def beside(i):
             for n in range(i, 5 * windows, 9):
-                make(jnp.maximum(18 - 5 * step - n // windows, 0), rv1, 0, (0, 1), (n % windows,))
+                make(xr, jnp.maximum(18 - 5 * step - n // windows, 0), rv1, 0, (0, 1), (n % windows,))
 
         products(rv0, beside)
 
@@ -285,7 +287,7 @@
             pltpu.VMEM((groups * chan_rows // 128, 128), F32),
             pltpu.SemaphoreType.DMA((2,)),
         ],
-        compiler_params=pltpu.CompilerParams(vmem_limit_bytes=60 * 2**20),
+        compiler_params=pltpu.CompilerParams(vmem_limit_bytes=48 * 2**20),
     )(group[None], ref_list, series)
     pool_x = flip(own_pool, "tm", 2)
     order = pl.pallas_call(
@@ -319,8 +321,6 @@
         )((me & 1)[None], mine, other)
 
     first_half = phases(series, series_c)
-    series_xc = flip(after(series_x, *pool), "tm", 1)
-    halves = [first_half, phases(series_x, series_xc)]
     placed = pl.pallas_call(
         refs_kernel,
         in_specs=[vmem] * (1 + len(pool)),
@@ -328,24 +328,33 @@
         out_shape=jax.ShapeDtypeStruct((2, PH, time_len // PH, refs), BF16),
         compiler_params=small,
         cost_estimate=pl.CostEstimate(flops=8 * 10**8, bytes_accessed=10**6, transcendentals=0),
-    )(after(order, halves[0]), *pool)
+    )(after(order, first_half), *pool)
     placed_c = flip(placed, "tm", 1)
+    series_xc = flip(after(series_x, placed), "tm", 1)
     windows = total // WIN
+    shifted_refs, differences = pl.pallas_call(
+        lag_kernel,
+        in_specs=[smem, vmem, vmem],
+        out_specs=[vmem] * 2,
+        out_shape=[
+            jax.ShapeDtypeStruct((windows, 47 * PER, refs), BF16),
+            jax.ShapeDtypeStruct((3, windows, 19 * PER, refs), BF16),
+        ],
+        scratch_shapes=[pltpu.VMEM((2, PH, total // PH + 16, 128), F32)],
+        compiler_params=pltpu.CompilerParams(vmem_limit_bytes=16 * 2**20),
+        cost_estimate=pl.CostEstimate(flops=1000, bytes_accessed=1000, transcendentals=0),
+    )(me[None], placed, placed_c)
+    halves = [first_half, phases(after(series_x, shifted_refs), series_xc)]
     out = pl.pallas_call(
         functools.partial(corr_kernel, windows=windows, scale=1.0 / math.sqrt(total)),
         grid=(8,),
-        in_specs=[smem] + [vmem] * 4,
+        in_specs=[vmem] * 4,
         out_specs=pl.BlockSpec((1, 4, 1, chan_rows, refs), lambda i: (i // 4, 0, i % 4, 0, 0)),
         out_shape=jax.ShapeDtypeStruct((2, 4, 4, chan_rows, refs), BF16),
-        scratch_shapes=[
-            pltpu.VMEM((2, PH, total // PH + 8, 128), F32),
-            pltpu.VMEM((windows, 47 * PER, refs), BF16),
-            pltpu.VMEM((3, windows, 19 * PER, refs), BF16),
-            pltpu.VMEM((3, windows, 19 * PER, refs), BF16),
-        ],
-        compiler_params=pltpu.CompilerParams(vmem_limit_bytes=40 * 2**20),
+        scratch_shapes=[pltpu.VMEM((3, windows, 19 * PER, refs), BF16)],
+        compiler_params=pltpu.CompilerParams(vmem_limit_bytes=28 * 2**20),
         cost_estimate=pl.CostEstimate(flops=15 * 10**9, bytes_accessed=2 * 10**7, transcendentals=0),
-    )(me[None], placed, placed_c, *halves)
+    )(shifted_refs, differences, *halves)
     return out.reshape(lags_dev, chan_rows, refs)
 
 

time: 50.9 us -> 49.8 us (0.978)
    pallas_call x1, Pallas kernels: 19.5 us -> 17.6 us  [block_shards(): pl.pallas_call(functools.partial(corr_kernel, windows=windows, scale=1.0...]
    pallas_call x0 -> x1, Pallas kernels: none -> 1.81 us  [block_shards(): pl.pallas_call(lag_kernel, in_specs=[smem, vmem, vmem], out_specs=[vmem]...]
    pallas_call x1, Pallas kernels: 2.42 us -> 1.48 us  [block_shards(): pl.pallas_call(select_kernel, in_specs=[smem, hbm, hbm], out_specs=[vmem,...]
    pallas_call x2, Pallas kernels: 2.78 us -> 3.67 us  [phases(): pl.pallas_call(series_kernel, in_specs=[smem, hbm, hbm], out_specs=vmem,...]
    ppermute x12, starting transfers between devices: 15.8 us -> 15.3 us  [flip(): lax.ppermute(array, axis, [(i, i ^ by) for i in range(lax.axis_size(axis))])]
  transfers between devices with their start and end apart: 12 -> 12, of which waited for: 4 -> 6; matrix products, arithmetic and copies ran while one was open for 0% -> 0% of each run, Pallas kernels for 8% -> 11%
where the time goes in v6:
time: 49.8 us; the launch traced here: 49.6 us
  Pallas kernels  25.9 us (52%)
  starting transfers between devices  15.3 us (31%)
  waiting for transfers between devices  7.59 us (15%)
  local copies, waits for them, and re-layouts  0.7 us (1%)
    pallas_call x1, Pallas kernels, block_shards(): pl.pallas_call(functools.partial(corr_kernel, windows=windows, scale=1.0...  17.6 us
    ppermute x12, starting transfers between devices, flip(): lax.ppermute(array, axis, [(i, i ^ by) for i in range(lax.axis_size(axis))])  15.3 us
    ppermute x12, waiting for transfers between devices, flip(): lax.ppermute(array, axis, [(i, i ^ by) for i in range(lax.axis_size(axis))])  7.59 us
    pallas_call x2, Pallas kernels, phases(): pl.pallas_call(series_kernel, in_specs=[smem, hbm, hbm], out_specs=vmem,...  3.67 us
    pallas_call x1, Pallas kernels, block_shards(): pl.pallas_call(lag_kernel, in_specs=[smem, vmem, vmem], out_specs=[vmem]...  1.81 us
    pallas_call x1, Pallas kernels, block_shards(): pl.pallas_call(select_kernel, in_specs=[smem, hbm, hbm], out_specs=[vmem,...  1.48 us
  transfers between devices with their start and end apart: 12, of which 6 were waited for; matrix products, arithmetic and copies ran while one was open for 0% of the time, Pallas kernels for 11%

profile of v6, /device:TPU:0, one launch (start us, length us, event | category | flops | bytes accessed | tf_op | source)
XLA Modules:
  0.0 49.6 jit_solution(17263919550123103736)
XLA Ops:
  0.0 0.0 copy-start
  0.0 0.7 %copy-done = s32[8,256]{1,0:T(8,128)S(1)} copy-done((s32[8,256]{1,0:T(8,128)S(1)}, s32[8,256]{1,0:T(8,128)}, u32[]{:S(2)}) %copy-start) | copy-done | bytes 8216
  0.7 1.5 %shard_map.28 = (bf16[32,768]{1,0:T(8,128)(2,1)S(1)}, bf16[64,768]{1,0:T(8,128)(2,1)S(1)}) custom-call(s32[1]{0:T(128)} %bitcast.1.group_ref, s32[8,256]{1,0:T(8,128)S(1)} %copy-done, bf16[512,768]{1,0:T(8,128)(2,1)} %mine_ref.1), custom_call_target="tpu_custom_call" | custom-call | tf_op jit(solution)/shard_map/pallas_call | solution.py:279
  2.2 0.5 %collective-permute-start = (bf16[512,768]{1,0:T(8,128)(2,1)}, bf16[512,768]{1,0:T(8,128)(2,1)S(1)}, u32[]{:S(2)}, u32[]{:S(2)}) collective-permute-start(bf16[512,768]{1,0:T(8,128)(2,1)} %mine_ref.1), channel_id=1, source_target_pairs={{0,1},{1,0},{2,3},{3,2},{4,5},{5,4},{6,7},{7,6},{8,9},{9,8},{10,11... | collective-permute-start | bytes 2359304 | tf_op jit(solution)/shard_map/ppermute | solution.py:259
  2.7 2.6 %collective-permute-start.1 = (bf16[32,768]{1,0:T(8,128)(2,1)S(1)}, bf16[32,768]{1,0:T(8,128)(2,1)S(1)}, u32[]{:S(2)}, u32[]{:S(2)}) collective-permute-start(bf16[32,768]{1,0:T(8,128)(2,1)S(1)} %get-tuple-element.16), channel_id=1, source_target_pairs={{0,2},{1,3},{2,0},{3,1},{4,6},{5,7},{6,4},{7,5},{8,10},{9,11},{10,... | collective-permute-start | bytes 147464 | tf_op jit(solution)/shard_map/ppermute | solution.py:259
  5.3 0.8 %shard_map.29.order_ref = bf16[256,256]{1,0:T(8,128)(2,1)S(1)} custom-call(s32[1]{0:T(128)} %bitcast.1.group_ref, s32[8,256]{1,0:T(8,128)S(1)} %copy-done), custom_call_target="tpu_custom_call" | custom-call | flops 1000000000 | bytes 1000000 | tf_op jit(solution)/shard_map/pallas_call | solution.py:293
  6.0 1.6 %collective-permute-done.1 = bf16[32,768]{1,0:T(8,128)(2,1)S(1)} collective-permute-done((bf16[32,768]{1,0:T(8,128)(2,1)S(1)}, bf16[32,768]{1,0:T(8,128)(2,1)S(1)}, u32[]{:S(2)}, u32[]{:S(2)}) %collective-permute-start.1) | collective-permute-done | bytes 49184 | tf_op jit(solution)/shard_map/ppermute | solution.py:259
  7.6 1.8 %collective-permute-start.10 = (bf16[512,768]{1,0:T(8,128)(2,1)}, bf16[512,768]{1,0:T(8,128)(2,1)S(1)}, u32[]{:S(2)}, u32[]{:S(2)}) collective-permute-start(bf16[512,768]{1,0:T(8,128)(2,1)} %mine_ref.1), channel_id=1, source_target_pairs={{0,2},{1,3},{2,0},{3,1},{4,6},{5,7},{6,4},{7,5},{8,10},{9,11},{10,... | collective-permute-start | bytes 2359304 | tf_op jit(solution)/shard_map/ppermute | solution.py:259
  9.4 0.0 collective-permute-done.other_ref
  9.4 2.6 %collective-permute-start.5 = (bf16[64,768]{1,0:T(8,128)(2,1)S(1)}, bf16[64,768]{1,0:T(8,128)(2,1)S(1)}, u32[]{:S(2)}, u32[]{:S(2)}) collective-permute-start(bf16[64,768]{1,0:T(8,128)(2,1)S(1)} %constant_dynamic-update-slice_fusion.refs_0_), channel_id=1, source_target_pairs={{0,16},{4,20},{8,24},{12,28},{16,0},{20,4},{24,8},{28,12},{1,17},{... | collective-permute-start | bytes 294920 | tf_op jit(solution)/shard_map/ppermute | solution.py:259
  12.0 1.6 %collective-permute-start.3 = (bf16[64,768]{1,0:T(8,128)(2,1)S(1)}, bf16[64,768]{1,0:T(8,128)(2,1)S(1)}, u32[]{:S(2)}, u32[]{:S(2)}) collective-permute-start(bf16[64,768]{1,0:T(8,128)(2,1)S(1)} %constant_dynamic-update-slice_fusion.refs_0_), channel_id=1, source_target_pairs={{0,8},{4,12},{8,0},{12,4},{16,24},{20,28},{24,16},{28,20},{1,9},{5... | collective-permute-start | bytes 294920 | tf_op jit(solution)/shard_map/ppermute | solution.py:259
  13.6 1.6 %collective-permute-done.5.refs_4_ = bf16[64,768]{1,0:T(8,128)(2,1)S(1)} collective-permute-done((bf16[64,768]{1,0:T(8,128)(2,1)S(1)}, bf16[64,768]{1,0:T(8,128)(2,1)S(1)}, u32[]{:S(2)}, u32[]{:S(2)}) %collective-permute-start.5) | collective-permute-done | bytes 98336 | tf_op jit(solution)/shard_map/ppermute | solution.py:259
  15.2 1.6 %collective-permute-start.7 = (bf16[64,768]{1,0:T(8,128)(2,1)S(1)}, bf16[64,768]{1,0:T(8,128)(2,1)S(1)}, u32[]{:S(2)}, u32[]{:S(2)}) collective-permute-start(bf16[64,768]{1,0:T(8,128)(2,1)S(1)} %collective-permute-done.5.refs_4_), channel_id=1, source_target_pairs={{0,8},{4,12},{8,0},{12,4},{16,24},{20,28},{24,16},{28,20},{1,9},{5... | collective-permute-start | bytes 294920 | tf_op jit(solution)/shard_map/ppermute | solution.py:259
  16.8 1.5 %collective-permute-start.2 = (bf16[64,768]{1,0:T(8,128)(2,1)S(1)}, bf16[64,768]{1,0:T(8,128)(2,1)S(1)}, u32[]{:S(2)}, u32[]{:S(2)}) collective-permute-start(bf16[64,768]{1,0:T(8,128)(2,1)S(1)} %constant_dynamic-update-slice_fusion.refs_0_), channel_id=1, source_target_pairs={{0,4},{4,0},{8,12},{12,8},{16,20},{20,16},{24,28},{28,24},{1,5},{5... | collective-permute-start | bytes 294920 | tf_op jit(solution)/shard_map/ppermute | solution.py:259
  18.3 0.5 %collective-permute-start.6 = (bf16[64,768]{1,0:T(8,128)(2,1)S(1)}, bf16[64,768]{1,0:T(8,128)(2,1)S(1)}, u32[]{:S(2)}, u32[]{:S(2)}) collective-permute-start(bf16[64,768]{1,0:T(8,128)(2,1)S(1)} %collective-permute-done.5.refs_4_), channel_id=1, source_target_pairs={{0,4},{4,0},{8,12},{12,8},{16,20},{20,16},{24,28},{28,24},{1,5},{5... | collective-permute-start | bytes 294920 | tf_op jit(solution)/shard_map/ppermute | solution.py:259
  18.8 0.0 collective-permute-done.3.refs_2_
  18.8 1.5 %collective-permute-start.4 = (bf16[64,768]{1,0:T(8,128)(2,1)S(1)}, bf16[64,768]{1,0:T(8,128)(2,1)S(1)}, u32[]{:S(2)}, u32[]{:S(2)}) collective-permute-start(bf16[64,768]{1,0:T(8,128)(2,1)S(1)} %collective-permute-done.3.refs_2_), channel_id=1, source_target_pairs={{0,4},{4,0},{8,12},{12,8},{16,20},{20,16},{24,28},{28,24},{1,5},{5... | collective-permute-start | bytes 294920 | tf_op jit(solution)/shard_map/ppermute | solution.py:259
  20.4 0.0 collective-permute-done.7.refs_6_
  20.4 1.0 %collective-permute-start.8 = (bf16[64,768]{1,0:T(8,128)(2,1)S(1)}, bf16[64,768]{1,0:T(8,128)(2,1)S(1)}, u32[]{:S(2)}, u32[]{:S(2)}) collective-permute-start(bf16[64,768]{1,0:T(8,128)(2,1)S(1)} %collective-permute-done.7.refs_6_), channel_id=1, source_target_pairs={{0,4},{4,0},{8,12},{12,8},{16,20},{20,16},{24,28},{28,24},{1,5},{5... | collective-permute-start | bytes 294920 | tf_op jit(solution)/shard_map/ppermute | solution.py:259
  21.3 2.3 %shard_map.30.refs_0_ = bf16[9,512,384]{2,1,0:T(8,128)(2,1)S(1)} custom-call(s32[1]{0:T(128)} %bitcast.2.core_ref, bf16[512,768]{1,0:T(8,128)(2,1)} %mine_ref.1, bf16[512,768]{1,0:T(8,128)(2,1)S(1)} %collective-permute-done.other_ref), custom_call_target="tpu_custom_call" | custom-call | flops 1000 | bytes 1000 | tf_op jit(solution)/shard_map/pallas_call | solution.py:311
  23.6 0.0 collective-permute-done.2.refs_1_
  23.6 0.0 collective-permute-done.6.refs_5_
  23.6 1.1 %collective-permute-done.4.refs_3_ = bf16[64,768]{1,0:T(8,128)(2,1)S(1)} collective-permute-done((bf16[64,768]{1,0:T(8,128)(2,1)S(1)}, bf16[64,768]{1,0:T(8,128)(2,1)S(1)}, u32[]{:S(2)}, u32[]{:S(2)}) %collective-permute-start.4) | collective-permute-done | bytes 98336 | tf_op jit(solution)/shard_map/ppermute | solution.py:259
  24.7 1.1 %collective-permute-done.8.refs_7_ = bf16[64,768]{1,0:T(8,128)(2,1)S(1)} collective-permute-done((bf16[64,768]{1,0:T(8,128)(2,1)S(1)}, bf16[64,768]{1,0:T(8,128)(2,1)S(1)}, u32[]{:S(2)}, u32[]{:S(2)}) %collective-permute-start.8) | collective-permute-done | bytes 98336 | tf_op jit(solution)/shard_map/ppermute | solution.py:259
  25.8 0.6 %shard_map.31.mine_ref = bf16[2,16,48,256]{3,2,1,0:T(8,128)(2,1)S(1)} custom-call(bf16[256,256]{1,0:T(8,128)(2,1)S(1)} %shard_map.29.order_ref, bf16[64,768]{1,0:T(8,128)(2,1)S(1)} %constant_dynamic-update-slice_fusion.refs_0_, bf16[64,768]{1,0:T(8,128)(2,1)S(1)} %collective-permute-done.2.refs_1_, bf16[64,768]{1,0:T(8,128)(2,1)S(1)} %collective-permute-done.3.refs_2_, ...), custom_call_target="tpu_custom_call" | custom-call | flops 800000000 | bytes 1000000 | tf_op jit(solution)/shard_map/pallas_call | solution.py:324
  26.4 0.1 collective-permute-start.9
  26.4 0.7 %collective-permute-done.10.mine_ref = bf16[512,768]{1,0:T(8,128)(2,1)S(1)} collective-permute-done((bf16[512,768]{1,0:T(8,128)(2,1)}, bf16[512,768]{1,0:T(8,128)(2,1)S(1)}, u32[]{:S(2)}, u32[]{:S(2)}) %collective-permute-start.10) | collective-permute-done | bytes 786464 | tf_op jit(solution)/shard_map/ppermute | solution.py:259
  27.1 0.0 collective-permute-start.11
  27.1 1.6 %collective-permute-done.9.other_ref = bf16[2,16,48,256]{3,2,1,0:T(8,128)(2,1)S(1)} collective-permute-done((bf16[2,16,48,256]{3,2,1,0:T(8,128)(2,1)S(1)}, bf16[2,16,48,256]{3,2,1,0:T(8,128)(2,1)S(1)}, u32[]{:S(2)}, u32[]{:S(2)}) %collective-permute-start.9) | collective-permute-done | bytes 786464 | tf_op jit(solution)/shard_map/ppermute | solution.py:259
  28.7 1.8 %shard_map.32 = (bf16[6,1504,256]{2,1,0:T(8,128)(2,1)S(1)}, bf16[3,6,608,256]{3,2,1,0:T(8,128)(2,1)S(1)}) custom-call(s32[1]{0:T(128)} %bitcast.tm_ref, bf16[2,16,48,256]{3,2,1,0:T(8,128)(2,1)S(1)} %shard_map.31.mine_ref, bf16[2,16,48,256]{3,2,1,0:T(8,128)(2,1)S(1)} %collective-permute-done.9.other_ref), custom_call_target="tpu_custom_call" | custom-call | flops 1000 | bytes 1000 | tf_op jit(solution)/shard_map/pallas_call | solution.py:335
  30.5 0.0 collective-permute-done.11.other_ref
  30.5 1.4 %shard_map.33.refs_1_ = bf16[9,512,384]{2,1,0:T(8,128)(2,1)S(1)} custom-call(s32[1]{0:T(128)} %bitcast.2.core_ref, bf16[512,768]{1,0:T(8,128)(2,1)S(1)} %collective-permute-done.10.mine_ref, bf16[512,768]{1,0:T(8,128)(2,1)S(1)} %collective-permute-done.11.other_ref), custom_call_target="tpu_custom_call" | custom-call | flops 1000 | bytes 1000 | tf_op jit(solution)/shard_map/pallas_call | solution.py:311
  31.9 17.6 %shard_map.34 = bf16[2,4,4,512,256]{4,3,2,1,0:T(8,128)(2,1)} custom-call(bf16[6,1504,256]{2,1,0:T(8,128)(2,1)S(1)} %get-tuple-element.22.xr, bf16[3,6,608,256]{3,2,1,0:T(8,128)(2,1)S(1)} %get-tuple-element.23.rv0, bf16[9,512,384]{2,1,0:T(8,128)(2,1)S(1)} %shard_map.30.refs_0_, bf16[9,512,384]{2,1,0:T(8,128)(2,1)S(1)} %shard_map.33.refs_1_), custom_call_target="tpu_custom_call" | custom-call | flops 15000000512 | bytes 20000000 | tf_op jit(solution)/shard_map/pallas_call | solution.py:348
  (1 shorter events, 0.0 us)
Async XLA Ops:
  0.0 0.7 %copy-start = (s32[8,256]{1,0:T(8,128)S(1)}, s32[8,256]{1,0:T(8,128)}, u32[]{:S(2)}) copy-start(s32[8,256]{1,0:T(8,128)} %list_ref) | copy-start | bytes 24580
  2.2 7.2 %collective-permute-start = (bf16[512,768]{1,0:T(8,128)(2,1)}, bf16[512,768]{1,0:T(8,128)(2,1)S(1)}, u32[]{:S(2)}, u32[]{:S(2)}) collective-permute-start(bf16[512,768]{1,0:T(8,128)(2,1)} %mine_ref.1), channel_id=1, source_target_pairs={{0,1},{1,0},{2,3},{3,2},{4,5},{5,4},{6,7},{7,6},{8,9},{9,8},{10,11... | collective-permute-start | bytes 2359304 | tf_op jit(solution)/shard_map/ppermute | solution.py:259
  2.7 4.9 %collective-permute-start.1 = (bf16[32,768]{1,0:T(8,128)(2,1)S(1)}, bf16[32,768]{1,0:T(8,128)(2,1)S(1)}, u32[]{:S(2)}, u32[]{:S(2)}) collective-permute-start(bf16[32,768]{1,0:T(8,128)(2,1)S(1)} %get-tuple-element.16), channel_id=1, source_target_pairs={{0,2},{1,3},{2,0},{3,1},{4,6},{5,7},{6,4},{7,5},{8,10},{9,11},{10,... | collective-permute-start | bytes 147464 | tf_op jit(solution)/shard_map/ppermute | solution.py:259
  7.6 19.5 %collective-permute-start.10 = (bf16[512,768]{1,0:T(8,128)(2,1)}, bf16[512,768]{1,0:T(8,128)(2,1)S(1)}, u32[]{:S(2)}, u32[]{:S(2)}) collective-permute-start(bf16[512,768]{1,0:T(8,128)(2,1)} %mine_ref.1), channel_id=1, source_target_pairs={{0,2},{1,3},{2,0},{3,1},{4,6},{5,7},{6,4},{7,5},{8,10},{9,11},{10,... | collective-permute-start | bytes 2359304 | tf_op jit(solution)/shard_map/ppermute | solution.py:259
  9.4 5.8 %collective-permute-start.5 = (bf16[64,768]{1,0:T(8,128)(2,1)S(1)}, bf16[64,768]{1,0:T(8,128)(2,1)S(1)}, u32[]{:S(2)}, u32[]{:S(2)}) collective-permute-start(bf16[64,768]{1,0:T(8,128)(2,1)S(1)} %constant_dynamic-update-slice_fusion.refs_0_), channel_id=1, source_target_pairs={{0,16},{4,20},{8,24},{12,28},{16,0},{20,4},{24,8},{28,12},{1,17},{... | collective-permute-start | bytes 294920 | tf_op jit(solution)/shard_map/ppermute | solution.py:259
  12.0 6.8 %collective-permute-start.3 = (bf16[64,768]{1,0:T(8,128)(2,1)S(1)}, bf16[64,768]{1,0:T(8,128)(2,1)S(1)}, u32[]{:S(2)}, u32[]{:S(2)}) collective-permute-start(bf16[64,768]{1,0:T(8,128)(2,1)S(1)} %constant_dynamic-update-slice_fusion.refs_0_), channel_id=1, source_target_pairs={{0,8},{4,12},{8,0},{12,4},{16,24},{20,28},{24,16},{28,20},{1,9},{5... | collective-permute-start | bytes 294920 | tf_op jit(solution)/shard_map/ppermute | solution.py:259
  15.2 5.2 %collective-permute-start.7 = (bf16[64,768]{1,0:T(8,128)(2,1)S(1)}, bf16[64,768]{1,0:T(8,128)(2,1)S(1)}, u32[]{:S(2)}, u32[]{:S(2)}) collective-permute-start(bf16[64,768]{1,0:T(8,128)(2,1)S(1)} %collective-permute-done.5.refs_4_), channel_id=1, source_target_pairs={{0,8},{4,12},{8,0},{12,4},{16,24},{20,28},{24,16},{28,20},{1,9},{5... | collective-permute-start | bytes 294920 | tf_op jit(solution)/shard_map/ppermute | solution.py:259
  16.8 6.8 %collective-permute-start.2 = (bf16[64,768]{1,0:T(8,128)(2,1)S(1)}, bf16[64,768]{1,0:T(8,128)(2,1)S(1)}, u32[]{:S(2)}, u32[]{:S(2)}) collective-permute-start(bf16[64,768]{1,0:T(8,128)(2,1)S(1)} %constant_dynamic-update-slice_fusion.refs_0_), channel_id=1, source_target_pairs={{0,4},{4,0},{8,12},{12,8},{16,20},{20,16},{24,28},{28,24},{1,5},{5... | collective-permute-start | bytes 294920 | tf_op jit(solution)/shard_map/ppermute | solution.py:259
  18.3 5.3 %collective-permute-start.6 = (bf16[64,768]{1,0:T(8,128)(2,1)S(1)}, bf16[64,768]{1,0:T(8,128)(2,1)S(1)}, u32[]{:S(2)}, u32[]{:S(2)}) collective-permute-start(bf16[64,768]{1,0:T(8,128)(2,1)S(1)} %collective-permute-done.5.refs_4_), channel_id=1, source_target_pairs={{0,4},{4,0},{8,12},{12,8},{16,20},{20,16},{24,28},{28,24},{1,5},{5... | collective-permute-start | bytes 294920 | tf_op jit(solution)/shard_map/ppermute | solution.py:259
  18.8 5.9 %collective-permute-start.4 = (bf16[64,768]{1,0:T(8,128)(2,1)S(1)}, bf16[64,768]{1,0:T(8,128)(2,1)S(1)}, u32[]{:S(2)}, u32[]{:S(2)}) collective-permute-start(bf16[64,768]{1,0:T(8,128)(2,1)S(1)} %collective-permute-done.3.refs_2_), channel_id=1, source_target_pairs={{0,4},{4,0},{8,12},{12,8},{16,20},{20,16},{24,28},{28,24},{1,5},{5... | collective-permute-start | bytes 294920 | tf_op jit(solution)/shard_map/ppermute | solution.py:259
  20.4 5.4 %collective-permute-start.8 = (bf16[64,768]{1,0:T(8,128)(2,1)S(1)}, bf16[64,768]{1,0:T(8,128)(2,1)S(1)}, u32[]{:S(2)}, u32[]{:S(2)}) collective-permute-start(bf16[64,768]{1,0:T(8,128)(2,1)S(1)} %collective-permute-done.7.refs_6_), channel_id=1, source_target_pairs={{0,4},{4,0},{8,12},{12,8},{16,20},{20,16},{24,28},{28,24},{1,5},{5... | collective-permute-start | bytes 294920 | tf_op jit(solution)/shard_map/ppermute | solution.py:259
  26.4 2.4 %collective-permute-start.9 = (bf16[2,16,48,256]{3,2,1,0:T(8,128)(2,1)S(1)}, bf16[2,16,48,256]{3,2,1,0:T(8,128)(2,1)S(1)}, u32[]{:S(2)}, u32[]{:S(2)}) collective-permute-start(bf16[2,16,48,256]{3,2,1,0:T(8,128)(2,1)S(1)} %shard_map.31.mine_ref), channel_id=1, source_target_pairs={{0,1},{1,0},{2,3},{3,2},{4,5},{5,4},{6,7},{7,6},{8,9},{9,8},{10,11... | collective-permute-start | bytes 2359304 | tf_op jit(solution)/shard_map/ppermute | solution.py:259
  27.1 3.4 %collective-permute-start.11 = (bf16[512,768]{1,0:T(8,128)(2,1)S(1)}, bf16[512,768]{1,0:T(8,128)(2,1)S(1)}, u32[]{:S(2)}, u32[]{:S(2)}) collective-permute-start(bf16[512,768]{1,0:T(8,128)(2,1)S(1)} %collective-permute-done.10.mine_ref), channel_id=1, source_target_pairs={{0,1},{1,0},{2,3},{3,2},{4,5},{5,4},{6,7},{7,6},{8,9},{9,8},{10,11... | collective-permute-start | bytes 2359304 | tf_op jit(solution)/shard_map/ppermute | solution.py:259

commit v7 on v6

--- a/solution.py
+++ b/solution.py
@@ -203,7 +203,7 @@
                     row = pl.multiple_of(8 + block_rows * (me ^ (c + 2 * x)), 8)
                     xf[h, p, pl.ds(row, block_rows), :] = ref[x, p, :, lanes].astype(F32)
 
-    @pl.loop(0, 47)
+    @pl.loop(0, 47, unroll=True)
     def _(idx):
         k = idx - 31
         for b in range(windows):
@@ -214,7 +214,7 @@
 
     for low, high, which in ((24, 35, (0, 1)), (20, 24, (1,)), (16, 20, ())):
 
-        @pl.loop(low, high)
+        @pl.loop(low, high, unroll=True)
         def _(idx):
             make(xr, idx, rv0, 16, which, range(windows))
 

time: 49.8 us -> 49.2 us (0.988)
  Pallas kernels: 25.9 us -> 25.3 us
    pallas_call x1, Pallas kernels: 1.81 us -> 1.22 us  [block_shards(): pl.pallas_call(lag_kernel, in_specs=[smem, vmem, vmem], out_specs=[vmem]...]
  transfers between devices with their start and end apart: 12 -> 12, of which waited for: 6 -> 6; matrix products, arithmetic and copies ran while one was open for 0% -> 0% of each run, Pallas kernels for 11% -> 10%
where the time goes in v7:
time: 49.2 us; the launch traced here: 49 us
  Pallas kernels  25.3 us (51%)
  starting transfers between devices  15.3 us (31%)
  waiting for transfers between devices  7.59 us (15%)
  local copies, waits for them, and re-layouts  0.7 us (1%)
    pallas_call x1, Pallas kernels, block_shards(): pl.pallas_call(functools.partial(corr_kernel, windows=windows, scale=1.0...  17.6 us
    ppermute x12, starting transfers between devices, flip(): lax.ppermute(array, axis, [(i, i ^ by) for i in range(lax.axis_size(axis))])  15.3 us
    ppermute x12, waiting for transfers between devices, flip(): lax.ppermute(array, axis, [(i, i ^ by) for i in range(lax.axis_size(axis))])  7.59 us
    pallas_call x2, Pallas kernels, phases(): pl.pallas_call(series_kernel, in_specs=[smem, hbm, hbm], out_specs=vmem,...  3.67 us
    pallas_call x1, Pallas kernels, block_shards(): pl.pallas_call(select_kernel, in_specs=[smem, hbm, hbm], out_specs=[vmem,...  1.48 us
    pallas_call x1, Pallas kernels, block_shards(): pl.pallas_call(lag_kernel, in_specs=[smem, vmem, vmem], out_specs=[vmem]...  1.22 us
  transfers between devices with their start and end apart: 12, of which 6 were waited for; matrix products, arithmetic and copies ran while one was open for 0% of the time, Pallas kernels for 10%

profile of v7, /device:TPU:0, one launch (start us, length us, event | category | flops | bytes accessed | tf_op | source)
XLA Modules:
  0.0 49.0 jit_solution(18188590289969840625)
XLA Ops:
  0.0 0.0 copy-start
  0.0 0.7 %copy-done = s32[8,256]{1,0:T(8,128)S(1)} copy-done((s32[8,256]{1,0:T(8,128)S(1)}, s32[8,256]{1,0:T(8,128)}, u32[]{:S(2)}) %copy-start) | copy-done | bytes 8216
  0.7 1.5 %shard_map.28 = (bf16[32,768]{1,0:T(8,128)(2,1)S(1)}, bf16[64,768]{1,0:T(8,128)(2,1)S(1)}) custom-call(s32[1]{0:T(128)} %bitcast.1.group_ref, s32[8,256]{1,0:T(8,128)S(1)} %copy-done, bf16[512,768]{1,0:T(8,128)(2,1)} %mine_ref.1), custom_call_target="tpu_custom_call" | custom-call | tf_op jit(solution)/shard_map/pallas_call | solution.py:279
  2.2 0.5 %collective-permute-start = (bf16[512,768]{1,0:T(8,128)(2,1)}, bf16[512,768]{1,0:T(8,128)(2,1)S(1)}, u32[]{:S(2)}, u32[]{:S(2)}) collective-permute-start(bf16[512,768]{1,0:T(8,128)(2,1)} %mine_ref.1), channel_id=1, source_target_pairs={{0,1},{1,0},{2,3},{3,2},{4,5},{5,4},{6,7},{7,6},{8,9},{9,8},{10,11... | collective-permute-start | bytes 2359304 | tf_op jit(solution)/shard_map/ppermute | solution.py:259
  2.7 2.6 %collective-permute-start.1 = (bf16[32,768]{1,0:T(8,128)(2,1)S(1)}, bf16[32,768]{1,0:T(8,128)(2,1)S(1)}, u32[]{:S(2)}, u32[]{:S(2)}) collective-permute-start(bf16[32,768]{1,0:T(8,128)(2,1)S(1)} %get-tuple-element.16), channel_id=1, source_target_pairs={{0,2},{1,3},{2,0},{3,1},{4,6},{5,7},{6,4},{7,5},{8,10},{9,11},{10,... | collective-permute-start | bytes 147464 | tf_op jit(solution)/shard_map/ppermute | solution.py:259
  5.3 0.8 %shard_map.29.order_ref = bf16[256,256]{1,0:T(8,128)(2,1)S(1)} custom-call(s32[1]{0:T(128)} %bitcast.1.group_ref, s32[8,256]{1,0:T(8,128)S(1)} %copy-done), custom_call_target="tpu_custom_call" | custom-call | flops 1000000000 | bytes 1000000 | tf_op jit(solution)/shard_map/pallas_call | solution.py:293
  6.0 1.6 %collective-permute-done.1 = bf16[32,768]{1,0:T(8,128)(2,1)S(1)} collective-permute-done((bf16[32,768]{1,0:T(8,128)(2,1)S(1)}, bf16[32,768]{1,0:T(8,128)(2,1)S(1)}, u32[]{:S(2)}, u32[]{:S(2)}) %collective-permute-start.1) | collective-permute-done | bytes 49184 | tf_op jit(solution)/shard_map/ppermute | solution.py:259
  7.6 1.8 %collective-permute-start.10 = (bf16[512,768]{1,0:T(8,128)(2,1)}, bf16[512,768]{1,0:T(8,128)(2,1)S(1)}, u32[]{:S(2)}, u32[]{:S(2)}) collective-permute-start(bf16[512,768]{1,0:T(8,128)(2,1)} %mine_ref.1), channel_id=1, source_target_pairs={{0,2},{1,3},{2,0},{3,1},{4,6},{5,7},{6,4},{7,5},{8,10},{9,11},{10,... | collective-permute-start | bytes 2359304 | tf_op jit(solution)/shard_map/ppermute | solution.py:259
  9.4 0.0 collective-permute-done.other_ref
  9.4 2.6 %collective-permute-start.5 = (bf16[64,768]{1,0:T(8,128)(2,1)S(1)}, bf16[64,768]{1,0:T(8,128)(2,1)S(1)}, u32[]{:S(2)}, u32[]{:S(2)}) collective-permute-start(bf16[64,768]{1,0:T(8,128)(2,1)S(1)} %constant_dynamic-update-slice_fusion.refs_0_), channel_id=1, source_target_pairs={{0,16},{4,20},{8,24},{12,28},{16,0},{20,4},{24,8},{28,12},{1,17},{... | collective-permute-start | bytes 294920 | tf_op jit(solution)/shard_map/ppermute | solution.py:259
  12.0 1.6 %collective-permute-start.3 = (bf16[64,768]{1,0:T(8,128)(2,1)S(1)}, bf16[64,768]{1,0:T(8,128)(2,1)S(1)}, u32[]{:S(2)}, u32[]{:S(2)}) collective-permute-start(bf16[64,768]{1,0:T(8,128)(2,1)S(1)} %constant_dynamic-update-slice_fusion.refs_0_), channel_id=1, source_target_pairs={{0,8},{4,12},{8,0},{12,4},{16,24},{20,28},{24,16},{28,20},{1,9},{5... | collective-permute-start | bytes 294920 | tf_op jit(solution)/shard_map/ppermute | solution.py:259
  13.6 1.6 %collective-permute-done.5.refs_4_ = bf16[64,768]{1,0:T(8,128)(2,1)S(1)} collective-permute-done((bf16[64,768]{1,0:T(8,128)(2,1)S(1)}, bf16[64,768]{1,0:T(8,128)(2,1)S(1)}, u32[]{:S(2)}, u32[]{:S(2)}) %collective-permute-start.5) | collective-permute-done | bytes 98336 | tf_op jit(solution)/shard_map/ppermute | solution.py:259
  15.2 1.6 %collective-permute-start.7 = (bf16[64,768]{1,0:T(8,128)(2,1)S(1)}, bf16[64,768]{1,0:T(8,128)(2,1)S(1)}, u32[]{:S(2)}, u32[]{:S(2)}) collective-permute-start(bf16[64,768]{1,0:T(8,128)(2,1)S(1)} %collective-permute-done.5.refs_4_), channel_id=1, source_target_pairs={{0,8},{4,12},{8,0},{12,4},{16,24},{20,28},{24,16},{28,20},{1,9},{5... | collective-permute-start | bytes 294920 | tf_op jit(solution)/shard_map/ppermute | solution.py:259
  16.8 1.5 %collective-permute-start.2 = (bf16[64,768]{1,0:T(8,128)(2,1)S(1)}, bf16[64,768]{1,0:T(8,128)(2,1)S(1)}, u32[]{:S(2)}, u32[]{:S(2)}) collective-permute-start(bf16[64,768]{1,0:T(8,128)(2,1)S(1)} %constant_dynamic-update-slice_fusion.refs_0_), channel_id=1, source_target_pairs={{0,4},{4,0},{8,12},{12,8},{16,20},{20,16},{24,28},{28,24},{1,5},{5... | collective-permute-start | bytes 294920 | tf_op jit(solution)/shard_map/ppermute | solution.py:259
  18.3 0.5 %collective-permute-start.6 = (bf16[64,768]{1,0:T(8,128)(2,1)S(1)}, bf16[64,768]{1,0:T(8,128)(2,1)S(1)}, u32[]{:S(2)}, u32[]{:S(2)}) collective-permute-start(bf16[64,768]{1,0:T(8,128)(2,1)S(1)} %collective-permute-done.5.refs_4_), channel_id=1, source_target_pairs={{0,4},{4,0},{8,12},{12,8},{16,20},{20,16},{24,28},{28,24},{1,5},{5... | collective-permute-start | bytes 294920 | tf_op jit(solution)/shard_map/ppermute | solution.py:259
  18.8 0.0 collective-permute-done.3.refs_2_
  18.8 1.5 %collective-permute-start.4 = (bf16[64,768]{1,0:T(8,128)(2,1)S(1)}, bf16[64,768]{1,0:T(8,128)(2,1)S(1)}, u32[]{:S(2)}, u32[]{:S(2)}) collective-permute-start(bf16[64,768]{1,0:T(8,128)(2,1)S(1)} %collective-permute-done.3.refs_2_), channel_id=1, source_target_pairs={{0,4},{4,0},{8,12},{12,8},{16,20},{20,16},{24,28},{28,24},{1,5},{5... | collective-permute-start | bytes 294920 | tf_op jit(solution)/shard_map/ppermute | solution.py:259
  20.4 0.0 collective-permute-done.7.refs_6_
  20.4 1.0 %collective-permute-start.8 = (bf16[64,768]{1,0:T(8,128)(2,1)S(1)}, bf16[64,768]{1,0:T(8,128)(2,1)S(1)}, u32[]{:S(2)}, u32[]{:S(2)}) collective-permute-start(bf16[64,768]{1,0:T(8,128)(2,1)S(1)} %collective-permute-done.7.refs_6_), channel_id=1, source_target_pairs={{0,4},{4,0},{8,12},{12,8},{16,20},{20,16},{24,28},{28,24},{1,5},{5... | collective-permute-start | bytes 294920 | tf_op jit(solution)/shard_map/ppermute | solution.py:259
  21.3 2.3 %shard_map.30.refs_0_ = bf16[9,512,384]{2,1,0:T(8,128)(2,1)S(1)} custom-call(s32[1]{0:T(128)} %bitcast.2.core_ref, bf16[512,768]{1,0:T(8,128)(2,1)} %mine_ref.1, bf16[512,768]{1,0:T(8,128)(2,1)S(1)} %collective-permute-done.other_ref), custom_call_target="tpu_custom_call" | custom-call | flops 1000 | bytes 1000 | tf_op jit(solution)/shard_map/pallas_call | solution.py:311
  23.6 0.0 collective-permute-done.2.refs_1_
  23.6 0.0 collective-permute-done.6.refs_5_
  23.6 1.1 %collective-permute-done.4.refs_3_ = bf16[64,768]{1,0:T(8,128)(2,1)S(1)} collective-permute-done((bf16[64,768]{1,0:T(8,128)(2,1)S(1)}, bf16[64,768]{1,0:T(8,128)(2,1)S(1)}, u32[]{:S(2)}, u32[]{:S(2)}) %collective-permute-start.4) | collective-permute-done | bytes 98336 | tf_op jit(solution)/shard_map/ppermute | solution.py:259
  24.7 1.1 %collective-permute-done.8.refs_7_ = bf16[64,768]{1,0:T(8,128)(2,1)S(1)} collective-permute-done((bf16[64,768]{1,0:T(8,128)(2,1)S(1)}, bf16[64,768]{1,0:T(8,128)(2,1)S(1)}, u32[]{:S(2)}, u32[]{:S(2)}) %collective-permute-start.8) | collective-permute-done | bytes 98336 | tf_op jit(solution)/shard_map/ppermute | solution.py:259
  25.8 0.6 %shard_map.31.mine_ref = bf16[2,16,48,256]{3,2,1,0:T(8,128)(2,1)S(1)} custom-call(bf16[256,256]{1,0:T(8,128)(2,1)S(1)} %shard_map.29.order_ref, bf16[64,768]{1,0:T(8,128)(2,1)S(1)} %constant_dynamic-update-slice_fusion.refs_0_, bf16[64,768]{1,0:T(8,128)(2,1)S(1)} %collective-permute-done.2.refs_1_, bf16[64,768]{1,0:T(8,128)(2,1)S(1)} %collective-permute-done.3.refs_2_, ...), custom_call_target="tpu_custom_call" | custom-call | flops 800000000 | bytes 1000000 | tf_op jit(solution)/shard_map/pallas_call | solution.py:324
  26.4 0.1 collective-permute-start.9
  26.4 0.7 %collective-permute-done.10.mine_ref = bf16[512,768]{1,0:T(8,128)(2,1)S(1)} collective-permute-done((bf16[512,768]{1,0:T(8,128)(2,1)}, bf16[512,768]{1,0:T(8,128)(2,1)S(1)}, u32[]{:S(2)}, u32[]{:S(2)}) %collective-permute-start.10) | collective-permute-done | bytes 786464 | tf_op jit(solution)/shard_map/ppermute | solution.py:259
  27.1 0.0 collective-permute-start.11
  27.1 1.6 %collective-permute-done.9.other_ref = bf16[2,16,48,256]{3,2,1,0:T(8,128)(2,1)S(1)} collective-permute-done((bf16[2,16,48,256]{3,2,1,0:T(8,128)(2,1)S(1)}, bf16[2,16,48,256]{3,2,1,0:T(8,128)(2,1)S(1)}, u32[]{:S(2)}, u32[]{:S(2)}) %collective-permute-start.9) | collective-permute-done | bytes 786464 | tf_op jit(solution)/shard_map/ppermute | solution.py:259
  28.7 1.2 %shard_map.32 = (bf16[6,1504,256]{2,1,0:T(8,128)(2,1)S(1)}, bf16[3,6,608,256]{3,2,1,0:T(8,128)(2,1)S(1)}) custom-call(s32[1]{0:T(128)} %bitcast.tm_ref, bf16[2,16,48,256]{3,2,1,0:T(8,128)(2,1)S(1)} %shard_map.31.mine_ref, bf16[2,16,48,256]{3,2,1,0:T(8,128)(2,1)S(1)} %collective-permute-done.9.other_ref), custom_call_target="tpu_custom_call" | custom-call | flops 1000 | bytes 1000 | tf_op jit(solution)/shard_map/pallas_call | solution.py:335
  29.9 0.0 collective-permute-done.11.other_ref
  30.0 1.4 %shard_map.33.refs_1_ = bf16[9,512,384]{2,1,0:T(8,128)(2,1)S(1)} custom-call(s32[1]{0:T(128)} %bitcast.2.core_ref, bf16[512,768]{1,0:T(8,128)(2,1)S(1)} %collective-permute-done.10.mine_ref, bf16[512,768]{1,0:T(8,128)(2,1)S(1)} %collective-permute-done.11.other_ref), custom_call_target="tpu_custom_call" | custom-call | flops 1000 | bytes 1000 | tf_op jit(solution)/shard_map/pallas_call | solution.py:311
  31.4 17.6 %shard_map.34 = bf16[2,4,4,512,256]{4,3,2,1,0:T(8,128)(2,1)} custom-call(bf16[6,1504,256]{2,1,0:T(8,128)(2,1)S(1)} %get-tuple-element.22.xr, bf16[3,6,608,256]{3,2,1,0:T(8,128)(2,1)S(1)} %get-tuple-element.23.rv0, bf16[9,512,384]{2,1,0:T(8,128)(2,1)S(1)} %shard_map.30.refs_0_, bf16[9,512,384]{2,1,0:T(8,128)(2,1)S(1)} %shard_map.33.refs_1_), custom_call_target="tpu_custom_call" | custom-call | flops 15000000512 | bytes 20000000 | tf_op jit(solution)/shard_map/pallas_call | solution.py:348
  (1 shorter events, 0.0 us)
Async XLA Ops:
  0.0 0.7 %copy-start = (s32[8,256]{1,0:T(8,128)S(1)}, s32[8,256]{1,0:T(8,128)}, u32[]{:S(2)}) copy-start(s32[8,256]{1,0:T(8,128)} %list_ref) | copy-start | bytes 24580
  2.2 7.2 %collective-permute-start = (bf16[512,768]{1,0:T(8,128)(2,1)}, bf16[512,768]{1,0:T(8,128)(2,1)S(1)}, u32[]{:S(2)}, u32[]{:S(2)}) collective-permute-start(bf16[512,768]{1,0:T(8,128)(2,1)} %mine_ref.1), channel_id=1, source_target_pairs={{0,1},{1,0},{2,3},{3,2},{4,5},{5,4},{6,7},{7,6},{8,9},{9,8},{10,11... | collective-permute-start | bytes 2359304 | tf_op jit(solution)/shard_map/ppermute | solution.py:259
  2.7 4.9 %collective-permute-start.1 = (bf16[32,768]{1,0:T(8,128)(2,1)S(1)}, bf16[32,768]{1,0:T(8,128)(2,1)S(1)}, u32[]{:S(2)}, u32[]{:S(2)}) collective-permute-start(bf16[32,768]{1,0:T(8,128)(2,1)S(1)} %get-tuple-element.16), channel_id=1, source_target_pairs={{0,2},{1,3},{2,0},{3,1},{4,6},{5,7},{6,4},{7,5},{8,10},{9,11},{10,... | collective-permute-start | bytes 147464 | tf_op jit(solution)/shard_map/ppermute | solution.py:259
  7.6 19.5 %collective-permute-start.10 = (bf16[512,768]{1,0:T(8,128)(2,1)}, bf16[512,768]{1,0:T(8,128)(2,1)S(1)}, u32[]{:S(2)}, u32[]{:S(2)}) collective-permute-start(bf16[512,768]{1,0:T(8,128)(2,1)} %mine_ref.1), channel_id=1, source_target_pairs={{0,2},{1,3},{2,0},{3,1},{4,6},{5,7},{6,4},{7,5},{8,10},{9,11},{10,... | collective-permute-start | bytes 2359304 | tf_op jit(solution)/shard_map/ppermute | solution.py:259
  9.4 5.8 %collective-permute-start.5 = (bf16[64,768]{1,0:T(8,128)(2,1)S(1)}, bf16[64,768]{1,0:T(8,128)(2,1)S(1)}, u32[]{:S(2)}, u32[]{:S(2)}) collective-permute-start(bf16[64,768]{1,0:T(8,128)(2,1)S(1)} %constant_dynamic-update-slice_fusion.refs_0_), channel_id=1, source_target_pairs={{0,16},{4,20},{8,24},{12,28},{16,0},{20,4},{24,8},{28,12},{1,17},{... | collective-permute-start | bytes 294920 | tf_op jit(solution)/shard_map/ppermute | solution.py:259
  12.0 6.8 %collective-permute-start.3 = (bf16[64,768]{1,0:T(8,128)(2,1)S(1)}, bf16[64,768]{1,0:T(8,128)(2,1)S(1)}, u32[]{:S(2)}, u32[]{:S(2)}) collective-permute-start(bf16[64,768]{1,0:T(8,128)(2,1)S(1)} %constant_dynamic-update-slice_fusion.refs_0_), channel_id=1, source_target_pairs={{0,8},{4,12},{8,0},{12,4},{16,24},{20,28},{24,16},{28,20},{1,9},{5... | collective-permute-start | bytes 294920 | tf_op jit(solution)/shard_map/ppermute | solution.py:259
  15.2 5.2 %collective-permute-start.7 = (bf16[64,768]{1,0:T(8,128)(2,1)S(1)}, bf16[64,768]{1,0:T(8,128)(2,1)S(1)}, u32[]{:S(2)}, u32[]{:S(2)}) collective-permute-start(bf16[64,768]{1,0:T(8,128)(2,1)S(1)} %collective-permute-done.5.refs_4_), channel_id=1, source_target_pairs={{0,8},{4,12},{8,0},{12,4},{16,24},{20,28},{24,16},{28,20},{1,9},{5... | collective-permute-start | bytes 294920 | tf_op jit(solution)/shard_map/ppermute | solution.py:259
  16.8 6.8 %collective-permute-start.2 = (bf16[64,768]{1,0:T(8,128)(2,1)S(1)}, bf16[64,768]{1,0:T(8,128)(2,1)S(1)}, u32[]{:S(2)}, u32[]{:S(2)}) collective-permute-start(bf16[64,768]{1,0:T(8,128)(2,1)S(1)} %constant_dynamic-update-slice_fusion.refs_0_), channel_id=1, source_target_pairs={{0,4},{4,0},{8,12},{12,8},{16,20},{20,16},{24,28},{28,24},{1,5},{5... | collective-permute-start | bytes 294920 | tf_op jit(solution)/shard_map/ppermute | solution.py:259
  18.3 5.3 %collective-permute-start.6 = (bf16[64,768]{1,0:T(8,128)(2,1)S(1)}, bf16[64,768]{1,0:T(8,128)(2,1)S(1)}, u32[]{:S(2)}, u32[]{:S(2)}) collective-permute-start(bf16[64,768]{1,0:T(8,128)(2,1)S(1)} %collective-permute-done.5.refs_4_), channel_id=1, source_target_pairs={{0,4},{4,0},{8,12},{12,8},{16,20},{20,16},{24,28},{28,24},{1,5},{5... | collective-permute-start | bytes 294920 | tf_op jit(solution)/shard_map/ppermute | solution.py:259
  18.8 5.9 %collective-permute-start.4 = (bf16[64,768]{1,0:T(8,128)(2,1)S(1)}, bf16[64,768]{1,0:T(8,128)(2,1)S(1)}, u32[]{:S(2)}, u32[]{:S(2)}) collective-permute-start(bf16[64,768]{1,0:T(8,128)(2,1)S(1)} %collective-permute-done.3.refs_2_), channel_id=1, source_target_pairs={{0,4},{4,0},{8,12},{12,8},{16,20},{20,16},{24,28},{28,24},{1,5},{5... | collective-permute-start | bytes 294920 | tf_op jit(solution)/shard_map/ppermute | solution.py:259
  20.4 5.4 %collective-permute-start.8 = (bf16[64,768]{1,0:T(8,128)(2,1)S(1)}, bf16[64,768]{1,0:T(8,128)(2,1)S(1)}, u32[]{:S(2)}, u32[]{:S(2)}) collective-permute-start(bf16[64,768]{1,0:T(8,128)(2,1)S(1)} %collective-permute-done.7.refs_6_), channel_id=1, source_target_pairs={{0,4},{4,0},{8,12},{12,8},{16,20},{20,16},{24,28},{28,24},{1,5},{5... | collective-permute-start | bytes 294920 | tf_op jit(solution)/shard_map/ppermute | solution.py:259
  26.4 2.4 %collective-permute-start.9 = (bf16[2,16,48,256]{3,2,1,0:T(8,128)(2,1)S(1)}, bf16[2,16,48,256]{3,2,1,0:T(8,128)(2,1)S(1)}, u32[]{:S(2)}, u32[]{:S(2)}) collective-permute-start(bf16[2,16,48,256]{3,2,1,0:T(8,128)(2,1)S(1)} %shard_map.31.mine_ref), channel_id=1, source_target_pairs={{0,1},{1,0},{2,3},{3,2},{4,5},{5,4},{6,7},{7,6},{8,9},{9,8},{10,11... | collective-permute-start | bytes 2359304 | tf_op jit(solution)/shard_map/ppermute | solution.py:259
  27.1 2.8 %collective-permute-start.11 = (bf16[512,768]{1,0:T(8,128)(2,1)S(1)}, bf16[512,768]{1,0:T(8,128)(2,1)S(1)}, u32[]{:S(2)}, u32[]{:S(2)}) collective-permute-start(bf16[512,768]{1,0:T(8,128)(2,1)S(1)} %collective-permute-done.10.mine_ref), channel_id=1, source_target_pairs={{0,1},{1,0},{2,3},{3,2},{4,5},{5,4},{6,7},{7,6},{8,9},{9,8},{10,11... | collective-permute-start | bytes 2359304 | tf_op jit(solution)/shard_map/ppermute | solution.py:259

commit v8 on v7

--- a/solution.py
+++ b/solution.py
@@ -223,13 +223,14 @@
     *halves, out_ref, rv1 = refs
     step = pl.program_id(0)
 
-    def products(rv, beside):
-        first = 15 - (step & 3)
+    def products(rv, sub, beside):
+        lag = 2 * step + sub
+        first = 15 - (lag & 3)
 
         def product(i):
             v, off = COMBOS[i]
             if v == 0:
-                rows = pl.ds(pl.multiple_of((first + 16 - 16 * (step >> 2)) * PER, PER), 4 * PER)
+                rows = pl.ds(pl.multiple_of((first + 16 - 16 * (lag >> 2)) * PER, PER), 4 * PER)
                 parts = [xr[b, rows, :] for b in range(windows)]
             else:
                 rows = pl.ds(pl.multiple_of((first - off) * PER, PER), 4 * PER)
@@ -240,19 +241,21 @@
         p = [product(i) for i in range(9)]
         w0, w1 = p[0] + p[3], p[0] + p[6]
         for at, value in enumerate((w0 + (p[1] + p[4]), w0 + (p[2] + p[5]), w1 + (p[1] + p[7]), w1 + (p[2] + p[8]))):
-            out_ref[0, at, 0] = (scale * value).astype(BF16)
-
-    @pl.when(step < 4)
+            out_ref[0, at, sub] = (scale * value).astype(BF16)
+
+    @pl.when(step < 2)
     def _():
         def beside(i):
-            for n in range(i, 5 * windows, 9):
-                make(xr, jnp.maximum(18 - 5 * step - n // windows, 0), rv1, 0, (0, 1), (n % windows,))
-
-        products(rv0, beside)
-
-    @pl.when(step >= 4)
+            for n in range(i, 10 * windows, 18):
+                make(xr, jnp.maximum(18 - 10 * step - n // windows, 0), rv1, 0, (0, 1), (n % windows,))
+
+        products(rv0, 0, beside)
+        products(rv0, 1, lambda i: beside(i + 9))
+
+    @pl.when(step >= 2)
     def _():
-        products(rv1, lambda i: None)
+        products(rv1, 0, lambda i: None)
+        products(rv1, 1, lambda i: None)
 
 
 def flip(array, axis, by):
@@ -347,9 +350,9 @@
     halves = [first_half, phases(after(series_x, shifted_refs), series_xc)]
     out = pl.pallas_call(
         functools.partial(corr_kernel, windows=windows, scale=1.0 / math.sqrt(total)),
-        grid=(8,),
+        grid=(4,),
         in_specs=[vmem] * 4,
-        out_specs=pl.BlockSpec((1, 4, 1, chan_rows, refs), lambda i: (i // 4, 0, i % 4, 0, 0)),
+        out_specs=pl.BlockSpec((1, 4, 2, chan_rows, refs), lambda i: (i // 2, 0, i % 2, 0, 0)),
         out_shape=jax.ShapeDtypeStruct((2, 4, 4, chan_rows, refs), BF16),
         scratch_shapes=[pltpu.VMEM((3, windows, 19 * PER, refs), BF16)],
         compiler_params=pltpu.CompilerParams(vmem_limit_bytes=28 * 2**20),

time: 49.2 us -> 48.7 us (0.990)
  Pallas kernels: 25.3 us -> 24.8 us
    pallas_call x1, Pallas kernels: 17.6 us -> 17.1 us  [block_shards(): pl.pallas_call(functools.partial(corr_kernel, windows=windows, scale=1.0...]
where the time goes in v8:
time: 48.7 us; the launch traced here: 48.5 us
  Pallas kernels  24.8 us (51%)
  starting transfers between devices  15.3 us (31%)
  waiting for transfers between devices  7.59 us (16%)
  local copies, waits for them, and re-layouts  0.7 us (1%)
    pallas_call x1, Pallas kernels, block_shards(): pl.pallas_call(functools.partial(corr_kernel, windows=windows, scale=1.0...  17.1 us
    ppermute x12, starting transfers between devices, flip(): lax.ppermute(array, axis, [(i, i ^ by) for i in range(lax.axis_size(axis))])  15.3 us
    ppermute x12, waiting for transfers between devices, flip(): lax.ppermute(array, axis, [(i, i ^ by) for i in range(lax.axis_size(axis))])  7.59 us
    pallas_call x2, Pallas kernels, phases(): pl.pallas_call(series_kernel, in_specs=[smem, hbm, hbm], out_specs=vmem,...  3.67 us
    pallas_call x1, Pallas kernels, block_shards(): pl.pallas_call(select_kernel, in_specs=[smem, hbm, hbm], out_specs=[vmem,...  1.48 us
    pallas_call x1, Pallas kernels, block_shards(): pl.pallas_call(lag_kernel, in_specs=[smem, vmem, vmem], out_specs=[vmem]...  1.22 us
  transfers between devices with their start and end apart: 12, of which 6 were waited for; matrix products, arithmetic and copies ran while one was open for 0% of the time, Pallas kernels for 10%

profile of v8, /device:TPU:0, one launch (start us, length us, event | category | flops | bytes accessed | tf_op | source)
XLA Modules:
  0.0 48.5 jit_solution(83159079990972872)
XLA Ops:
  0.0 0.0 copy-start
  0.0 0.7 %copy-done = s32[8,256]{1,0:T(8,128)S(1)} copy-done((s32[8,256]{1,0:T(8,128)S(1)}, s32[8,256]{1,0:T(8,128)}, u32[]{:S(2)}) %copy-start) | copy-done | bytes 8216
  0.7 1.5 %shard_map.28 = (bf16[32,768]{1,0:T(8,128)(2,1)S(1)}, bf16[64,768]{1,0:T(8,128)(2,1)S(1)}) custom-call(s32[1]{0:T(128)} %bitcast.1.group_ref, s32[8,256]{1,0:T(8,128)S(1)} %copy-done, bf16[512,768]{1,0:T(8,128)(2,1)} %mine_ref.1), custom_call_target="tpu_custom_call" | custom-call | tf_op jit(solution)/shard_map/pallas_call | solution.py:282
  2.2 0.5 %collective-permute-start = (bf16[512,768]{1,0:T(8,128)(2,1)}, bf16[512,768]{1,0:T(8,128)(2,1)S(1)}, u32[]{:S(2)}, u32[]{:S(2)}) collective-permute-start(bf16[512,768]{1,0:T(8,128)(2,1)} %mine_ref.1), channel_id=1, source_target_pairs={{0,1},{1,0},{2,3},{3,2},{4,5},{5,4},{6,7},{7,6},{8,9},{9,8},{10,11... | collective-permute-start | bytes 2359304 | tf_op jit(solution)/shard_map/ppermute | solution.py:262
  2.7 2.6 %collective-permute-start.1 = (bf16[32,768]{1,0:T(8,128)(2,1)S(1)}, bf16[32,768]{1,0:T(8,128)(2,1)S(1)}, u32[]{:S(2)}, u32[]{:S(2)}) collective-permute-start(bf16[32,768]{1,0:T(8,128)(2,1)S(1)} %get-tuple-element.16), channel_id=1, source_target_pairs={{0,2},{1,3},{2,0},{3,1},{4,6},{5,7},{6,4},{7,5},{8,10},{9,11},{10,... | collective-permute-start | bytes 147464 | tf_op jit(solution)/shard_map/ppermute | solution.py:262
  5.3 0.8 %shard_map.29.order_ref = bf16[256,256]{1,0:T(8,128)(2,1)S(1)} custom-call(s32[1]{0:T(128)} %bitcast.1.group_ref, s32[8,256]{1,0:T(8,128)S(1)} %copy-done), custom_call_target="tpu_custom_call" | custom-call | flops 1000000000 | bytes 1000000 | tf_op jit(solution)/shard_map/pallas_call | solution.py:296
  6.0 1.6 %collective-permute-done.1 = bf16[32,768]{1,0:T(8,128)(2,1)S(1)} collective-permute-done((bf16[32,768]{1,0:T(8,128)(2,1)S(1)}, bf16[32,768]{1,0:T(8,128)(2,1)S(1)}, u32[]{:S(2)}, u32[]{:S(2)}) %collective-permute-start.1) | collective-permute-done | bytes 49184 | tf_op jit(solution)/shard_map/ppermute | solution.py:262
  7.6 1.8 %collective-permute-start.10 = (bf16[512,768]{1,0:T(8,128)(2,1)}, bf16[512,768]{1,0:T(8,128)(2,1)S(1)}, u32[]{:S(2)}, u32[]{:S(2)}) collective-permute-start(bf16[512,768]{1,0:T(8,128)(2,1)} %mine_ref.1), channel_id=1, source_target_pairs={{0,2},{1,3},{2,0},{3,1},{4,6},{5,7},{6,4},{7,5},{8,10},{9,11},{10,... | collective-permute-start | bytes 2359304 | tf_op jit(solution)/shard_map/ppermute | solution.py:262
  9.4 0.0 collective-permute-done.other_ref
  9.4 2.6 %collective-permute-start.5 = (bf16[64,768]{1,0:T(8,128)(2,1)S(1)}, bf16[64,768]{1,0:T(8,128)(2,1)S(1)}, u32[]{:S(2)}, u32[]{:S(2)}) collective-permute-start(bf16[64,768]{1,0:T(8,128)(2,1)S(1)} %constant_dynamic-update-slice_fusion.refs_0_), channel_id=1, source_target_pairs={{0,16},{4,20},{8,24},{12,28},{16,0},{20,4},{24,8},{28,12},{1,17},{... | collective-permute-start | bytes 294920 | tf_op jit(solution)/shard_map/ppermute | solution.py:262
  12.0 1.6 %collective-permute-start.3 = (bf16[64,768]{1,0:T(8,128)(2,1)S(1)}, bf16[64,768]{1,0:T(8,128)(2,1)S(1)}, u32[]{:S(2)}, u32[]{:S(2)}) collective-permute-start(bf16[64,768]{1,0:T(8,128)(2,1)S(1)} %constant_dynamic-update-slice_fusion.refs_0_), channel_id=1, source_target_pairs={{0,8},{4,12},{8,0},{12,4},{16,24},{20,28},{24,16},{28,20},{1,9},{5... | collective-permute-start | bytes 294920 | tf_op jit(solution)/shard_map/ppermute | solution.py:262
  13.6 1.6 %collective-permute-done.5.refs_4_ = bf16[64,768]{1,0:T(8,128)(2,1)S(1)} collective-permute-done((bf16[64,768]{1,0:T(8,128)(2,1)S(1)}, bf16[64,768]{1,0:T(8,128)(2,1)S(1)}, u32[]{:S(2)}, u32[]{:S(2)}) %collective-permute-start.5) | collective-permute-done | bytes 98336 | tf_op jit(solution)/shard_map/ppermute | solution.py:262
  15.2 1.6 %collective-permute-start.7 = (bf16[64,768]{1,0:T(8,128)(2,1)S(1)}, bf16[64,768]{1,0:T(8,128)(2,1)S(1)}, u32[]{:S(2)}, u32[]{:S(2)}) collective-permute-start(bf16[64,768]{1,0:T(8,128)(2,1)S(1)} %collective-permute-done.5.refs_4_), channel_id=1, source_target_pairs={{0,8},{4,12},{8,0},{12,4},{16,24},{20,28},{24,16},{28,20},{1,9},{5... | collective-permute-start | bytes 294920 | tf_op jit(solution)/shard_map/ppermute | solution.py:262
  16.8 1.5 %collective-permute-start.2 = (bf16[64,768]{1,0:T(8,128)(2,1)S(1)}, bf16[64,768]{1,0:T(8,128)(2,1)S(1)}, u32[]{:S(2)}, u32[]{:S(2)}) collective-permute-start(bf16[64,768]{1,0:T(8,128)(2,1)S(1)} %constant_dynamic-update-slice_fusion.refs_0_), channel_id=1, source_target_pairs={{0,4},{4,0},{8,12},{12,8},{16,20},{20,16},{24,28},{28,24},{1,5},{5... | collective-permute-start | bytes 294920 | tf_op jit(solution)/shard_map/ppermute | solution.py:262
  18.3 0.5 %collective-permute-start.6 = (bf16[64,768]{1,0:T(8,128)(2,1)S(1)}, bf16[64,768]{1,0:T(8,128)(2,1)S(1)}, u32[]{:S(2)}, u32[]{:S(2)}) collective-permute-start(bf16[64,768]{1,0:T(8,128)(2,1)S(1)} %collective-permute-done.5.refs_4_), channel_id=1, source_target_pairs={{0,4},{4,0},{8,12},{12,8},{16,20},{20,16},{24,28},{28,24},{1,5},{5... | collective-permute-start | bytes 294920 | tf_op jit(solution)/shard_map/ppermute | solution.py:262
  18.8 0.0 collective-permute-done.3.refs_2_
  18.8 1.5 %collective-permute-start.4 = (bf16[64,768]{1,0:T(8,128)(2,1)S(1)}, bf16[64,768]{1,0:T(8,128)(2,1)S(1)}, u32[]{:S(2)}, u32[]{:S(2)}) collective-permute-start(bf16[64,768]{1,0:T(8,128)(2,1)S(1)} %collective-permute-done.3.refs_2_), channel_id=1, source_target_pairs={{0,4},{4,0},{8,12},{12,8},{16,20},{20,16},{24,28},{28,24},{1,5},{5... | collective-permute-start | bytes 294920 | tf_op jit(solution)/shard_map/ppermute | solution.py:262
  20.4 0.0 collective-permute-done.7.refs_6_
  20.4 1.0 %collective-permute-start.8 = (bf16[64,768]{1,0:T(8,128)(2,1)S(1)}, bf16[64,768]{1,0:T(8,128)(2,1)S(1)}, u32[]{:S(2)}, u32[]{:S(2)}) collective-permute-start(bf16[64,768]{1,0:T(8,128)(2,1)S(1)} %collective-permute-done.7.refs_6_), channel_id=1, source_target_pairs={{0,4},{4,0},{8,12},{12,8},{16,20},{20,16},{24,28},{28,24},{1,5},{5... | collective-permute-start | bytes 294920 | tf_op jit(solution)/shard_map/ppermute | solution.py:262
  21.3 2.3 %shard_map.30.refs_0_ = bf16[9,512,384]{2,1,0:T(8,128)(2,1)S(1)} custom-call(s32[1]{0:T(128)} %bitcast.2.core_ref, bf16[512,768]{1,0:T(8,128)(2,1)} %mine_ref.1, bf16[512,768]{1,0:T(8,128)(2,1)S(1)} %collective-permute-done.other_ref), custom_call_target="tpu_custom_call" | custom-call | flops 1000 | bytes 1000 | tf_op jit(solution)/shard_map/pallas_call | solution.py:314
  23.6 0.0 collective-permute-done.2.refs_1_
  23.6 0.0 collective-permute-done.6.refs_5_
  23.6 1.1 %collective-permute-done.4.refs_3_ = bf16[64,768]{1,0:T(8,128)(2,1)S(1)} collective-permute-done((bf16[64,768]{1,0:T(8,128)(2,1)S(1)}, bf16[64,768]{1,0:T(8,128)(2,1)S(1)}, u32[]{:S(2)}, u32[]{:S(2)}) %collective-permute-start.4) | collective-permute-done | bytes 98336 | tf_op jit(solution)/shard_map/ppermute | solution.py:262
  24.7 1.1 %collective-permute-done.8.refs_7_ = bf16[64,768]{1,0:T(8,128)(2,1)S(1)} collective-permute-done((bf16[64,768]{1,0:T(8,128)(2,1)S(1)}, bf16[64,768]{1,0:T(8,128)(2,1)S(1)}, u32[]{:S(2)}, u32[]{:S(2)}) %collective-permute-start.8) | collective-permute-done | bytes 98336 | tf_op jit(solution)/shard_map/ppermute | solution.py:262
  25.8 0.6 %shard_map.31.mine_ref = bf16[2,16,48,256]{3,2,1,0:T(8,128)(2,1)S(1)} custom-call(bf16[256,256]{1,0:T(8,128)(2,1)S(1)} %shard_map.29.order_ref, bf16[64,768]{1,0:T(8,128)(2,1)S(1)} %constant_dynamic-update-slice_fusion.refs_0_, bf16[64,768]{1,0:T(8,128)(2,1)S(1)} %collective-permute-done.2.refs_1_, bf16[64,768]{1,0:T(8,128)(2,1)S(1)} %collective-permute-done.3.refs_2_, ...), custom_call_target="tpu_custom_call" | custom-call | flops 800000000 | bytes 1000000 | tf_op jit(solution)/shard_map/pallas_call | solution.py:327
  26.4 0.1 collective-permute-start.9
  26.4 0.7 %collective-permute-done.10.mine_ref = bf16[512,768]{1,0:T(8,128)(2,1)S(1)} collective-permute-done((bf16[512,768]{1,0:T(8,128)(2,1)}, bf16[512,768]{1,0:T(8,128)(2,1)S(1)}, u32[]{:S(2)}, u32[]{:S(2)}) %collective-permute-start.10) | collective-permute-done | bytes 786464 | tf_op jit(solution)/shard_map/ppermute | solution.py:262
  27.1 0.0 collective-permute-start.11
  27.1 1.6 %collective-permute-done.9.other_ref = bf16[2,16,48,256]{3,2,1,0:T(8,128)(2,1)S(1)} collective-permute-done((bf16[2,16,48,256]{3,2,1,0:T(8,128)(2,1)S(1)}, bf16[2,16,48,256]{3,2,1,0:T(8,128)(2,1)S(1)}, u32[]{:S(2)}, u32[]{:S(2)}) %collective-permute-start.9) | collective-permute-done | bytes 786464 | tf_op jit(solution)/shard_map/ppermute | solution.py:262
  28.7 1.2 %shard_map.32 = (bf16[6,1504,256]{2,1,0:T(8,128)(2,1)S(1)}, bf16[3,6,608,256]{3,2,1,0:T(8,128)(2,1)S(1)}) custom-call(s32[1]{0:T(128)} %bitcast.tm_ref, bf16[2,16,48,256]{3,2,1,0:T(8,128)(2,1)S(1)} %shard_map.31.mine_ref, bf16[2,16,48,256]{3,2,1,0:T(8,128)(2,1)S(1)} %collective-permute-done.9.other_ref), custom_call_target="tpu_custom_call" | custom-call | flops 1000 | bytes 1000 | tf_op jit(solution)/shard_map/pallas_call | solution.py:338
  29.9 0.0 collective-permute-done.11.other_ref
  30.0 1.4 %shard_map.33.refs_1_ = bf16[9,512,384]{2,1,0:T(8,128)(2,1)S(1)} custom-call(s32[1]{0:T(128)} %bitcast.2.core_ref, bf16[512,768]{1,0:T(8,128)(2,1)S(1)} %collective-permute-done.10.mine_ref, bf16[512,768]{1,0:T(8,128)(2,1)S(1)} %collective-permute-done.11.other_ref), custom_call_target="tpu_custom_call" | custom-call | flops 1000 | bytes 1000 | tf_op jit(solution)/shard_map/pallas_call | solution.py:314
  31.4 17.1 %shard_map.34 = bf16[2,4,4,512,256]{4,3,2,1,0:T(8,128)(2,1)} custom-call(bf16[6,1504,256]{2,1,0:T(8,128)(2,1)S(1)} %get-tuple-element.22.xr, bf16[3,6,608,256]{3,2,1,0:T(8,128)(2,1)S(1)} %get-tuple-element.23.rv0, bf16[9,512,384]{2,1,0:T(8,128)(2,1)S(1)} %shard_map.30.refs_0_, bf16[9,512,384]{2,1,0:T(8,128)(2,1)S(1)} %shard_map.33.refs_1_), custom_call_target="tpu_custom_call" | custom-call | flops 15000000512 | bytes 20000000 | tf_op jit(solution)/shard_map/pallas_call | solution.py:351
  (1 shorter events, 0.0 us)
Async XLA Ops:
  0.0 0.7 %copy-start = (s32[8,256]{1,0:T(8,128)S(1)}, s32[8,256]{1,0:T(8,128)}, u32[]{:S(2)}) copy-start(s32[8,256]{1,0:T(8,128)} %list_ref) | copy-start | bytes 24580
  2.2 7.2 %collective-permute-start = (bf16[512,768]{1,0:T(8,128)(2,1)}, bf16[512,768]{1,0:T(8,128)(2,1)S(1)}, u32[]{:S(2)}, u32[]{:S(2)}) collective-permute-start(bf16[512,768]{1,0:T(8,128)(2,1)} %mine_ref.1), channel_id=1, source_target_pairs={{0,1},{1,0},{2,3},{3,2},{4,5},{5,4},{6,7},{7,6},{8,9},{9,8},{10,11... | collective-permute-start | bytes 2359304 | tf_op jit(solution)/shard_map/ppermute | solution.py:262
  2.7 4.9 %collective-permute-start.1 = (bf16[32,768]{1,0:T(8,128)(2,1)S(1)}, bf16[32,768]{1,0:T(8,128)(2,1)S(1)}, u32[]{:S(2)}, u32[]{:S(2)}) collective-permute-start(bf16[32,768]{1,0:T(8,128)(2,1)S(1)} %get-tuple-element.16), channel_id=1, source_target_pairs={{0,2},{1,3},{2,0},{3,1},{4,6},{5,7},{6,4},{7,5},{8,10},{9,11},{10,... | collective-permute-start | bytes 147464 | tf_op jit(solution)/shard_map/ppermute | solution.py:262
  7.6 19.5 %collective-permute-start.10 = (bf16[512,768]{1,0:T(8,128)(2,1)}, bf16[512,768]{1,0:T(8,128)(2,1)S(1)}, u32[]{:S(2)}, u32[]{:S(2)}) collective-permute-start(bf16[512,768]{1,0:T(8,128)(2,1)} %mine_ref.1), channel_id=1, source_target_pairs={{0,2},{1,3},{2,0},{3,1},{4,6},{5,7},{6,4},{7,5},{8,10},{9,11},{10,... | collective-permute-start | bytes 2359304 | tf_op jit(solution)/shard_map/ppermute | solution.py:262
  9.4 5.8 %collective-permute-start.5 = (bf16[64,768]{1,0:T(8,128)(2,1)S(1)}, bf16[64,768]{1,0:T(8,128)(2,1)S(1)}, u32[]{:S(2)}, u32[]{:S(2)}) collective-permute-start(bf16[64,768]{1,0:T(8,128)(2,1)S(1)} %constant_dynamic-update-slice_fusion.refs_0_), channel_id=1, source_target_pairs={{0,16},{4,20},{8,24},{12,28},{16,0},{20,4},{24,8},{28,12},{1,17},{... | collective-permute-start | bytes 294920 | tf_op jit(solution)/shard_map/ppermute | solution.py:262
  12.0 6.8 %collective-permute-start.3 = (bf16[64,768]{1,0:T(8,128)(2,1)S(1)}, bf16[64,768]{1,0:T(8,128)(2,1)S(1)}, u32[]{:S(2)}, u32[]{:S(2)}) collective-permute-start(bf16[64,768]{1,0:T(8,128)(2,1)S(1)} %constant_dynamic-update-slice_fusion.refs_0_), channel_id=1, source_target_pairs={{0,8},{4,12},{8,0},{12,4},{16,24},{20,28},{24,16},{28,20},{1,9},{5... | collective-permute-start | bytes 294920 | tf_op jit(solution)/shard_map/ppermute | solution.py:262
  15.2 5.2 %collective-permute-start.7 = (bf16[64,768]{1,0:T(8,128)(2,1)S(1)}, bf16[64,768]{1,0:T(8,128)(2,1)S(1)}, u32[]{:S(2)}, u32[]{:S(2)}) collective-permute-start(bf16[64,768]{1,0:T(8,128)(2,1)S(1)} %collective-permute-done.5.refs_4_), channel_id=1, source_target_pairs={{0,8},{4,12},{8,0},{12,4},{16,24},{20,28},{24,16},{28,20},{1,9},{5... | collective-permute-start | bytes 294920 | tf_op jit(solution)/shard_map/ppermute | solution.py:262
  16.8 6.8 %collective-permute-start.2 = (bf16[64,768]{1,0:T(8,128)(2,1)S(1)}, bf16[64,768]{1,0:T(8,128)(2,1)S(1)}, u32[]{:S(2)}, u32[]{:S(2)}) collective-permute-start(bf16[64,768]{1,0:T(8,128)(2,1)S(1)} %constant_dynamic-update-slice_fusion.refs_0_), channel_id=1, source_target_pairs={{0,4},{4,0},{8,12},{12,8},{16,20},{20,16},{24,28},{28,24},{1,5},{5... | collective-permute-start | bytes 294920 | tf_op jit(solution)/shard_map/ppermute | solution.py:262
  18.3 5.3 %collective-permute-start.6 = (bf16[64,768]{1,0:T(8,128)(2,1)S(1)}, bf16[64,768]{1,0:T(8,128)(2,1)S(1)}, u32[]{:S(2)}, u32[]{:S(2)}) collective-permute-start(bf16[64,768]{1,0:T(8,128)(2,1)S(1)} %collective-permute-done.5.refs_4_), channel_id=1, source_target_pairs={{0,4},{4,0},{8,12},{12,8},{16,20},{20,16},{24,28},{28,24},{1,5},{5... | collective-permute-start | bytes 294920 | tf_op jit(solution)/shard_map/ppermute | solution.py:262
  18.8 5.9 %collective-permute-start.4 = (bf16[64,768]{1,0:T(8,128)(2,1)S(1)}, bf16[64,768]{1,0:T(8,128)(2,1)S(1)}, u32[]{:S(2)}, u32[]{:S(2)}) collective-permute-start(bf16[64,768]{1,0:T(8,128)(2,1)S(1)} %collective-permute-done.3.refs_2_), channel_id=1, source_target_pairs={{0,4},{4,0},{8,12},{12,8},{16,20},{20,16},{24,28},{28,24},{1,5},{5... | collective-permute-start | bytes 294920 | tf_op jit(solution)/shard_map/ppermute | solution.py:262
  20.4 5.4 %collective-permute-start.8 = (bf16[64,768]{1,0:T(8,128)(2,1)S(1)}, bf16[64,768]{1,0:T(8,128)(2,1)S(1)}, u32[]{:S(2)}, u32[]{:S(2)}) collective-permute-start(bf16[64,768]{1,0:T(8,128)(2,1)S(1)} %collective-permute-done.7.refs_6_), channel_id=1, source_target_pairs={{0,4},{4,0},{8,12},{12,8},{16,20},{20,16},{24,28},{28,24},{1,5},{5... | collective-permute-start | bytes 294920 | tf_op jit(solution)/shard_map/ppermute | solution.py:262
  26.4 2.4 %collective-permute-start.9 = (bf16[2,16,48,256]{3,2,1,0:T(8,128)(2,1)S(1)}, bf16[2,16,48,256]{3,2,1,0:T(8,128)(2,1)S(1)}, u32[]{:S(2)}, u32[]{:S(2)}) collective-permute-start(bf16[2,16,48,256]{3,2,1,0:T(8,128)(2,1)S(1)} %shard_map.31.mine_ref), channel_id=1, source_target_pairs={{0,1},{1,0},{2,3},{3,2},{4,5},{5,4},{6,7},{7,6},{8,9},{9,8},{10,11... | collective-permute-start | bytes 2359304 | tf_op jit(solution)/shard_map/ppermute | solution.py:262
  27.1 2.8 %collective-permute-start.11 = (bf16[512,768]{1,0:T(8,128)(2,1)S(1)}, bf16[512,768]{1,0:T(8,128)(2,1)S(1)}, u32[]{:S(2)}, u32[]{:S(2)}) collective-permute-start(bf16[512,768]{1,0:T(8,128)(2,1)S(1)} %collective-permute-done.10.mine_ref), channel_id=1, source_target_pairs={{0,1},{1,0},{2,3},{3,2},{4,5},{5,4},{6,7},{7,6},{8,9},{9,8},{10,11... | collective-permute-start | bytes 2359304 | tf_op jit(solution)/shard_map/ppermute | solution.py:262
